TPU v7x, 32 devices: a whole 2x2x4 slice. The times are simulated.
32 devices in a mesh: dp: 16 (over z, x, core), split: 2 (over y).
Axes of the slice: x: 2, y: 2, z: 4, core: 2. Of those that a mesh axis runs over, the one named last changes fastest.
Arguments:
- gene_ids: int32 [16, 1024], P('dp'), may hold values from 0 to 7679
- expr_bins: int32 [16, 1024], P('dp'), may hold values from 0 to 50
- gene_order: int32 [16, 1024], P('dp'), may hold values from 0 to 1023, each once within a row
- cell_ids: int32 [16, 2, 512], P('dp'), may hold values from 0 to 3, never falling along the last dimension, each value on 1 to 256 neighbouring positions
- target_bins: int32 [64, 7680], P(None, ('dp', 'split')), may hold values from 0 to 50
- matrices: float32 [9216, 512], P(('dp', 'split'))
- vectors: float32 [3, 6, 512], replicated
- value_table: float32 [51, 512], replicated, may hold values from -0.75 to 0.75
- gene_table: float32 [7680, 512], P(('dp', 'split'))
- matrices_mom: float32 [9216, 512], P(('dp', 'split'))
- vectors_mom: float32 [3, 6, 512], replicated
- value_mom: float32 [51, 512], replicated
- gene_mom: float32 [7680, 512], P(('dp', 'split'))
- matrices_avg: float32 [9216, 512], P(('dp', 'split'))
- vectors_avg: float32 [3, 6, 512], replicated
- value_avg: float32 [51, 512], replicated, may hold values from -0.75 to 0.75
- gene_avg: float32 [7680, 512], P(('dp', 'split'))
Outputs:
- loss_sum: float32 [], replicated
- grad_norm: float32 [], replicated
- matrices_mom_new: float32 [9216, 512], P(('dp', 'split'))
- matrices_new: float32 [9216, 512], P(('dp', 'split'))
- matrices_avg_new: float32 [9216, 512], P(('dp', 'split'))
- vectors_mom_new: float32 [3, 6, 512], replicated
- vectors_new: float32 [3, 6, 512], replicated
- vectors_avg_new: float32 [3, 6, 512], replicated
- value_mom_new: float32 [51, 512], replicated
- value_new: float32 [51, 512], replicated
- value_avg_new: float32 [51, 512], replicated
- gene_mom_new: float32 [7680, 512], P(('dp', 'split'))
- gene_new: float32 [7680, 512], P(('dp', 'split'))
- gene_avg_new: float32 [7680, 512], P(('dp', 'split'))
Inputs may be any that keep to these rules, and one draw needn't show every extreme that they name: Each row of gene_order is a permutation of 0 to 1023. `cell_ids`: along each half of a row the cell numbers never fall; each of the 4 cells holds 1 to 256 positions of each half, and one holds exactly 256.
All inputs are finite; a program needn't handle non-finite values.
Results may differ from a plain program's by a relative error of at most 0.011.
Values may be sent and summed in bfloat16 or wider, within the bound.
No kernel may reach another device: no remote copies, remote signals or barrier semaphores. Data moves between devices by JAX's collectives and lax.ppermute only.
A program may use at most 320 MiB of HBM per device.

v0:
```python
from functools import partial
import math

import jax
import jax.numpy as jnp
from jax import lax
from jax.sharding import PartitionSpec as P

D = 512
HEADS = 8
HEAD_DIM = 64
BINS = 51
LAYERS = 3
CELLS_ROW = 4


EPSILON = 1e-05
NEGATIVE = -1e30
LEARN_RATE = 200.0
MOMENTUM = 0.9
AVERAGE_DECAY = 0.7
CLIP_NORM = 0.25
HIGHEST = lax.Precision.HIGHEST


def from_behind(block, axis, distance):
    devices = range(lax.axis_size(axis))
    route = [(i - distance, i) for i in devices if i - distance in devices]
    return lax.ppermute(block, axis, route)


def split_heads(array):
    return array.reshape(array.shape[0], HEADS, HEAD_DIM)


def blocked(array, block_count):
    return array.reshape((block_count, -1) + array.shape[1:])


def norm_forward(summed, gains, offset):
    average = jnp.mean(summed, axis=-1, keepdims=True)
    centered = summed - average
    scaling = lax.rsqrt(jnp.mean(centered * centered, axis=-1, keepdims=True) + EPSILON)
    normed = centered * scaling
    return (normed * gains + offset, normed, scaling)


def norm_backward(upstream, normed, scaling, gains):
    weighted = upstream * gains
    centered = weighted - jnp.mean(weighted, axis=-1, keepdims=True)
    centered = centered - normed * jnp.mean(weighted * normed, axis=-1, keepdims=True)
    return (centered * scaling, jnp.sum(upstream * normed, axis=0), jnp.sum(upstream, axis=0))


def block_scores(queries, self_keys, key_rows, allowed, self_on):
    scaling = 1.0 / math.sqrt(HEAD_DIM)
    scores = (
        jnp.einsum("thc,shc->hts", queries, key_rows, preferred_element_type=jnp.float32) * scaling
    )
    scores = jnp.where(allowed[None], scores, NEGATIVE)
    self_score = (
        jnp.einsum("thc,thc->ht", queries, self_keys, preferred_element_type=jnp.float32) * scaling
    )
    self_score = jnp.where(self_on, self_score, NEGATIVE)
    return (scores, self_score)


def attend_forward(queries, self_keys, self_values, key_rows, value_rows, allowed, self_on):
    scores, self_score = block_scores(queries, self_keys, key_rows, allowed, self_on)
    row_max = jnp.maximum(jnp.max(scores, axis=-1), self_score)
    exps = jnp.exp(scores - row_max[..., None])
    self_exp = jnp.exp(self_score - row_max)
    row_total = jnp.sum(exps, axis=-1) + self_exp
    probability = (exps / row_total[..., None]).astype(jnp.bfloat16)
    self_prob = (self_exp / row_total).astype(jnp.bfloat16)
    mixture = jnp.einsum(
        "hts,shc->thc", probability, value_rows, preferred_element_type=jnp.float32
    )
    mixture = mixture + self_prob.T[..., None].astype(jnp.float32) * self_values.astype(jnp.float32)
    return (mixture, row_max + jnp.log(row_total))


def attend_backward(
    queries, self_keys, self_values, key_rows, value_rows, allowed, self_on, block_lse, grad_mix
):
    scaling = 1.0 / math.sqrt(HEAD_DIM)
    scores, self_score = block_scores(queries, self_keys, key_rows, allowed, self_on)
    probability = jnp.exp(scores - block_lse[..., None])
    self_prob = jnp.exp(self_score - block_lse)
    grad_prob = jnp.einsum("thc,shc->hts", grad_mix, value_rows, preferred_element_type=jnp.float32)
    grad_self = jnp.einsum("thc,thc->ht", grad_mix, self_values, preferred_element_type=jnp.float32)
    delta = jnp.sum(probability * grad_prob, axis=-1) + self_prob * grad_self
    grad_score = (probability * (grad_prob - delta[..., None])).astype(jnp.bfloat16)
    grad_self_score = (self_prob * (grad_self - delta)).astype(jnp.bfloat16)
    self_weight = grad_self_score.T[..., None].astype(jnp.float32)
    grad_query = jnp.einsum(
        "hts,shc->thc", grad_score, key_rows, preferred_element_type=jnp.float32
    )
    grad_query = scaling * (grad_query + self_weight * self_keys.astype(jnp.float32))
    grad_keys = scaling * jnp.einsum(
        "hts,thc->shc", grad_score, queries, preferred_element_type=jnp.float32
    )
    grad_values = jnp.einsum(
        "hts,thc->shc",
        probability.astype(jnp.bfloat16),
        grad_mix,
        preferred_element_type=jnp.float32,
    )
    grad_self_key = scaling * self_weight * queries.astype(jnp.float32)
    grad_self_value = self_prob.astype(jnp.bfloat16).T[..., None].astype(
        jnp.float32
    ) * grad_mix.astype(jnp.float32)
    return (grad_query, grad_self_key, grad_self_value, grad_keys, grad_values)


def layer_forward(hidden_state, weight, vector_row, known_cells, own_cells, self_on, on_known):
    rows_here = hidden_state.shape[0]
    inputs = hidden_state.astype(jnp.bfloat16)
    projected = jnp.einsum(
        "td,jde->jte", inputs, weight[0:3], preferred_element_type=jnp.float32
    ).astype(jnp.bfloat16)
    remote = from_behind((projected[1], projected[2]), "split", 1)
    key_rows = jnp.where(on_known, projected[1], remote[0])
    value_rows = jnp.where(on_known, projected[2], remote[1])
    block_rows = min(512, rows_here)
    block_count = rows_here // block_rows

    def attend_block(block_items):
        queries, self_keys, self_values, block_cells = block_items
        allowed = block_cells[:, None] == known_cells[None, :]
        mixture, block_lse = attend_forward(
            split_heads(queries),
            split_heads(self_keys),
            split_heads(self_values),
            split_heads(key_rows),
            split_heads(value_rows),
            allowed,
            self_on,
        )
        return (mixture.reshape(block_rows, D), block_lse)

    mixture, row_lse = lax.map(
        attend_block,
        (
            blocked(projected[0], block_count),
            blocked(projected[1], block_count),
            blocked(projected[2], block_count),
            blocked(own_cells, block_count),
        ),
    )
    mixture = mixture.reshape(rows_here, D).astype(jnp.bfloat16)
    branch = jnp.dot(mixture, weight[3], preferred_element_type=jnp.float32)
    first_out, normed_one, scale_one = norm_forward(
        hidden_state + branch, vector_row[0], vector_row[1]
    )
    first_low = first_out.astype(jnp.bfloat16)
    hidden = jnp.dot(first_low, weight[4], preferred_element_type=jnp.float32) + vector_row[4]
    activated = jax.nn.gelu(hidden, approximate=False).astype(jnp.bfloat16)
    branch_two = jnp.dot(activated, weight[5], preferred_element_type=jnp.float32) + vector_row[5]
    layer_out, normed_two, scale_two = norm_forward(
        first_out + branch_two, vector_row[2], vector_row[3]
    )
    saved_layer = (
        inputs,
        projected,
        key_rows,
        value_rows,
        row_lse,
        mixture,
        normed_one,
        scale_one,
        first_low,
        hidden,
        activated,
        normed_two,
        scale_two,
    )
    return (layer_out, saved_layer)


def layer_backward(
    gradient, weight, vector_row, saved_layer, known_cells, own_cells, self_on, on_known
):
    (
        inputs,
        projected,
        key_rows,
        value_rows,
        row_lse,
        mixture,
        normed_one,
        scale_one,
        first_low,
        hidden,
        activated,
        normed_two,
        scale_two,
    ) = saved_layer
    rows_here = inputs.shape[0]
    block_rows = min(512, rows_here)
    block_count = rows_here // block_rows
    grad_sum_two, grad_gain_two, grad_shift_two = norm_backward(
        gradient, normed_two, scale_two, vector_row[2]
    )
    grad_branch_two = grad_sum_two.astype(jnp.bfloat16)
    grad_bias_out = jnp.sum(grad_branch_two.astype(jnp.float32), axis=0)
    grad_w_out = jnp.einsum(
        "td,te->de", activated, grad_branch_two, preferred_element_type=jnp.float32
    )
    grad_act = jnp.einsum(
        "te,de->td", grad_branch_two, weight[5], preferred_element_type=jnp.float32
    )
    _, gelu_pull = jax.vjp(partial(jax.nn.gelu, approximate=False), hidden)
    grad_hidden = gelu_pull(grad_act)[0].astype(jnp.bfloat16)
    grad_bias_in = jnp.sum(grad_hidden.astype(jnp.float32), axis=0)
    grad_w_in = jnp.einsum("td,te->de", first_low, grad_hidden, preferred_element_type=jnp.float32)
    grad_first = grad_sum_two + jnp.einsum(
        "te,de->td", grad_hidden, weight[4], preferred_element_type=jnp.float32
    )
    grad_sum_one, grad_gain_one, grad_shift_one = norm_backward(
        grad_first, normed_one, scale_one, vector_row[0]
    )
    grad_branch = grad_sum_one.astype(jnp.bfloat16)
    grad_w_mix = jnp.einsum("td,te->de", mixture, grad_branch, preferred_element_type=jnp.float32)
    grad_mixture = jnp.einsum(
        "te,de->td", grad_branch, weight[3], preferred_element_type=jnp.float32
    ).astype(jnp.bfloat16)

    def block_step(carried, block_items):
        queries, self_keys, self_values, block_cells, block_lse, block_grad = block_items
        allowed = block_cells[:, None] == known_cells[None, :]
        grad_query, grad_self_key, grad_self_value, grad_keys, grad_values = attend_backward(
            split_heads(queries),
            split_heads(self_keys),
            split_heads(self_values),
            split_heads(key_rows),
            split_heads(value_rows),
            allowed,
            self_on,
            block_lse,
            split_heads(block_grad),
        )
        return (
            (carried[0] + grad_keys, carried[1] + grad_values),
            (
                grad_query.reshape(block_rows, D),
                grad_self_key.reshape(block_rows, D),
                grad_self_value.reshape(block_rows, D),
            ),
        )

    zero_keys = jnp.zeros((rows_here, HEADS, HEAD_DIM), jnp.float32)
    key_sums, block_grads = lax.scan(
        block_step,
        (zero_keys, zero_keys),
        (
            blocked(projected[0], block_count),
            blocked(projected[1], block_count),
            blocked(projected[2], block_count),
            blocked(own_cells, block_count),
            row_lse,
            blocked(grad_mixture, block_count),
        ),
    )
    known_key_grad = key_sums[0].reshape(rows_here, D)
    known_value_grad = key_sums[1].reshape(rows_here, D)
    returned = (
        from_behind(known_key_grad.astype(jnp.bfloat16), "split", -1).astype(known_key_grad.dtype),
        from_behind(known_value_grad.astype(jnp.bfloat16), "split", -1).astype(
            known_value_grad.dtype
        ),
    )
    key_total = jnp.where(on_known, known_key_grad + returned[0], 0.0) + block_grads[1].reshape(
        rows_here, D
    )
    value_total = jnp.where(on_known, known_value_grad + returned[1], 0.0) + block_grads[2].reshape(
        rows_here, D
    )
    grad_projected = jnp.stack(
        [block_grads[0].reshape(rows_here, D), key_total, value_total]
    ).astype(jnp.bfloat16)
    grad_w_qkv = jnp.einsum(
        "td,jte->jde", inputs, grad_projected, preferred_element_type=jnp.float32
    )
    grad_state = grad_sum_one + jnp.einsum(
        "jte,jde->td", grad_projected, weight[0:3], preferred_element_type=jnp.float32
    )
    grad_weight = jnp.concatenate([grad_w_qkv, grad_w_mix[None], grad_w_in[None], grad_w_out[None]])
    grad_vector = jnp.stack(
        [grad_gain_one, grad_shift_one, grad_gain_two, grad_shift_two, grad_bias_in, grad_bias_out]
    )
    return (grad_state, grad_weight, grad_vector)


def local(
    gene_ids,
    expr_bins,
    gene_order,
    cell_ids,
    target_bins,
    matrices,
    vectors,
    value_table,
    gene_table,
    matrices_mom,
    vectors_mom,
    value_mom,
    gene_mom,
    matrices_avg,
    vectors_avg,
    value_avg,
    gene_avg,
):
    split_index = lax.axis_index("split")
    on_known = split_index == 0
    self_on = split_index == 1
    cell_rows = cell_ids[0]
    half = cell_rows.shape[1]
    known_cells = cell_rows[0]
    own_cells = jnp.where(on_known, cell_rows[0], cell_rows[1])
    picks = lax.dynamic_slice_in_dim(gene_order[0], split_index * half, half)
    genes = jnp.take(gene_ids[0], picks)
    levels = jnp.take(expr_bins[0], picks)
    rows_dev = gene_table.shape[0]
    vocab_size = rows_dev * lax.axis_size(("dp", "split"))
    gathered = lax.all_gather(matrices.astype(jnp.bfloat16), ("dp", "split"), axis=0, tiled=True)
    weights = gathered.reshape(LAYERS, 6, D, D)
    table_low = gene_table.astype(jnp.bfloat16)
    shard_rows = lax.all_gather(table_low, ("dp", "split"), axis=0, tiled=True)
    one_hot = (genes[:, None] == jnp.arange(shard_rows.shape[0])[None, :]).astype(jnp.bfloat16)
    embedded = jnp.dot(one_hot, shard_rows, preferred_element_type=jnp.float32)
    level_hot = (levels[:, None] == jnp.arange(BINS)[None, :]).astype(jnp.float32)
    hidden_state = math.sqrt(D) * embedded + jnp.dot(level_hot, value_table, precision=HIGHEST)
    saved_all = []
    for layer_index in range(LAYERS):
        hidden_state, saved_layer = layer_forward(
            hidden_state,
            weights[layer_index],
            vectors[layer_index],
            known_cells,
            own_cells,
            self_on,
            on_known,
        )
        saved_all.append(saved_layer)
    cell_numbers = jnp.arange(CELLS_ROW)
    member = (own_cells[None, :] == cell_numbers[:, None]).astype(jnp.float32)
    counts = jnp.sum(
        (cell_rows[:, :, None] == cell_numbers[None, None, :]).astype(jnp.float32), axis=(0, 1)
    )
    cell_share = jnp.dot(member, hidden_state, precision=HIGHEST) / counts[:, None]
    pooled_parts = lax.all_gather(cell_share, ("dp", "split"), axis=0, tiled=True)
    pooled = jnp.sum(pooled_parts.reshape(-1, 2, CELLS_ROW, D), axis=1).reshape(-1, D)
    pooled_low = pooled.astype(jnp.bfloat16)
    predicted = lax.dot_general(
        pooled_low, table_low, (((1,), (1,)), ((), ())), preferred_element_type=jnp.float32
    )
    target = target_bins.astype(jnp.float32) * (4.0 / (BINS - 1)) - 2.0
    errors = predicted - target
    loss_part = jnp.sum(errors * errors)
    loss_sum = lax.psum(loss_part, ("dp", "split"))
    grad_pred = (errors * (2.0 / vocab_size)).astype(jnp.bfloat16)
    head_table_grad = jnp.einsum(
        "cv,cd->vd", grad_pred, pooled_low, preferred_element_type=jnp.float32
    )
    grad_pooled = jnp.dot(grad_pred, table_low, preferred_element_type=jnp.float32)
    grad_pooled = lax.psum_scatter(grad_pooled, "dp", scatter_dimension=0, tiled=True)
    grad_pooled = lax.psum(grad_pooled, "split")
    gradient = jnp.einsum("ct,cd->td", member, grad_pooled / counts[:, None], precision=HIGHEST)
    weight_grads = [None] * LAYERS
    vector_grads = [None] * LAYERS
    for layer_index in reversed(range(LAYERS)):
        gradient, weight_grads[layer_index], vector_grads[layer_index] = layer_backward(
            gradient,
            weights[layer_index],
            vectors[layer_index],
            saved_all[layer_index],
            known_cells,
            own_cells,
            self_on,
            on_known,
        )
    grad_vectors = jnp.stack(vector_grads)
    grad_value = jnp.einsum("tb,td->bd", level_hot, gradient, precision=HIGHEST)
    grad_embedded = (math.sqrt(D) * gradient).astype(jnp.bfloat16)
    grad_matrices = lax.psum_scatter(
        jnp.stack(weight_grads).reshape(LAYERS * 6 * D, D),
        ("dp", "split"),
        scatter_dimension=0,
        tiled=True,
    )
    every_gene = lax.all_gather(genes, ("dp", "split"), axis=0, tiled=True)
    own_start = lax.axis_index(("dp", "split")) * rows_dev
    one_hot = ((jnp.arange(rows_dev) + own_start)[:, None] == every_gene[None, :]).astype(
        jnp.bfloat16
    )
    embed_grads = jnp.dot(
        one_hot,
        lax.all_gather(grad_embedded, ("dp", "split"), axis=0, tiled=True),
        preferred_element_type=jnp.float32,
    )
    grad_table = embed_grads + head_table_grad
    squares = jnp.sum(grad_matrices * grad_matrices) + jnp.sum(grad_table * grad_table)
    squares, grad_vectors, grad_value = lax.psum(
        (squares, grad_vectors, grad_value), ("dp", "split")
    )
    grad_norm = jnp.sqrt(
        squares + jnp.sum(grad_vectors * grad_vectors) + jnp.sum(grad_value * grad_value)
    )
    factor = CLIP_NORM / grad_norm

    def update(weight, moment, average, grad_full):
        clipped = factor * grad_full
        moment_new = MOMENTUM * moment + clipped
        weight_new = weight - LEARN_RATE * (clipped + MOMENTUM * moment_new)
        return (
            moment_new,
            weight_new,
            AVERAGE_DECAY * average + (1.0 - AVERAGE_DECAY) * weight_new,
        )

    mat_out = update(matrices, matrices_mom, matrices_avg, grad_matrices)
    vec_out = update(vectors, vectors_mom, vectors_avg, grad_vectors)
    value_out = update(value_table, value_mom, value_avg, grad_value)
    gene_out = update(gene_table, gene_mom, gene_avg, grad_table)
    return (
        loss_sum,
        grad_norm,
        mat_out[0],
        mat_out[1],
        mat_out[2],
        vec_out[0],
        vec_out[1],
        vec_out[2],
        value_out[0],
        value_out[1],
        value_out[2],
        gene_out[0],
        gene_out[1],
        gene_out[2],
    )


def solution(mesh):
    in_specs = (
        P("dp", None),
        P("dp", None),
        P("dp", None),
        P("dp", None, None),
        P(None, ("dp", "split")),
        P(("dp", "split"), None),
        P(),
        P(),
        P(("dp", "split"), None),
        P(("dp", "split"), None),
        P(),
        P(),
        P(("dp", "split"), None),
        P(("dp", "split"), None),
        P(),
        P(),
        P(("dp", "split"), None),
    )
    out_specs = (
        P(),
        P(),
        P(("dp", "split"), None),
        P(("dp", "split"), None),
        P(("dp", "split"), None),
        P(),
        P(),
        P(),
        P(),
        P(),
        P(),
        P(("dp", "split"), None),
        P(("dp", "split"), None),
        P(("dp", "split"), None),
    )
    return jax.shard_map(local, mesh=mesh, in_specs=in_specs, out_specs=out_specs, check_vma=False)
```

profile of v0, /device:TPU:0, one launch (start us, length us, event | category | flops | bytes accessed | tf_op | source)
XLA Modules:
  0.0 1133.4 jit_solution(11121702760885947803)
XLA Ops:
  19.9 69.8 %all-gather.6.cloned.1.call-done = bf16[7680,512]{1,0:T(8,128)(2,1)} async-done(((bf16[240,512]{1,0:T(8,128)(2,1)}), bf16[7680,512]{1,0:T(8,128)(2,1)}) %all-gather.6.cloned.1.call-update) | async-done | bytes 7864336 | tf_op jit(solution)/shard_map/all_gather | solution.py:329
  89.7 9.8 fusion.27
  100.3 73.5 %all-gather.8.cloned.1.call-done = bf16[9216,512]{1,0:T(8,128)(2,1)} async-done(((bf16[288,512]{1,0:T(8,128)(2,1)}), bf16[9216,512]{1,0:T(8,128)(2,1)}) %all-gather.8.cloned.1.call-update) | async-done | bytes 9437200 | tf_op jit(solution)/shard_map/all_gather | solution.py:326
  184.6 8.8 collective-permute-done.1
  193.4 10.6 collective-permute-done
  225.9 10.7 collective-permute-done.3
  236.5 9.6 collective-permute-done.2
  265.4 10.5 collective-permute-done.5
  275.9 8.7 collective-permute-done.4
  299.9 67.3 %all-gather = f32[32,4,512]{2,1,0:T(4,128)S(1)} all-gather(f32[1,4,512]{2,1,0:T(4,128)S(1)} %fusion.52), channel_id=1, replica_groups=mesh['dp'=16,'split'=2] {'dp','split'}, dimensions={0}, use_global_device_ids=true | all-gather | bytes 270336 | tf_op jit(solution)/shard_map/all_gather | solution.py:352
  372.3 81.1 %all-reduce.7.cloned.1.call-done = f32[64,512]{1,0:T(8,128)} async-done(((f32[64,512]{1,0:T(8,128)}), f32[64,512]{1,0:T(8,128)}) %all-reduce.7.cloned.1.call-update) | async-done | bytes 131088
  454.1 5.4 psum.36
  493.3 7.6 collective-permute-done.7
  502.2 7.9 collective-permute-done.6
  548.2 7.0 collective-permute-done.8
  585.2 5.5 collective-permute-done.11
  592.0 6.1 collective-permute-done.10
  607.7 12.6 %pad_maximum_fusion = f32[3,6,512,512]{3,2,1,0:T(8,128)} fusion(f32[1,6,512,512]{3,2,1,0:T(8,128)} %maximum_bitcast_fusion.2, f32[1,6,512,512]{3,2,1,0:T(8,128)} %maximum_bitcast_fusion.1, f32[1,6,512,512]{3,2,1,0:T(8,128)S(1)} %maximum_bitcast_fusion), kind=kLoop, calls=%fused_computation.2 | loop fusion | flops 9437184 | bytes 37748736 | tf_op jit(solution)/shard_map/stack | solution.py:387
  621.0 63.6 %all-gather.1 = s32[32,1,512]{2,1,0:T(1,128)S(1)} all-gather(s32[1,1,512]{2,1,0:T(1,128)S(1)} %bitcast.689), channel_id=1, replica_groups=mesh['dp'=16,'split'=2] {'dp','split'}, dimensions={0}, use_global_device_ids=true | all-gather | bytes 67584 | tf_op jit(solution)/shard_map/all_gather | solution.py:392
  684.8 37.8 %all-reduce.5.cloned.1.call-done = f32[51,512]{1,0:T(8,128)} async-done(((f32[51,512]{1,0:T(8,128)}), f32[51,512]{1,0:T(8,128)}) %all-reduce.5.cloned.1.call-update) | async-done | bytes 104464 | tf_op jit(solution)/shard_map/psum | solution.py:404
  724.1 212.1 %reduce-scatter.2.cloned.1.call-done = f32[288,512]{1,0:T(8,128)} async-done(((f32[9216,512]{1,0:T(8,128)}), f32[288,512]{1,0:T(8,128)}) %reduce-scatter.2.cloned.1.call-update) | async-done | bytes 589840 | tf_op jit(solution)/shard_map/reduce_scatter | solution.py:386
  938.1 127.3 %all-gather.10.cloned.1.call-done = bf16[16384,512]{0,1:T(8,128)(2,1)} async-done(((bf16[512,512]{0,1:T(8,128)(2,1)}), bf16[16384,512]{0,1:T(8,128)(2,1)}) %all-gather.10.cloned.1.call-update) | async-done | bytes 16777232 | tf_op jit(solution)/shard_map/all_gather | solution.py:399
  1065.5 8.4 fusion.1
  1076.1 39.0 %all-reduce.1 = (f32[]{:T(128)}, f32[]{:T(128)}, f32[3,6,512]{2,1,0:T(8,128)S(1)}) all-reduce(f32[]{:T(128)} %get-tuple-element.390, f32[]{:T(128)S(6)} %add.544, f32[3,6,512]{2,1,0:T(8,128)S(1)} %pad_maximum_fusion.10), channel_id=1, replica_groups=mesh['dp'=16,'split'=2] {'dp','split'}, use_global_device_ids=true, to_apply=%region_21.23 | all-reduce | flops 9218 | bytes 73744 | tf_op jit(solution)/shard_map/psum | solution.py:361
  (481 shorter events, 210.7 us)
Async XLA Ops:
  7.2 82.5 %all-gather.6.cloned.1.call-start = ((), (), s32[]{:S(2)}) async-start(), calls=%async_computation.1 | async-start | bytes 8110080 | tf_op jit(solution)/shard_map/all_gather | solution.py:329
  9.0 164.8 %all-gather.8.cloned.1.call-start = ((), (), s32[]{:S(2)}) async-start(), calls=%async_computation.2 | async-start | bytes 9732096 | tf_op jit(solution)/shard_map/all_gather | solution.py:326
  10.9 442.5 %all-reduce.7.cloned.1.call-start = ((), (), s32[]{:S(2)}) async-start(), calls=%async_computation.6 | async-start | bytes 262144
  19.9 197.7 %copy-start.105 = (f32[1,1,512]{2,1,0:T(1,128)}, f32[1,1,512]{2,1,0:T(1,128)S(1)}, u32[]{:S(2)}) copy-start(f32[1,1,512]{2,1,0:T(1,128)S(1)} %get-tuple-element.362) | copy-start | bytes 6148
  19.9 231.4 %copy-start.107 = (f32[1,1,512]{2,1,0:T(1,128)}, f32[1,1,512]{2,1,0:T(1,128)S(1)}, u32[]{:S(2)}) copy-start(f32[1,1,512]{2,1,0:T(1,128)S(1)} %get-tuple-element.359) | copy-start | bytes 6148
  19.9 231.4 %copy-start.120 = (f32[1,1,512]{2,1,0:T(1,128)}, f32[1,1,512]{2,1,0:T(1,128)S(1)}, u32[]{:S(2)}) copy-start(f32[1,1,512]{2,1,0:T(1,128)S(1)} %get-tuple-element.358) | copy-start | bytes 6148
  19.9 236.3 %copy-start.88 = (f32[1,1,512]{2,1,0:T(1,128)}, f32[1,1,512]{2,1,0:T(1,128)S(1)}, u32[]{:S(2)}) copy-start(f32[1,1,512]{2,1,0:T(1,128)S(1)} %get-tuple-element.357) | copy-start | bytes 6148
  19.9 236.3 %copy-start.109 = (f32[1,1,512]{2,1,0:T(1,128)}, f32[1,1,512]{2,1,0:T(1,128)S(1)}, u32[]{:S(2)}) copy-start(f32[1,1,512]{2,1,0:T(1,128)S(1)} %get-tuple-element.356) | copy-start | bytes 6148
  100.3 109.8 %copy-start.34 = (f32[512,512]{0,1:T(8,128)}, f32[512,512]{0,1:T(8,128)S(1)}, u32[]{:S(2)}) copy-start(f32[512,512]{0,1:T(8,128)S(1)} %convolution_add_fusion.12) | copy-start | bytes 3145732
  177.8 15.6 %collective-permute-start.1 = (bf16[512,512]{0,1:T(8,128)(2,1)S(1)}, bf16[512,512]{0,1:T(8,128)(2,1)S(1)}, u32[]{:S(2)}, u32[]{:S(2)}) collective-permute-start(bf16[512,512]{0,1:T(8,128)(2,1)S(1)} %get-tuple-element.342), channel_id=1, source_target_pairs={{0,1},{2,3},{4,5},{6,7},{8,9},{10,11},{12,13},{14,15},{16,17},{18,... | collective-permute-start | bytes 1572872 | tf_op jit(solution)/shard_map/ppermute | solution.py:29
  181.2 22.8 %collective-permute-start = (bf16[512,512]{0,1:T(8,128)(2,1)S(1)}, bf16[512,512]{0,1:T(8,128)(2,1)S(1)}, u32[]{:S(2)}, u32[]{:S(2)}) collective-permute-start(bf16[512,512]{0,1:T(8,128)(2,1)S(1)} %get-tuple-element.341), channel_id=1, source_target_pairs={{0,1},{2,3},{4,5},{6,7},{8,9},{10,11},{12,13},{14,15},{16,17},{18,... | collective-permute-start | bytes 1572872 | tf_op jit(solution)/shard_map/ppermute | solution.py:29
  219.8 16.8 %collective-permute-start.3 = (bf16[512,512]{0,1:T(8,128)(2,1)S(1)}, bf16[512,512]{0,1:T(8,128)(2,1)S(1)}, u32[]{:S(2)}, u32[]{:S(2)}) collective-permute-start(bf16[512,512]{0,1:T(8,128)(2,1)S(1)} %get-tuple-element.335), channel_id=1, source_target_pairs={{0,1},{2,3},{4,5},{6,7},{8,9},{10,11},{12,13},{14,15},{16,17},{18,... | collective-permute-start | bytes 1572872 | tf_op jit(solution)/shard_map/ppermute | solution.py:29
  224.2 22.0 %collective-permute-start.2 = (bf16[512,512]{0,1:T(8,128)(2,1)S(1)}, bf16[512,512]{0,1:T(8,128)(2,1)S(1)}, u32[]{:S(2)}, u32[]{:S(2)}) collective-permute-start(bf16[512,512]{0,1:T(8,128)(2,1)S(1)} %get-tuple-element.334), channel_id=1, source_target_pairs={{0,1},{2,3},{4,5},{6,7},{8,9},{10,11},{12,13},{14,15},{16,17},{18,... | collective-permute-start | bytes 1572872 | tf_op jit(solution)/shard_map/ppermute | solution.py:29
  259.1 16.8 %collective-permute-start.5 = (bf16[512,512]{0,1:T(8,128)(2,1)S(1)}, bf16[512,512]{0,1:T(8,128)(2,1)S(1)}, u32[]{:S(2)}, u32[]{:S(2)}) collective-permute-start(bf16[512,512]{0,1:T(8,128)(2,1)S(1)} %get-tuple-element.328), channel_id=1, source_target_pairs={{0,1},{2,3},{4,5},{6,7},{8,9},{10,11},{12,13},{14,15},{16,17},{18,... | collective-permute-start | bytes 1572872 | tf_op jit(solution)/shard_map/ppermute | solution.py:29
  263.6 21.0 %collective-permute-start.4 = (bf16[512,512]{0,1:T(8,128)(2,1)S(1)}, bf16[512,512]{0,1:T(8,128)(2,1)S(1)}, u32[]{:S(2)}, u32[]{:S(2)}) collective-permute-start(bf16[512,512]{0,1:T(8,128)(2,1)S(1)} %get-tuple-element.327), channel_id=1, source_target_pairs={{0,1},{2,3},{4,5},{6,7},{8,9},{10,11},{12,13},{14,15},{16,17},{18,... | collective-permute-start | bytes 1572872 | tf_op jit(solution)/shard_map/ppermute | solution.py:29
  370.4 352.2 %all-reduce.5.cloned.1.call-start = ((), (), s32[]{:S(2)}) async-start(), calls=%async_computation.5 | async-start | bytes 229376 | tf_op jit(solution)/shard_map/psum | solution.py:404
  484.0 16.9 %collective-permute-start.7 = (bf16[512,512]{0,1:T(8,128)(2,1)S(1)}, bf16[512,512]{0,1:T(8,128)(2,1)}, u32[]{:S(2)}, u32[]{:S(2)}) collective-permute-start(bf16[512,512]{0,1:T(8,128)(2,1)S(1)} %bitcast_convert_fusion.4), channel_id=1, source_target_pairs={{1,0},{3,2},{5,4},{7,6},{9,8},{11,10},{13,12},{15,14},{17,16},{19,... | collective-permute-start | bytes 1572872 | tf_op jit(solution)/shard_map/ppermute | solution.py:29
  489.4 20.8 %collective-permute-start.6 = (bf16[512,512]{0,1:T(8,128)(2,1)S(1)}, bf16[512,512]{0,1:T(8,128)(2,1)S(1)}, u32[]{:S(2)}, u32[]{:S(2)}) collective-permute-start(bf16[512,512]{0,1:T(8,128)(2,1)S(1)} %bitcast_convert_fusion.5), channel_id=1, source_target_pairs={{1,0},{3,2},{5,4},{7,6},{9,8},{11,10},{13,12},{15,14},{17,16},{19,... | collective-permute-start | bytes 1572872 | tf_op jit(solution)/shard_map/ppermute | solution.py:29
  529.8 17.1 %collective-permute-start.9 = (bf16[512,512]{0,1:T(8,128)(2,1)}, bf16[512,512]{0,1:T(8,128)(2,1)}, u32[]{:S(2)}, u32[]{:S(2)}) collective-permute-start(bf16[512,512]{0,1:T(8,128)(2,1)} %bitcast_convert_fusion.2), channel_id=1, source_target_pairs={{1,0},{3,2},{5,4},{7,6},{9,8},{11,10},{13,12},{15,14},{17,16},{19,... | collective-permute-start | bytes 1572872 | tf_op jit(solution)/shard_map/ppermute | solution.py:29
  535.1 20.1 %collective-permute-start.8 = (bf16[512,512]{0,1:T(8,128)(2,1)S(1)}, bf16[512,512]{0,1:T(8,128)(2,1)S(1)}, u32[]{:S(2)}, u32[]{:S(2)}) collective-permute-start(bf16[512,512]{0,1:T(8,128)(2,1)S(1)} %bitcast_convert_fusion.3), channel_id=1, source_target_pairs={{1,0},{3,2},{5,4},{7,6},{9,8},{11,10},{13,12},{15,14},{17,16},{19,... | collective-permute-start | bytes 1572872 | tf_op jit(solution)/shard_map/ppermute | solution.py:29
  573.8 16.9 %collective-permute-start.11 = (bf16[512,512]{0,1:T(8,128)(2,1)S(1)}, bf16[512,512]{0,1:T(8,128)(2,1)}, u32[]{:S(2)}, u32[]{:S(2)}) collective-permute-start(bf16[512,512]{0,1:T(8,128)(2,1)S(1)} %bitcast_convert_fusion), channel_id=1, source_target_pairs={{1,0},{3,2},{5,4},{7,6},{9,8},{11,10},{13,12},{15,14},{17,16},{19,... | collective-permute-start | bytes 1572872 | tf_op jit(solution)/shard_map/ppermute | solution.py:29
  579.2 18.9 %collective-permute-start.10 = (bf16[512,512]{0,1:T(8,128)(2,1)S(1)}, bf16[512,512]{0,1:T(8,128)(2,1)S(1)}, u32[]{:S(2)}, u32[]{:S(2)}) collective-permute-start(bf16[512,512]{0,1:T(8,128)(2,1)S(1)} %bitcast_convert_fusion.1), channel_id=1, source_target_pairs={{1,0},{3,2},{5,4},{7,6},{9,8},{11,10},{13,12},{15,14},{17,16},{19,... | collective-permute-start | bytes 1572872 | tf_op jit(solution)/shard_map/ppermute | solution.py:29
  605.3 330.9 %reduce-scatter.2.cloned.1.call-start = ((), (), s32[]{:S(2)}) async-start(), calls=%async_computation.3 | async-start | bytes 19464192 | tf_op jit(solution)/shard_map/reduce_scatter | solution.py:386
  620.3 445.1 %all-gather.10.cloned.1.call-start = ((), (), s32[]{:S(2)}) async-start(), calls=%async_computation.4 | async-start | bytes 17301504 | tf_op jit(solution)/shard_map/all_gather | solution.py:399
  (132 other events, 2160.3 us)
Sparse Core Ops, SparseCore 0:
  11.5 78.1 all-gather.5
  93.2 80.5 all-gather.7
  370.5 82.8 all-reduce.6
  605.5 117.0 all-reduce.4
  728.8 207.3 reduce-scatter.1
  939.6 125.8 all-gather.9
where the time goes:
time: 1140 us; the launch traced here: 1130 us
  waiting for transfers between devices  700 us (61%)
  blocking collectives  175 us (15%)
  matrix products  118 us (10%)
  other arithmetic  69.1 us (6%)
  starting transfers between devices  26.1 us (2%)
  local copies, waits for them, and re-layouts  22.8 us (2%)
  between operations  22.1 us (2%)
    reduce_scatter x1, waiting for transfers between devices, local(): lax.psum_scatter(jnp.stack(weight_grads).reshape(LAYERS * 6 * D, D), ('dp...  212 us
    all_gather x1, waiting for transfers between devices, local(): lax.all_gather(grad_embedded, ('dp', 'split'), axis=0, tiled=True)  127 us
    ppermute x12, waiting for transfers between devices, from_behind(): return lax.ppermute(block, axis, route)  97.3 us
    unnamed x7, waiting for transfers between devices  81.7 us
    all_gather x1, waiting for transfers between devices, local(): lax.all_gather(matrices.astype(jnp.bfloat16), ('dp', 'split'), axis=0, ti...  73.5 us
    all_gather x1, waiting for transfers between devices, local(): shard_rows = lax.all_gather(table_low, ('dp', 'split'), axis=0, tiled=True)  69.8 us
    all_gather x1, blocking collectives, local(): lax.all_gather(cell_share, ('dp', 'split'), axis=0, tiled=True)  67.3 us
    all_gather x1, blocking collectives, local(): every_gene = lax.all_gather(genes, ('dp', 'split'), axis=0, tiled=True)  63.6 us
  transfers between devices with their start and end apart: 18, of which 18 were waited for; matrix products, arithmetic and copies ran while one was open for 6% of the time, Pallas kernels for 0%

commit v1 on v0

v1 whole, which is shorter than its diff:
```python
import math

import jax
import jax.numpy as jnp
from jax import lax
from jax.sharding import Mesh, PartitionSpec as P

D = 512
HEADS = 8
HEAD_DIM = 64
BINS = 51
LAYERS = 3
CELLS_ROW = 4

EPSILON = 1e-05
NEGATIVE = -1e30
LEARN_RATE = 200.0
MOMENTUM = 0.9
AVERAGE_DECAY = 0.7
CLIP_NORM = 0.25
HIGHEST = lax.Precision.HIGHEST
SCALING = 1.0 / math.sqrt(HEAD_DIM)
F32 = jnp.float32
BF16 = jnp.bfloat16


def flip(block, axis):
    return lax.ppermute(block, axis, [(0, 1), (1, 0)])


def ordered(own, other, bit, axis=0):
    low = jnp.where(bit == 0, own, other)
    high = jnp.where(bit == 0, other, own)
    return jnp.stack([low, high], axis=axis)


def short_z(planes):
    return planes in (2, 4)


def slot_of(plane, z, planes):
    return plane ^ z if short_z(planes) else plane


def z_gather(block, planes):
    if not short_z(planes):
        return lax.all_gather(block, "z")
    got = [block]
    for k in range(1, planes):
        got.append(lax.ppermute(block, "z", [(i, i ^ k) for i in range(planes)]))
    return jnp.stack(got)


def z_exchange(blocks, planes):
    if not short_z(planes):
        return lax.all_to_all(blocks, "z", 0, 0)
    got = [blocks[0]]
    for k in range(1, planes):
        got.append(lax.ppermute(blocks[k], "z", [(i, i ^ k) for i in range(planes)]))
    return jnp.stack(got)


def xy_gather(block, cut_axis):
    first, second = jnp.split(block, 2, axis=cut_axis)
    first = jnp.stack([first, flip(first, "x")])
    second = jnp.stack([second, flip(second, "y")])
    first = jnp.stack([first, flip(first, "y")], axis=1)
    second = jnp.stack([second, flip(second, "x")], axis=0)
    return jnp.concatenate([first, second], axis=cut_axis + 2)


def xy_reduce(blocks, cut_axis):
    first, second = jnp.split(blocks, 2, axis=cut_axis + 2)
    add = lambda a, b: (a.astype(F32) + b.astype(F32)).astype(blocks.dtype)
    first = add(first[0], flip(first[1], "x"))
    second = add(second[:, 0], flip(second[:, 1], "y"))
    first = add(first[0], flip(first[1], "y"))
    second = add(second[0], flip(second[1], "x"))
    return jnp.concatenate([first, second], axis=cut_axis)


def by_distance(blocks, bit, axis):
    return jnp.where(bit == 0, blocks, jnp.flip(blocks, axis))


def all_sum(block, planes):
    block = block + flip(block, "c")
    block = block + flip(block, "x")
    block = block + flip(block, "y")
    if not short_z(planes):
        return lax.psum(block, "z")
    k = 1
    while k < planes:
        block = block + lax.ppermute(block, "z", [(i, i ^ k) for i in range(planes)])
        k *= 2
    return block


def norm_forward(summed, gains, offset):
    average = jnp.mean(summed, axis=-1, keepdims=True)
    centered = summed - average
    scaling = lax.rsqrt(jnp.mean(centered * centered, axis=-1, keepdims=True) + EPSILON)
    normed = centered * scaling
    return (normed * gains + offset, normed, scaling)


def norm_backward(upstream, normed, scaling, gains):
    weighted = upstream * gains
    centered = weighted - jnp.mean(weighted, axis=-1, keepdims=True)
    centered = centered - normed * jnp.mean(weighted * normed, axis=-1, keepdims=True)
    return (centered * scaling, jnp.sum(upstream * normed, axis=0), jnp.sum(upstream, axis=0))


def heads_of(array):
    return array.reshape(array.shape[0], HEADS, HEAD_DIM)


def dot(a, b):
    return jnp.dot(a, b, preferred_element_type=F32)


def dot_tn(a, b):
    return lax.dot_general(a, b, (((0,), (0,)), ((), ())), preferred_element_type=F32)


def dot_nt(a, b):
    return lax.dot_general(a, b, (((1,), (1,)), ((), ())), preferred_element_type=F32)


def scores_of(queries, keys, self_keys, allowed, self_on):
    scores = jnp.einsum("thc,shc->hts", queries, keys, preferred_element_type=F32) * SCALING
    scores = jnp.where(allowed[None], scores, NEGATIVE)
    own = jnp.einsum("thc,thc->ht", queries, self_keys, preferred_element_type=F32) * SCALING
    return (scores, jnp.where(self_on[None], own, NEGATIVE))


def layer_forward(state, mats, vecs, allowed, self_on):
    quarter = state.shape[0] // 2
    inputs = state.astype(BF16)
    queries = dot(inputs, mats[0]).astype(BF16)
    keys = dot(inputs, mats[1]).astype(BF16)
    values = dot(inputs, mats[2]).astype(BF16)
    remote = flip(jnp.concatenate([keys[:quarter], values[:quarter]], axis=1), "c")
    key_rows = jnp.concatenate([keys[:quarter], remote[:, :D]])
    value_rows = jnp.concatenate([values[:quarter], remote[:, D:]])
    scores, own = scores_of(
        heads_of(queries), heads_of(key_rows), heads_of(keys), allowed, self_on
    )
    row_max = jnp.maximum(jnp.max(scores, axis=-1), own)
    exps = jnp.exp(scores - row_max[..., None])
    own = jnp.exp(own - row_max)
    total = jnp.sum(exps, axis=-1) + own
    prob = (exps / total[..., None]).astype(BF16)
    own_prob = (own / total).astype(BF16)
    mixture = jnp.einsum("hts,shc->thc", prob, heads_of(value_rows), preferred_element_type=F32)
    mixture = mixture + own_prob.T[..., None].astype(F32) * heads_of(values).astype(F32)
    mixture = mixture.reshape(state.shape).astype(BF16)
    lse = row_max + jnp.log(total)
    first, normed_one, scale_one = norm_forward(
        state + dot(mixture, mats[3]), vecs[0:1], vecs[1:2]
    )
    first_low = first.astype(BF16)
    hidden = dot(first_low, mats[4]) + vecs[4:5]
    activated = jax.nn.gelu(hidden, approximate=False).astype(BF16)
    out, normed_two, scale_two = norm_forward(
        first + dot(activated, mats[5]) + vecs[5:6], vecs[2:3], vecs[3:4]
    )
    saved = (
        inputs, queries, keys, values, key_rows, value_rows, lse, mixture,
        normed_one, scale_one, first_low, hidden, activated, normed_two, scale_two,
    )
    return (out, saved)


def layer_backward(gradient, mats, vecs, saved, allowed, self_on):
    (
        inputs, queries, keys, values, key_rows, value_rows, lse, mixture,
        normed_one, scale_one, first_low, hidden, activated, normed_two, scale_two,
    ) = saved
    quarter = inputs.shape[0] // 2
    sum_two, gain_two, shift_two = norm_backward(gradient, normed_two, scale_two, vecs[2:3])
    low_two = sum_two.astype(BF16)
    bias_out = jnp.sum(low_two.astype(F32), axis=0)
    w_out = dot_tn(activated, low_two)
    grad_act = dot_nt(low_two, mats[5])
    _, gelu_pull = jax.vjp(lambda h: jax.nn.gelu(h, approximate=False), hidden)
    grad_hidden = gelu_pull(grad_act)[0].astype(BF16)
    bias_in = jnp.sum(grad_hidden.astype(F32), axis=0)
    w_in = dot_tn(first_low, grad_hidden)
    grad_first = sum_two + dot_nt(grad_hidden, mats[4])
    sum_one, gain_one, shift_one = norm_backward(grad_first, normed_one, scale_one, vecs[0:1])
    low_one = sum_one.astype(BF16)
    w_mix = dot_tn(mixture, low_one)
    grad_mix = heads_of(dot_nt(low_one, mats[3]).astype(BF16))
    scores, own = scores_of(
        heads_of(queries), heads_of(key_rows), heads_of(keys), allowed, self_on
    )
    prob = jnp.exp(scores - lse[..., None])
    own_prob = jnp.exp(own - lse)
    grad_prob = jnp.einsum("thc,shc->hts", grad_mix, heads_of(value_rows), preferred_element_type=F32)
    grad_own = jnp.einsum("thc,thc->ht", grad_mix, heads_of(values), preferred_element_type=F32)
    delta = jnp.sum(prob * grad_prob, axis=-1) + own_prob * grad_own
    grad_score = (prob * (grad_prob - delta[..., None])).astype(BF16)
    own_score = (own_prob * (grad_own - delta)).astype(BF16).T[..., None].astype(F32)
    grad_q = jnp.einsum("hts,shc->thc", grad_score, heads_of(key_rows), preferred_element_type=F32)
    grad_q = SCALING * (grad_q + own_score * heads_of(keys).astype(F32))
    grad_k = SCALING * jnp.einsum("hts,thc->shc", grad_score, heads_of(queries), preferred_element_type=F32)
    grad_v = jnp.einsum("hts,thc->shc", prob.astype(BF16), grad_mix, preferred_element_type=F32)
    self_k = SCALING * own_score * heads_of(queries).astype(F32)
    self_v = own_prob.astype(BF16).T[..., None].astype(F32) * grad_mix.astype(F32)
    flat = lambda a: a.reshape(a.shape[0], D)
    grad_q, grad_k, grad_v, self_k, self_v = map(flat, (grad_q, grad_k, grad_v, self_k, self_v))
    remote = flip(
        jnp.concatenate([grad_k[quarter:], grad_v[quarter:]], axis=1).astype(BF16), "c"
    ).astype(F32)
    grad_q = grad_q.astype(BF16)
    grad_k = jnp.concatenate([grad_k[:quarter] + remote[:, :D], self_k[quarter:]]).astype(BF16)
    grad_v = jnp.concatenate([grad_v[:quarter] + remote[:, D:], self_v[quarter:]]).astype(BF16)
    state_grad = sum_one + dot_nt(grad_q, mats[0]) + dot_nt(grad_k, mats[1]) + dot_nt(grad_v, mats[2])
    mat_grads = [
        dot_tn(inputs, grad_q), dot_tn(inputs, grad_k), dot_tn(inputs, grad_v), w_mix, w_in, w_out,
    ]
    vec_grads = jnp.stack([gain_one, shift_one, gain_two, shift_two, bias_in, bias_out])
    return (state_grad, [g.astype(BF16) for g in mat_grads], vec_grads)


def local(
    gene_ids, expr_bins, gene_order, cell_ids, target_bins,
    matrices, vectors, value_table, gene_table,
    matrices_mom, vectors_mom, value_mom, gene_mom,
    matrices_avg, vectors_avg, value_avg, gene_avg,
):
    planes = lax.axis_size("z")
    z, x, c, y = (lax.axis_index(a) for a in ("z", "x", "c", "y"))
    half = cell_ids.shape[2]
    quarter = half // 2
    rows_dev = gene_table.shape[0]
    vocab = rows_dev * planes * 8
    mat_rows = matrices.shape[0]

    table_low = gene_table.astype(BF16)
    plane_cells = 4 * CELLS_ROW
    targets = target_bins.astype(BF16).reshape(planes, plane_cells, rows_dev)
    if short_z(planes):
        slots = jnp.stack([lax.dynamic_index_in_dim(targets, z ^ k, 0, False) for k in range(planes)])
    else:
        slots = targets
    table_z = z_gather(table_low, planes)
    target_z = z_exchange(slots, planes)
    table_col = jnp.stack([table_z, flip(table_z, "c")])
    target_col = jnp.stack([target_z, flip(target_z, "c")])
    table_col = table_col.reshape(-1, D)
    col_rows = table_col.shape[0]
    own_rows = col_rows // 2

    codes = gene_ids[0] * 64 + expr_bins[0]
    mine = jnp.stack([codes, gene_order[0], cell_ids[0].reshape(-1)])
    mine = jnp.where(c == y, mine, flip(mine, "c"))
    codes, order, cells = mine[0], mine[1], mine[2]

    def own_part(array):
        return jnp.concatenate(
            [
                lax.dynamic_slice_in_dim(array, c * quarter, quarter),
                lax.dynamic_slice_in_dim(array, half + c * quarter, quarter),
            ]
        )

    picks = own_part(order)
    own_cells = own_part(cells)
    far_known = lax.dynamic_slice_in_dim(cells, (1 - c) * quarter, quarter)
    key_cells = jnp.concatenate([own_cells[:quarter], far_known])
    tokens = picks.shape[0]
    place = jnp.arange(codes.shape[0])
    code = jnp.sum(jnp.where(picks[:, None] == place[None, :], codes[None, :], 0), axis=1)
    genes, levels = code >> 6, code & 63
    allowed = own_cells[:, None] == key_cells[None, :]
    self_on = jnp.arange(tokens) >= quarter

    plane_genes = xy_gather(genes, 0).reshape(-1)
    owner, inner = plane_genes // rows_dev, plane_genes % rows_dev
    dist = jnp.arange(4).repeat(tokens)
    owner_xy = ((owner >> 2) & 1) * 2 + (owner & 1)
    here = owner_xy == x * 2 + y
    slot = ((owner >> 1) & 1 ^ c) * planes + slot_of(owner >> 3, z, planes)
    index = jnp.where(here, slot * rows_dev + inner, -1)
    hot = (index[:, None] == jnp.arange(col_rows)[None, :]).astype(BF16)
    found = dot(hot, table_col).astype(BF16).reshape(2, 2, tokens, D)
    embedded = xy_reduce(found, 0)
    level_hot = (levels[:, None] == jnp.arange(BINS)[None, :]).astype(F32)
    state = math.sqrt(D) * embedded.astype(F32) + jnp.dot(level_hot, value_table, precision=HIGHEST)

    mats_low = matrices.astype(BF16)
    mats_z = z_gather(mats_low, planes)
    if short_z(planes):
        mats_z = jnp.stack([lax.dynamic_index_in_dim(mats_z, z ^ p, 0, False) for p in range(planes)])
    group = planes // 2
    mats = []
    for g in range(2):
        part = mats_z[g * group : (g + 1) * group]
        part = xy_gather(part, 1)
        part = by_distance(by_distance(part, x, 0), y, 1)
        part = ordered(part, flip(part, "c"), c, 0)
        part = part.transpose(3, 1, 0, 2, 4, 5).reshape(-1, D, D)
        mats += [part[i] for i in range(part.shape[0])]

    saved = []
    for layer in range(LAYERS):
        state, kept = layer_forward(
            state, mats[6 * layer : 6 * layer + 6], vectors[layer], allowed, self_on
        )
        saved.append(kept)

    numbers = jnp.arange(CELLS_ROW)
    member = (own_cells[None, :] == numbers[:, None]).astype(F32)
    counts = jnp.sum((cells[None, :] == numbers[:, None]).astype(F32), axis=1)
    share = jnp.dot(member, state, precision=HIGHEST) / counts[:, None]
    pooled = share + flip(share, "c")
    pooled = ordered(pooled, flip(pooled, "y"), y)
    pooled = ordered(pooled, flip(pooled, "x"), x)
    pooled_low = pooled.reshape(plane_cells, D).astype(BF16)
    target_col = target_col.transpose(2, 0, 1, 3).reshape(plane_cells, col_rows).astype(F32)
    predicted = dot_nt(pooled_low, table_col)
    errors = predicted - (target_col * (4.0 / (BINS - 1)) - 2.0)
    loss_part = jnp.sum(errors[:, :own_rows] * errors[:, :own_rows])
    grad_pred = (errors * (2.0 / vocab)).astype(BF16)
    head_grad = dot_tn(grad_pred[:, :own_rows], pooled_low)
    grad_pooled = dot(grad_pred, table_col).reshape(2, 2, CELLS_ROW, D)
    grad_pooled = by_distance(by_distance(grad_pooled, x, 0), y, 1)
    grad_pooled = grad_pooled[0] + flip(grad_pooled[1], "x")
    grad_pooled = grad_pooled[0] + flip(grad_pooled[1], "y")
    gradient = lax.dot_general(
        member, grad_pooled / counts[:, None], (((0,), (0,)), ((), ())), precision=HIGHEST
    )

    mat_grads = [None] * (6 * LAYERS)
    vec_grads = [None] * LAYERS
    for layer in reversed(range(LAYERS)):
        span = slice(6 * layer, 6 * layer + 6)
        gradient, mat_grads[span], vec_grads[layer] = layer_backward(
            gradient, mats[span], vectors[layer], saved[layer], allowed, self_on
        )

    grad_value = jnp.einsum("tb,td->bd", level_hot, gradient, precision=HIGHEST)
    grad_embedded = (math.sqrt(D) * gradient).astype(BF16)
    grad_plane = xy_gather(grad_embedded, 0).reshape(-1, D)
    grad_col = dot_tn(hot, grad_plane)
    grad_own = grad_col[:own_rows] + flip(grad_col[own_rows:].astype(BF16), "c").astype(F32)
    grad_own = (grad_own + head_grad).astype(BF16).reshape(planes, rows_dev, D)
    grad_table = jnp.sum(z_exchange(grad_own, planes).astype(F32), axis=0)

    blocks = [None, None]
    for g in (1, 0):
        part = jnp.stack(mat_grads[9 * g : 9 * g + 9]).reshape(group, 2, 2, 2, mat_rows, D)
        part = jnp.where(c == 0, part, jnp.flip(part, 2))
        near, far = part[:, :, 0], part[:, :, 1]
        part = (near.astype(F32) + flip(far, "c").astype(F32)).astype(BF16)
        part = by_distance(by_distance(part.transpose(1, 2, 0, 3, 4), x, 0), y, 1)
        blocks[g] = xy_reduce(part, 1)
    blocks = jnp.concatenate(blocks)
    if short_z(planes):
        blocks = jnp.stack([lax.dynamic_index_in_dim(blocks, z ^ k, 0, False) for k in range(planes)])
    grad_matrices = jnp.sum(z_exchange(blocks, planes).astype(F32), axis=0)

    small = all_sum(jnp.concatenate([jnp.concatenate(vec_grads), grad_value]), planes)
    grad_vectors = small[: 6 * LAYERS].reshape(vectors.shape)
    grad_value = small[6 * LAYERS :]
    squares = jnp.sum(grad_matrices * grad_matrices) + jnp.sum(grad_table * grad_table)
    lanes = jnp.arange(128)[None, :]
    sums = jnp.where(lanes == 0, squares, jnp.where(lanes == 1, loss_part, 0.0))
    sums = all_sum(jnp.broadcast_to(sums, (8, 128)), planes)
    loss_sum = sums[0, 1]
    grad_norm = jnp.sqrt(sums[0, 0] + jnp.sum(small * small))
    factor = CLIP_NORM / grad_norm

    def update(weight, moment, average, grad_full):
        clipped = factor * grad_full
        moment_new = MOMENTUM * moment + clipped
        weight_new = weight - LEARN_RATE * (clipped + MOMENTUM * moment_new)
        return (
            moment_new,
            weight_new,
            AVERAGE_DECAY * average + (1.0 - AVERAGE_DECAY) * weight_new,
        )

    return (
        loss_sum,
        grad_norm,
        *update(matrices, matrices_mom, matrices_avg, grad_matrices),
        *update(vectors, vectors_mom, vectors_avg, grad_vectors),
        *update(value_table, value_mom, value_avg, grad_value),
        *update(gene_table, gene_mom, gene_avg, grad_table),
    )


def solution(mesh):
    devices = mesh.devices
    fine = Mesh(devices.reshape(devices.shape[0] // 4, 2, 2, devices.shape[1]), ("z", "x", "c", "y"))
    dp = ("z", "x", "c")
    every = ("z", "x", "c", "y")
    weights = (P(every, None), P(), P(), P(every, None))
    in_specs = (P(dp, None),) * 3 + (P(dp, None, None), P(None, every)) + weights * 3
    out_specs = (P(), P()) + (P(every, None),) * 3 + (P(),) * 6 + (P(every, None),) * 3
    return jax.shard_map(local, mesh=fine, in_specs=in_specs, out_specs=out_specs, check_vma=False)
```

time: 1140 us -> 463 us (0.41)
  waiting for transfers between devices: 700 us -> 132 us
  blocking collectives: 175 us -> 0 us
  starting transfers between devices: 26.1 us -> 74.2 us
  local copies, waits for them, and re-layouts: 22.8 us -> 48.5 us
  other arithmetic: 69.1 us -> 83.2 us
  between operations: 22.1 us -> 8.79 us
    all_gather x3 -> x0, waiting for transfers between devices: 271 us -> none  [the longest x1 127 us: local(): lax.all_gather(grad_embedded, ('dp', 'split'), axis=0, tiled=True)]
    reduce_scatter x1 -> x0, waiting for transfers between devices: 212 us -> none  [local(): lax.psum_scatter(jnp.stack(weight_grads).reshape(LAYERS * 6 * D, D), ('dp...]
    all_gather x2 -> x0, blocking collectives: 131 us -> none  [the longest x1 67.3 us: local(): lax.all_gather(cell_share, ('dp', 'split'), axis=0, tiled=True)]
    unnamed x7 -> x0, waiting for transfers between devices: 81.7 us -> none
    ppermute x12 -> x72, starting transfers between devices: 25.8 us -> 74.2 us  [the longest x53 46.6 us: flip(): return lax.ppermute(block, axis, [(0, 1), (1, 0)])]
    psum x2 -> x0, blocking collectives: 44.4 us -> none  [the longest x1 39 us: local(): loss_sum = lax.psum(loss_part, ('dp', 'split'))]
    psum x1 -> x0, waiting for transfers between devices: 37.8 us -> none  [local(): lax.psum((squares, grad_vectors, grad_value), ('dp', 'split'))]
    ppermute x12 -> x72, waiting for transfers between devices: 97.3 us -> 132 us  [the longest x53 86.9 us: flip(): return lax.ppermute(block, axis, [(0, 1), (1, 0)])]
  transfers between devices with their start and end apart: 18 -> 72, of which waited for: 18 -> 36; matrix products, arithmetic and copies ran while one was open for 6% -> 28% of each run, Pallas kernels for 0% -> 0%
where the time goes in v1:
time: 463 us; the launch traced here: 456 us
  waiting for transfers between devices  132 us (29%)
  matrix products  109 us (24%)
  other arithmetic  83.2 us (18%)
  starting transfers between devices  74.2 us (16%)
  local copies, waits for them, and re-layouts  48.5 us (10%)
  between operations  8.79 us (2%)
    ppermute x53, waiting for transfers between devices, flip(): return lax.ppermute(block, axis, [(0, 1), (1, 0)])  86.9 us
    ppermute x53, starting transfers between devices, flip(): return lax.ppermute(block, axis, [(0, 1), (1, 0)])  46.6 us
    dot_general x20, matrix products, dot(): return jnp.dot(a, b, preferred_element_type=F32)  29.4 us
    dot_general x20, matrix products, dot_tn(): lax.dot_general(a, b, (((0,), (0,)), ((), ())), preferred_element_type=F32)  26.1 us
    dot_general x19, matrix products, dot_nt(): lax.dot_general(a, b, (((1,), (1,)), ((), ())), preferred_element_type=F32)  21.5 us
    ppermute x6, waiting for transfers between devices, z_gather(): got.append(lax.ppermute(block, 'z', [(i, i ^ k) for i in range(planes)]))  17.6 us
    ppermute x9, waiting for transfers between devices, z_exchange(): lax.ppermute(blocks[k], 'z', [(i, i ^ k) for i in range(planes)])  17.3 us
    unnamed x437, local copies, waits for them, and re-layouts  13.4 us
  transfers between devices with their start and end apart: 72, of which 36 were waited for; matrix products, arithmetic and copies ran while one was open for 28% of the time, Pallas kernels for 0%

profile of v1, /device:TPU:0, one launch (start us, length us, event | category | flops | bytes accessed | tf_op | source)
XLA Modules:
  0.0 455.7 jit_solution(16226442749399854959)
XLA Ops:
  1.7 5.1 %collective-permute-start.15 = (bf16[288,512]{1,0:T(8,128)(2,1)S(1)}, bf16[288,512]{1,0:T(8,128)(2,1)S(1)}, u32[]{:S(2)}, u32[]{:S(2)}) collective-permute-start(bf16[288,512]{1,0:T(8,128)(2,1)S(1)} %convert_element_type.603), channel_id=1, source_target_pairs={{0,24},{8,16},{16,8},{24,0},{1,25},{9,17},{17,9},{25,1},{2,26},{10... | collective-permute-start | bytes 884744 | tf_op jit(solution)/shard_map/ppermute | solution.py:50
  10.8 3.8 collective-permute-start.7
  28.0 15.5 %collective-permute-done.14 = bf16[288,512]{1,0:T(8,128)(2,1)S(1)} collective-permute-done((bf16[288,512]{1,0:T(8,128)(2,1)S(1)}, bf16[288,512]{1,0:T(8,128)(2,1)S(1)}, u32[]{:S(2)}, u32[]{:S(2)}) %collective-permute-start.14) | collective-permute-done | bytes 294944 | tf_op jit(solution)/shard_map/ppermute | solution.py:50
  62.1 17.8 %collective-permute-done.25 = bf16[2,144,512]{2,1,0:T(8,128)(2,1)S(1)} collective-permute-done((bf16[2,144,512]{2,1,0:T(8,128)(2,1)S(1)}, bf16[2,144,512]{2,1,0:T(8,128)(2,1)S(1)}, u32[]{:S(2)}, u32[]{:S(2)}) %collective-permute-start.25) | collective-permute-done | bytes 294944 | tf_op jit(solution)/shard_map/ppermute | solution.py:28
  84.7 5.3 %fusion.24 = bf16[2048,512]{1,0:T(8,128)(2,1)S(1)} fusion(bf16[1920,512]{1,0:T(8,128)(2,1)S(1)} %bitcast.901, s32[2048]{0:T(1024)S(1)} %fusion.194), kind=kOutput, calls=%fused_computation.52 | convolution fusion | flops 4031512576 | bytes 4071424 | tf_op jit(solution)/shard_map/dot_general | solution.py:119
  104.5 4.4 collective-permute-done.11
  116.0 5.6 %collective-permute-done.24 = bf16[2,2,144,512]{3,2,1,0:T(8,128)(2,1)} collective-permute-done((bf16[2,2,144,512]{3,2,1,0:T(8,128)(2,1)}, bf16[2,2,144,512]{3,2,1,0:T(8,128)(2,1)}, u32[]{:S(2)}, u32[]{:S(2)}) %collective-permute-start.24) | collective-permute-done | bytes 589856 | tf_op jit(solution)/shard_map/ppermute | solution.py:28
  126.4 2.9 select_bitcast_fusion.3
  140.9 4.2 multiply_convert_fusion.6
  158.0 5.0 %multiply_convert_fusion.5 = (bf16[512,512]{1,0:T(8,128)(2,1)S(1)}, f32[512,512]{1,0:T(8,128)}, f32[512,512]{1,0:T(8,128)}) fusion(f32[512]{0:T(512)S(1)} %bitcast.1113, bf16[9,512,512]{2,1,0:T(8,128)(2,1)S(1)} %bitcast.925, f32[512,512]{0,1:T(8,128)S(1)} %get-tuple-element.210, f32[512]{0:T(512)} %bitcast.115, f32[512]{0:T(512)S(1)} %bitcast.1063, ...), kind=kOutput, calls=%fused_computation.281 | convolution fusion | flops 287047680 | bytes 4204544 | tf_op jit(solution)/shard_map/dot_general | solution.py:119
  177.6 4.4 multiply_convert_fusion.4
  222.5 2.9 convert_reduce_fusion.3
  254.3 2.8 multiply_convert_fusion.1
  310.8 4.7 %collective-permute-done.56 = bf16[256,512]{0,1:T(8,128)(2,1)S(1)} collective-permute-done((bf16[256,512]{0,1:T(8,128)(2,1)S(1)}, bf16[256,512]{0,1:T(8,128)(2,1)S(1)}, u32[]{:S(2)}, u32[]{:S(2)}) %collective-permute-start.56) | collective-permute-done | bytes 262176 | tf_op jit(solution)/shard_map/ppermute | solution.py:28
  321.1 7.9 %collective-permute-done.57 = bf16[2,256,512]{1,2,0:T(8,128)(2,1)S(1)} collective-permute-done((bf16[2,256,512]{1,2,0:T(8,128)(2,1)S(1)}, bf16[2,256,512]{1,2,0:T(8,128)(2,1)S(1)}, u32[]{:S(2)}, u32[]{:S(2)}) %collective-permute-start.57) | collective-permute-done | bytes 524320 | tf_op jit(solution)/shard_map/ppermute | solution.py:28
  333.1 6.6 %fusion = f32[1920,512]{1,0:T(8,128)S(1)} fusion(bf16[2048,512]{1,0:T(8,128)(2,1)} %bitcast.978, s32[2048]{0:T(1024)S(1)} %copy-done.187), kind=kOutput, calls=%fused_computation.1 | convolution fusion | flops 4030464000 | bytes 6037504 | tf_op jit(solution)/shard_map/dot_general | solution.py:123
  341.0 2.8 fusion.26
  350.0 5.8 %concatenate.130 = f32[69,512]{1,0:T(8,128)} concatenate(f32[1,512]{1,0:T(1,128)} %bitcast.1080, f32[1,512]{1,0:T(1,128)} %bitcast.1081, f32[1,512]{1,0:T(1,128)} %bitcast.1100, f32[1,512]{1,0:T(1,128)} %bitcast.1101, f32[1,512]{1,0:T(1,128)} %bitcast.1102, f32[1,512]{1,0:T(1,128)} %bitcast.1079, f32[1,512]{1,0:T(1,128)} %bitcast.1077, f32[1,512]{1,0:T(1,128)} %bitcast.1078, ...), dimensions={0} | concatenate | bytes 282624 | tf_op jit(solution)/shard_map/concatenate | solution.py:365
  375.3 9.5 %collective-permute-done.42 = bf16[2,2,144,512]{3,2,1,0:T(8,128)(2,1)S(1)} collective-permute-done((bf16[2,2,144,512]{3,2,1,0:T(8,128)(2,1)S(1)}, bf16[2,2,144,512]{3,2,1,0:T(8,128)(2,1)S(1)}, u32[]{:S(2)}, u32[]{:S(2)}) %collective-permute-start.42) | collective-permute-done | bytes 589856 | tf_op jit(solution)/shard_map/ppermute | solution.py:28
  387.5 4.5 collective-permute-done.48
  393.5 5.2 %collective-permute-done.43 = bf16[2,144,512]{2,1,0:T(8,128)(2,1)S(1)} collective-permute-done((bf16[2,144,512]{2,1,0:T(8,128)(2,1)S(1)}, bf16[2,144,512]{2,1,0:T(8,128)(2,1)S(1)}, u32[]{:S(2)}, u32[]{:S(2)}) %collective-permute-start.43) | collective-permute-done | bytes 294944 | tf_op jit(solution)/shard_map/ppermute | solution.py:28
  406.2 4.6 %collective-permute-done.53 = bf16[288,512]{1,0:T(8,128)(2,1)S(1)} collective-permute-done((bf16[288,512]{1,0:T(8,128)(2,1)S(1)}, bf16[288,512]{1,0:T(8,128)(2,1)S(1)}, u32[]{:S(2)}, u32[]{:S(2)}) %collective-permute-start.53) | collective-permute-done | bytes 294944 | tf_op jit(solution)/shard_map/ppermute | solution.py:59
  410.9 11.9 %collective-permute-done.52 = bf16[288,512]{1,0:T(8,128)(2,1)S(1)} collective-permute-done((bf16[288,512]{1,0:T(8,128)(2,1)S(1)}, bf16[288,512]{1,0:T(8,128)(2,1)S(1)}, u32[]{:S(2)}, u32[]{:S(2)}) %collective-permute-start.52) | collective-permute-done | bytes 294944 | tf_op jit(solution)/shard_map/ppermute | solution.py:59
  427.9 5.1 %collective-permute-done.70 = f32[69,512]{1,0:T(8,128)S(1)} collective-permute-done((f32[69,512]{1,0:T(8,128)S(1)}, f32[69,512]{1,0:T(8,128)S(1)}, u32[]{:S(2)}, u32[]{:S(2)}) %collective-permute-start.70) | collective-permute-done | bytes 141344 | tf_op jit(solution)/shard_map/ppermute | solution.py:94
  (896 shorter events, 298.6 us)
Async XLA Ops:
  1.7 25.3 %collective-permute-start.15 = (bf16[288,512]{1,0:T(8,128)(2,1)S(1)}, bf16[288,512]{1,0:T(8,128)(2,1)S(1)}, u32[]{:S(2)}, u32[]{:S(2)}) collective-permute-start(bf16[288,512]{1,0:T(8,128)(2,1)S(1)} %convert_element_type.603), channel_id=1, source_target_pairs={{0,24},{8,16},{16,8},{24,0},{1,25},{9,17},{17,9},{25,1},{2,26},{10... | collective-permute-start | bytes 884744 | tf_op jit(solution)/shard_map/ppermute | solution.py:50
  6.9 36.7 %collective-permute-start.14 = (bf16[288,512]{1,0:T(8,128)(2,1)S(1)}, bf16[288,512]{1,0:T(8,128)(2,1)S(1)}, u32[]{:S(2)}, u32[]{:S(2)}) collective-permute-start(bf16[288,512]{1,0:T(8,128)(2,1)S(1)} %convert_element_type.603), channel_id=1, source_target_pairs={{0,16},{8,24},{16,0},{24,8},{1,17},{9,25},{17,1},{25,9},{2,18},{10... | collective-permute-start | bytes 884744 | tf_op jit(solution)/shard_map/ppermute | solution.py:50
  6.9 38.1 %collective-permute-start.13 = (bf16[288,512]{1,0:T(8,128)(2,1)S(1)}, bf16[288,512]{1,0:T(8,128)(2,1)S(1)}, u32[]{:S(2)}, u32[]{:S(2)}) collective-permute-start(bf16[288,512]{1,0:T(8,128)(2,1)S(1)} %convert_element_type.603), channel_id=1, source_target_pairs={{0,8},{8,0},{16,24},{24,16},{1,9},{9,1},{17,25},{25,17},{2,10},{10... | collective-permute-start | bytes 884744 | tf_op jit(solution)/shard_map/ppermute | solution.py:50
  10.8 40.2 %collective-permute-start.7 = (bf16[240,512]{1,0:T(8,128)(2,1)S(1)}, bf16[240,512]{1,0:T(8,128)(2,1)S(1)}, u32[]{:S(2)}, u32[]{:S(2)}) collective-permute-start(bf16[240,512]{1,0:T(8,128)(2,1)S(1)} %convert_element_type.583), channel_id=1, source_target_pairs={{0,24},{8,16},{16,8},{24,0},{1,25},{9,17},{17,9},{25,1},{2,26},{10... | collective-permute-start | bytes 737288 | tf_op jit(solution)/shard_map/ppermute | solution.py:50
  27.0 26.1 %collective-permute-start.6 = (bf16[240,512]{1,0:T(8,128)(2,1)S(1)}, bf16[240,512]{1,0:T(8,128)(2,1)S(1)}, u32[]{:S(2)}, u32[]{:S(2)}) collective-permute-start(bf16[240,512]{1,0:T(8,128)(2,1)S(1)} %convert_element_type.583), channel_id=1, source_target_pairs={{0,16},{8,24},{16,0},{24,8},{1,17},{9,25},{17,1},{25,9},{2,18},{10... | collective-permute-start | bytes 737288 | tf_op jit(solution)/shard_map/ppermute | solution.py:50
  27.0 26.1 %collective-permute-start.5 = (bf16[240,512]{1,0:T(8,128)(2,1)S(1)}, bf16[240,512]{1,0:T(8,128)(2,1)S(1)}, u32[]{:S(2)}, u32[]{:S(2)}) collective-permute-start(bf16[240,512]{1,0:T(8,128)(2,1)S(1)} %convert_element_type.583), channel_id=1, source_target_pairs={{0,8},{8,0},{16,24},{24,16},{1,9},{9,1},{17,25},{25,17},{2,10},{10... | collective-permute-start | bytes 737288 | tf_op jit(solution)/shard_map/ppermute | solution.py:50
  54.6 28.8 %collective-permute-start.8 = (bf16[4,240,512]{2,1,0:T(8,128)(2,1)}, bf16[4,240,512]{2,1,0:T(8,128)(2,1)}, u32[]{:S(2)}, u32[]{:S(2)}) collective-permute-start(bf16[4,240,512]{2,1,0:T(8,128)(2,1)} %get-tuple-element.114), channel_id=1, source_target_pairs={{0,2},{2,0},{1,3},{3,1},{4,6},{6,4},{5,7},{7,5},{8,10},{10,8},{9,1... | collective-permute-start | bytes 2949128 | tf_op jit(solution)/shard_map/ppermute | solution.py:28
  56.2 25.1 %collective-permute-start.19 = (bf16[2,2,144,512]{3,2,1,0:T(8,128)(2,1)}, bf16[2,2,144,512]{3,2,1,0:T(8,128)(2,1)}, u32[]{:S(2)}, u32[]{:S(2)}) collective-permute-start(bf16[2,2,144,512]{3,2,1,0:T(8,128)(2,1)} %get-tuple-element.120), channel_id=1, source_target_pairs={{0,4},{4,0},{1,5},{5,1},{2,6},{6,2},{3,7},{7,3},{8,12},{12,8},{9,1... | collective-permute-start | bytes 1769480 | tf_op jit(solution)/shard_map/ppermute | solution.py:28
  58.0 23.2 %collective-permute-start.17 = (bf16[2,2,144,512]{3,2,1,0:T(8,128)(2,1)}, bf16[2,2,144,512]{3,2,1,0:T(8,128)(2,1)}, u32[]{:S(2)}, u32[]{:S(2)}) collective-permute-start(bf16[2,2,144,512]{3,2,1,0:T(8,128)(2,1)} %get-tuple-element.116), channel_id=1, source_target_pairs={{0,1},{1,0},{2,3},{3,2},{4,5},{5,4},{6,7},{7,6},{8,9},{9,8},{10,11... | collective-permute-start | bytes 1769480 | tf_op jit(solution)/shard_map/ppermute | solution.py:28
  60.1 19.7 %collective-permute-start.25 = (bf16[2,144,512]{2,1,0:T(8,128)(2,1)S(1)}, bf16[2,144,512]{2,1,0:T(8,128)(2,1)S(1)}, u32[]{:S(2)}, u32[]{:S(2)}) collective-permute-start(bf16[2,144,512]{2,1,0:T(8,128)(2,1)S(1)} %get-tuple-element.124), channel_id=1, source_target_pairs={{0,1},{1,0},{2,3},{3,2},{4,5},{5,4},{6,7},{7,6},{8,9},{9,8},{10,11... | collective-permute-start | bytes 884744 | tf_op jit(solution)/shard_map/ppermute | solution.py:28
  60.9 39.7 %collective-permute-start.23 = (bf16[2,144,512]{2,1,0:T(8,128)(2,1)}, bf16[2,144,512]{2,1,0:T(8,128)(2,1)}, u32[]{:S(2)}, u32[]{:S(2)}) collective-permute-start(bf16[2,144,512]{2,1,0:T(8,128)(2,1)} %get-tuple-element.123), channel_id=1, source_target_pairs={{0,4},{4,0},{1,5},{5,1},{2,6},{6,2},{3,7},{7,3},{8,12},{12,8},{9,1... | collective-permute-start | bytes 884744 | tf_op jit(solution)/shard_map/ppermute | solution.py:28
  80.7 35.2 %collective-permute-start.26 = (bf16[2,2,144,512]{3,2,0,1:T(8,128)(2,1)}, bf16[2,2,144,512]{3,2,0,1:T(8,128)(2,1)}, u32[]{:S(2)}, u32[]{:S(2)}) collective-permute-start(bf16[2,2,144,512]{3,2,0,1:T(8,128)(2,1)} %get-tuple-element.126), channel_id=1, source_target_pairs={{0,4},{4,0},{1,5},{5,1},{2,6},{6,2},{3,7},{7,3},{8,12},{12,8},{9,1... | collective-permute-start | bytes 1769480 | tf_op jit(solution)/shard_map/ppermute | solution.py:28
  98.0 28.4 %collective-permute-start.20 = (bf16[2,2,2,288,512]{4,3,1,0,2:T(8,128)(2,1)}, bf16[2,2,2,288,512]{4,3,1,0,2:T(8,128)(2,1)}, u32[]{:S(2)}, u32[]{:S(2)}) collective-permute-start(bf16[2,2,2,288,512]{4,3,1,0,2:T(8,128)(2,1)} %copy_select_fusion.1), channel_id=1, source_target_pairs={{0,2},{2,0},{1,3},{3,1},{4,6},{6,4},{5,7},{7,5},{8,10},{10,8},{9,1... | collective-permute-start | bytes 7077896 | tf_op jit(solution)/shard_map/ppermute | solution.py:28
  102.6 19.0 %collective-permute-start.24 = (bf16[2,2,144,512]{3,2,1,0:T(8,128)(2,1)}, bf16[2,2,144,512]{3,2,1,0:T(8,128)(2,1)}, u32[]{:S(2)}, u32[]{:S(2)}) collective-permute-start(bf16[2,2,144,512]{3,2,1,0:T(8,128)(2,1)} %get-tuple-element.122), channel_id=1, source_target_pairs={{0,1},{1,0},{2,3},{3,2},{4,5},{5,4},{6,7},{7,6},{8,9},{9,8},{10,11... | collective-permute-start | bytes 1769480 | tf_op jit(solution)/shard_map/ppermute | solution.py:28
  275.6 65.3 %collective-permute-start.46 = (bf16[2,2,2,288,512]{4,3,0,1,2:T(8,128)(2,1)}, bf16[2,2,2,288,512]{4,3,0,1,2:T(8,128)(2,1)}, u32[]{:S(2)}, u32[]{:S(2)}) collective-permute-start(bf16[2,2,2,288,512]{4,3,0,1,2:T(8,128)(2,1)} %slice_bitcast_fusion), channel_id=1, source_target_pairs={{0,2},{2,0},{1,3},{3,1},{4,6},{6,4},{5,7},{7,5},{8,10},{10,8},{9,1... | collective-permute-start | bytes 7077896 | tf_op jit(solution)/shard_map/ppermute | solution.py:28
  321.1 44.2 %collective-permute-start.41 = (bf16[2,2,2,288,512]{4,3,0,1,2:T(8,128)(2,1)}, bf16[2,2,2,288,512]{4,3,0,1,2:T(8,128)(2,1)}, u32[]{:S(2)}, u32[]{:S(2)}) collective-permute-start(bf16[2,2,2,288,512]{4,3,0,1,2:T(8,128)(2,1)} %slice_bitcast_fusion.2), channel_id=1, source_target_pairs={{0,2},{2,0},{1,3},{3,1},{4,6},{6,4},{5,7},{7,5},{8,10},{10,8},{9,1... | collective-permute-start | bytes 7077896 | tf_op jit(solution)/shard_map/ppermute | solution.py:28
  341.0 18.3 %collective-permute-start.58 = (bf16[960,512]{1,0:T(8,128)(2,1)}, bf16[960,512]{1,0:T(8,128)(2,1)}, u32[]{:S(2)}, u32[]{:S(2)}) collective-permute-start(bf16[960,512]{1,0:T(8,128)(2,1)} %slice.915), channel_id=1, source_target_pairs={{0,2},{2,0},{1,3},{3,1},{4,6},{6,4},{5,7},{7,5},{8,10},{10,8},{9,1... | collective-permute-start | bytes 2949128 | tf_op jit(solution)/shard_map/ppermute | solution.py:28
  345.6 16.2 %collective-permute-start.47 = (bf16[2,2,144,512]{3,2,1,0:T(8,128)(2,1)}, bf16[2,2,144,512]{3,2,1,0:T(8,128)(2,1)S(1)}, u32[]{:S(2)}, u32[]{:S(2)}) collective-permute-start(bf16[2,2,144,512]{3,2,1,0:T(8,128)(2,1)} %slice_bitcast_fusion.6), channel_id=1, source_target_pairs={{0,4},{4,0},{1,5},{5,1},{2,6},{6,2},{3,7},{7,3},{8,12},{12,8},{9,1... | collective-permute-start | bytes 1769480 | tf_op jit(solution)/shard_map/ppermute | solution.py:28
  358.3 43.2 %collective-permute-start.68 = (f32[69,512]{1,0:T(8,128)S(1)}, f32[69,512]{1,0:T(8,128)S(1)}, u32[]{:S(2)}, u32[]{:S(2)}) collective-permute-start(f32[69,512]{1,0:T(8,128)S(1)} %add.668), channel_id=1, source_target_pairs={{0,4},{4,0},{1,5},{5,1},{2,6},{6,2},{3,7},{7,3},{8,12},{12,8},{9,1... | collective-permute-start | bytes 423944 | tf_op jit(solution)/shard_map/ppermute | solution.py:28
  371.0 30.6 %collective-permute-start.61 = (bf16[240,512]{1,0:T(8,128)(2,1)S(1)}, bf16[240,512]{1,0:T(8,128)(2,1)S(1)}, u32[]{:S(2)}, u32[]{:S(2)}) collective-permute-start(bf16[240,512]{1,0:T(8,128)(2,1)S(1)} %get-tuple-element.110), channel_id=1, source_target_pairs={{0,24},{8,16},{16,8},{24,0},{1,25},{9,17},{17,9},{25,1},{2,26},{10... | collective-permute-start | bytes 737288 | tf_op jit(solution)/shard_map/ppermute | solution.py:59
  374.1 30.0 %collective-permute-start.60 = (bf16[240,512]{1,0:T(8,128)(2,1)S(1)}, bf16[240,512]{1,0:T(8,128)(2,1)S(1)}, u32[]{:S(2)}, u32[]{:S(2)}) collective-permute-start(bf16[240,512]{1,0:T(8,128)(2,1)S(1)} %get-tuple-element.111), channel_id=1, source_target_pairs={{0,16},{8,24},{16,0},{24,8},{1,17},{9,25},{17,1},{25,9},{2,18},{10... | collective-permute-start | bytes 737288 | tf_op jit(solution)/shard_map/ppermute | solution.py:59
  401.6 21.1 %collective-permute-start.52 = (bf16[288,512]{1,0:T(8,128)(2,1)S(1)}, bf16[288,512]{1,0:T(8,128)(2,1)S(1)}, u32[]{:S(2)}, u32[]{:S(2)}) collective-permute-start(bf16[288,512]{1,0:T(8,128)(2,1)S(1)} %get-tuple-element.97), channel_id=1, source_target_pairs={{0,16},{8,24},{16,0},{24,8},{1,17},{9,25},{17,1},{25,9},{2,18},{10... | collective-permute-start | bytes 884744 | tf_op jit(solution)/shard_map/ppermute | solution.py:59
  401.6 21.1 %collective-permute-start.51 = (bf16[288,512]{1,0:T(8,128)(2,1)S(1)}, bf16[288,512]{1,0:T(8,128)(2,1)S(1)}, u32[]{:S(2)}, u32[]{:S(2)}) collective-permute-start(bf16[288,512]{1,0:T(8,128)(2,1)S(1)} %get-tuple-element.98), channel_id=1, source_target_pairs={{0,8},{8,0},{16,24},{24,16},{1,9},{9,1},{17,25},{25,17},{2,10},{10... | collective-permute-start | bytes 884744 | tf_op jit(solution)/shard_map/ppermute | solution.py:59
  404.2 21.5 %collective-permute-start.69 = (f32[69,512]{1,0:T(8,128)S(1)}, f32[69,512]{1,0:T(8,128)}, u32[]{:S(2)}, u32[]{:S(2)}) collective-permute-start(f32[69,512]{1,0:T(8,128)S(1)} %add.669), channel_id=1, source_target_pairs={{0,1},{1,0},{2,3},{3,2},{4,5},{5,4},{6,7},{7,6},{8,9},{9,8},{10,11... | collective-permute-start | bytes 423944 | tf_op jit(solution)/shard_map/ppermute | solution.py:28
  (269 other events, 2619.6 us)

commit v2 on v1

--- a/solution.py
+++ b/solution.py
@@ -3,6 +3,8 @@
 import jax
 import jax.numpy as jnp
 from jax import lax
+from jax.experimental import pallas as pl
+from jax.experimental.pallas import tpu as pltpu
 from jax.sharding import Mesh, PartitionSpec as P
 
 D = 512
@@ -11,6 +13,7 @@
 BINS = 51
 LAYERS = 3
 CELLS_ROW = 4
+PAIR = 128
 
 EPSILON = 1e-05
 NEGATIVE = -1e30
@@ -96,132 +99,337 @@
     return block
 
 
-def norm_forward(summed, gains, offset):
+LIMIT = 16 * 2**20
+
+
+def call(body, outs, args, scratch=(), flops=10**9):
+    size = lambda a: math.prod(a.shape) * a.dtype.itemsize
+    shapes = [jax.ShapeDtypeStruct(*o) for o in outs]
+    return pl.pallas_call(
+        body,
+        out_shape=shapes,
+        scratch_shapes=list(scratch),
+        compiler_params=pltpu.CompilerParams(vmem_limit_bytes=LIMIT),
+        cost_estimate=pl.CostEstimate(
+            flops=flops,
+            bytes_accessed=sum(map(size, args)) + sum(map(size, shapes)),
+            transcendentals=0,
+        ),
+    )(*args)
+
+
+def dot(a, b):
+    return jnp.dot(a, b, preferred_element_type=F32)
+
+
+def dot_tn(a, b):
+    return lax.dot_general(a, b, (((0,), (0,)), ((), ())), preferred_element_type=F32)
+
+
+def dot_nt(a, b):
+    return lax.dot_general(a, b, (((1,), (1,)), ((), ())), preferred_element_type=F32)
+
+
+def head_marks(width):
+    rows = lax.broadcasted_iota(jnp.int32, (D, width), 0) // HEAD_DIM
+    return (rows == lax.broadcasted_iota(jnp.int32, (D, width), 1)).astype(F32)
+
+
+def lane_marks(side, value):
+    lanes = lax.broadcasted_iota(jnp.int32, (1, PAIR), 1) // HEAD_DIM
+    return jnp.where(lanes == side, value, 0.0)
+
+
+def norm(summed):
     average = jnp.mean(summed, axis=-1, keepdims=True)
     centered = summed - average
     scaling = lax.rsqrt(jnp.mean(centered * centered, axis=-1, keepdims=True) + EPSILON)
-    normed = centered * scaling
-    return (normed * gains + offset, normed, scaling)
-
-
-def norm_backward(upstream, normed, scaling, gains):
-    weighted = upstream * gains
+    return (centered * scaling, scaling)
+
+
+def norm_pull(weighted, normed, scaling):
     centered = weighted - jnp.mean(weighted, axis=-1, keepdims=True)
-    centered = centered - normed * jnp.mean(weighted * normed, axis=-1, keepdims=True)
-    return (centered * scaling, jnp.sum(upstream * normed, axis=0), jnp.sum(upstream, axis=0))
-
-
-def heads_of(array):
-    return array.reshape(array.shape[0], HEADS, HEAD_DIM)
-
-
-def dot(a, b):
-    return jnp.dot(a, b, preferred_element_type=F32)
-
-
-def dot_tn(a, b):
-    return lax.dot_general(a, b, (((0,), (0,)), ((), ())), preferred_element_type=F32)
-
-
-def dot_nt(a, b):
-    return lax.dot_general(a, b, (((1,), (1,)), ((), ())), preferred_element_type=F32)
-
-
-def scores_of(queries, keys, self_keys, allowed, self_on):
-    scores = jnp.einsum("thc,shc->hts", queries, keys, preferred_element_type=F32) * SCALING
-    scores = jnp.where(allowed[None], scores, NEGATIVE)
-    own = jnp.einsum("thc,thc->ht", queries, self_keys, preferred_element_type=F32) * SCALING
-    return (scores, jnp.where(self_on[None], own, NEGATIVE))
-
-
-def layer_forward(state, mats, vecs, allowed, self_on):
-    quarter = state.shape[0] // 2
-    inputs = state.astype(BF16)
-    queries = dot(inputs, mats[0]).astype(BF16)
-    keys = dot(inputs, mats[1]).astype(BF16)
-    values = dot(inputs, mats[2]).astype(BF16)
-    remote = flip(jnp.concatenate([keys[:quarter], values[:quarter]], axis=1), "c")
-    key_rows = jnp.concatenate([keys[:quarter], remote[:, :D]])
-    value_rows = jnp.concatenate([values[:quarter], remote[:, D:]])
-    scores, own = scores_of(
-        heads_of(queries), heads_of(key_rows), heads_of(keys), allowed, self_on
-    )
-    row_max = jnp.maximum(jnp.max(scores, axis=-1), own)
-    exps = jnp.exp(scores - row_max[..., None])
-    own = jnp.exp(own - row_max)
-    total = jnp.sum(exps, axis=-1) + own
-    prob = (exps / total[..., None]).astype(BF16)
-    own_prob = (own / total).astype(BF16)
-    mixture = jnp.einsum("hts,shc->thc", prob, heads_of(value_rows), preferred_element_type=F32)
-    mixture = mixture + own_prob.T[..., None].astype(F32) * heads_of(values).astype(F32)
-    mixture = mixture.reshape(state.shape).astype(BF16)
-    lse = row_max + jnp.log(total)
-    first, normed_one, scale_one = norm_forward(
-        state + dot(mixture, mats[3]), vecs[0:1], vecs[1:2]
-    )
-    first_low = first.astype(BF16)
-    hidden = dot(first_low, mats[4]) + vecs[4:5]
-    activated = jax.nn.gelu(hidden, approximate=False).astype(BF16)
-    out, normed_two, scale_two = norm_forward(
-        first + dot(activated, mats[5]) + vecs[5:6], vecs[2:3], vecs[3:4]
-    )
-    saved = (
-        inputs, queries, keys, values, key_rows, value_rows, lse, mixture,
-        normed_one, scale_one, first_low, hidden, activated, normed_two, scale_two,
-    )
-    return (out, saved)
-
-
-def layer_backward(gradient, mats, vecs, saved, allowed, self_on):
-    (
-        inputs, queries, keys, values, key_rows, value_rows, lse, mixture,
-        normed_one, scale_one, first_low, hidden, activated, normed_two, scale_two,
-    ) = saved
-    quarter = inputs.shape[0] // 2
-    sum_two, gain_two, shift_two = norm_backward(gradient, normed_two, scale_two, vecs[2:3])
-    low_two = sum_two.astype(BF16)
-    bias_out = jnp.sum(low_two.astype(F32), axis=0)
-    w_out = dot_tn(activated, low_two)
-    grad_act = dot_nt(low_two, mats[5])
-    _, gelu_pull = jax.vjp(lambda h: jax.nn.gelu(h, approximate=False), hidden)
-    grad_hidden = gelu_pull(grad_act)[0].astype(BF16)
-    bias_in = jnp.sum(grad_hidden.astype(F32), axis=0)
-    w_in = dot_tn(first_low, grad_hidden)
-    grad_first = sum_two + dot_nt(grad_hidden, mats[4])
-    sum_one, gain_one, shift_one = norm_backward(grad_first, normed_one, scale_one, vecs[0:1])
-    low_one = sum_one.astype(BF16)
-    w_mix = dot_tn(mixture, low_one)
-    grad_mix = heads_of(dot_nt(low_one, mats[3]).astype(BF16))
-    scores, own = scores_of(
-        heads_of(queries), heads_of(key_rows), heads_of(keys), allowed, self_on
-    )
-    prob = jnp.exp(scores - lse[..., None])
-    own_prob = jnp.exp(own - lse)
-    grad_prob = jnp.einsum("thc,shc->hts", grad_mix, heads_of(value_rows), preferred_element_type=F32)
-    grad_own = jnp.einsum("thc,thc->ht", grad_mix, heads_of(values), preferred_element_type=F32)
-    delta = jnp.sum(prob * grad_prob, axis=-1) + own_prob * grad_own
-    grad_score = (prob * (grad_prob - delta[..., None])).astype(BF16)
-    own_score = (own_prob * (grad_own - delta)).astype(BF16).T[..., None].astype(F32)
-    grad_q = jnp.einsum("hts,shc->thc", grad_score, heads_of(key_rows), preferred_element_type=F32)
-    grad_q = SCALING * (grad_q + own_score * heads_of(keys).astype(F32))
-    grad_k = SCALING * jnp.einsum("hts,thc->shc", grad_score, heads_of(queries), preferred_element_type=F32)
-    grad_v = jnp.einsum("hts,thc->shc", prob.astype(BF16), grad_mix, preferred_element_type=F32)
-    self_k = SCALING * own_score * heads_of(queries).astype(F32)
-    self_v = own_prob.astype(BF16).T[..., None].astype(F32) * grad_mix.astype(F32)
-    flat = lambda a: a.reshape(a.shape[0], D)
-    grad_q, grad_k, grad_v, self_k, self_v = map(flat, (grad_q, grad_k, grad_v, self_k, self_v))
-    remote = flip(
-        jnp.concatenate([grad_k[quarter:], grad_v[quarter:]], axis=1).astype(BF16), "c"
-    ).astype(F32)
-    grad_q = grad_q.astype(BF16)
-    grad_k = jnp.concatenate([grad_k[:quarter] + remote[:, :D], self_k[quarter:]]).astype(BF16)
-    grad_v = jnp.concatenate([grad_v[:quarter] + remote[:, D:], self_v[quarter:]]).astype(BF16)
-    state_grad = sum_one + dot_nt(grad_q, mats[0]) + dot_nt(grad_k, mats[1]) + dot_nt(grad_v, mats[2])
-    mat_grads = [
-        dot_tn(inputs, grad_q), dot_tn(inputs, grad_k), dot_tn(inputs, grad_v), w_mix, w_in, w_out,
-    ]
-    vec_grads = jnp.stack([gain_one, shift_one, gain_two, shift_two, bias_in, bias_out])
-    return (state_grad, [g.astype(BF16) for g in mat_grads], vec_grads)
+    return scaling * (centered - normed * jnp.mean(weighted * normed, axis=-1, keepdims=True))
+
+
+def project_kernel(x_ref, wq_ref, wk_ref, wv_ref, q_ref, k_ref, v_ref, near_ref):
+    quarter = near_ref.shape[0]
+    low = x_ref[...].astype(BF16)
+    keys = dot(low, wk_ref[...]).astype(BF16)
+    values = dot(low, wv_ref[...]).astype(BF16)
+    k_ref[...] = keys
+    v_ref[...] = values
+    near_ref[:, :D] = keys[:quarter]
+    near_ref[:, D:] = values[:quarter]
+    q_ref[...] = dot(low, wq_ref[...]).astype(BF16)
+
+
+def join_keys(k_ref, v_ref, far_ref, keys_ref, values_ref):
+    quarter = far_ref.shape[0]
+    keys_ref[:quarter] = k_ref[:quarter]
+    keys_ref[quarter:] = far_ref[:, :D]
+    values_ref[:quarter] = v_ref[:quarter]
+    values_ref[quarter:] = far_ref[:, D:]
+
+
+def weigh(marks, array):
+    return lax.dot_general(
+        marks, array, (((0,), (1,)), ((), ())), preferred_element_type=F32, precision=HIGHEST
+    )[:HEADS]
+
+
+def spread(marks, array):
+    return lax.dot_general(
+        array.astype(BF16), marks[:, :HEADS].astype(BF16), (((0,), (1,)), ((), ())),
+        preferred_element_type=F32,
+    )
+
+
+def forward_kernel(
+    x_ref, q_ref, k_ref, v_ref, far_ref, own_row_ref, key_col_ref, wo_ref, w1_ref, w2_ref, vec_ref,
+    out_ref, mix_ref, lse_ref, u1_ref, r1_ref, low1_ref, slope_ref, act_ref, u2_ref, r2_ref,
+    keys_ref, values_ref, bias_ref, own_ref, wide_ref, turned_ref,
+):
+    tokens = x_ref.shape[0]
+    quarter = far_ref.shape[0]
+    far_half = slice(quarter, tokens)
+    keys_ref[:quarter] = k_ref[:quarter]
+    keys_ref[quarter:] = far_ref[:, :D]
+    values_ref[:, :quarter] = v_ref[:quarter].T
+    values_ref[:, quarter:] = far_ref[:, D:].T
+    bias_ref[...] = jnp.where(key_col_ref[...] == own_row_ref[...], 0.0, NEGATIVE)
+    marks = head_marks(PAIR)
+    product = q_ref[far_half].astype(F32) * k_ref[far_half].astype(F32) * SCALING
+    own_ref[...] = weigh(marks, product)
+
+    def pair_step(pair, carry):
+        lanes = pl.ds(pl.multiple_of(pair * PAIR, PAIR), PAIR)
+        key_pair = keys_ref[:, lanes]
+        q_pair = q_ref[:, lanes]
+        for side in range(2):
+            head = pl.ds(2 * pair + side, 1)
+            scores = dot_nt(key_pair, q_pair * lane_marks(side, SCALING).astype(BF16))
+            scores = scores + bias_ref[...]
+            top = jnp.max(scores, axis=0, keepdims=True)
+            own = own_ref[head, :]
+            top = jnp.concatenate([top[:, :quarter], jnp.maximum(top[:, quarter:], own)], axis=1)
+            exps = jnp.exp(scores - top)
+            own = jnp.exp(own - top[:, quarter:])
+            amount = jnp.sum(exps, axis=0, keepdims=True)
+            amount = jnp.concatenate([amount[:, :quarter], amount[:, quarter:] + own], axis=1)
+            inverse = 1.0 / amount
+            own_ref[head, :] = own * inverse[:, quarter:]
+            lse_ref[head, :] = top + jnp.log(amount)
+            prob = (exps * inverse).astype(BF16)
+            part = pl.ds(pl.multiple_of(pair * PAIR + side * HEAD_DIM, HEAD_DIM), HEAD_DIM)
+            turned_ref[part, :] = dot(values_ref[part, :], prob)
+        return carry
+
+    lax.fori_loop(0, D // PAIR, pair_step, 0)
+    wide_ref[...] = turned_ref[...].T
+    own_share = spread(marks, own_ref[...]) * v_ref[far_half].astype(F32)
+    mix_ref[:quarter] = wide_ref[:quarter].astype(BF16)
+    mix_ref[far_half] = (wide_ref[far_half] + own_share).astype(BF16)
+    for start in range(0, tokens, quarter):
+        rows = slice(start, start + quarter)
+        normed, scaling = norm(x_ref[rows] + dot(mix_ref[rows], wo_ref[...]))
+        u1_ref[rows] = normed
+        r1_ref[rows] = scaling
+        first = normed * vec_ref[0:1] + vec_ref[1:2]
+        first_low = first.astype(BF16)
+        low1_ref[rows] = first_low
+        hidden = dot(first_low, w1_ref[...]) + vec_ref[4:5]
+        share = 0.5 + 0.5 * lax.erf(hidden * math.sqrt(0.5))
+        active = (hidden * share).astype(BF16)
+        act_ref[rows] = active
+        density = jnp.exp(-0.5 * hidden * hidden) * (1.0 / math.sqrt(2.0 * math.pi))
+        slope_ref[rows] = share + hidden * density
+        normed, scaling = norm(first + dot(active, w2_ref[...]) + vec_ref[5:6])
+        u2_ref[rows] = normed
+        r2_ref[rows] = scaling
+        out_ref[rows] = normed * vec_ref[2:3] + vec_ref[3:4]
+
+
+def backward_kernel(
+    grad_ref, u2_ref, r2_ref, slope_ref, u1_ref, r1_ref, q_ref, k_ref, v_ref, far_ref, lse_ref,
+    own_row_ref, key_col_ref, wo_ref, w1_ref, w2_ref, vec_ref,
+    sum1_ref, low2_ref, hid_ref, low1_ref, gq_ref, gk_ref, gv_ref, send_ref, gvec_ref,
+    keys_ref, values_ref, bias_ref, gmix_ref, own_p_ref, own_s_ref, turned_ref, wide_ref,
+):
+    tokens = grad_ref.shape[0]
+    quarter = far_ref.shape[0]
+    join_keys(k_ref, v_ref, far_ref, keys_ref, values_ref)
+    turned_ref[...] = keys_ref[...].T
+    bias_ref[...] = jnp.where(key_col_ref[...] == own_row_ref[...], 0.0, NEGATIVE)
+    sums = [jnp.zeros((1, D), F32) for _ in range(6)]
+
+    def gather(index, value):
+        sums[index] = sums[index] + jnp.sum(value, axis=0, keepdims=True)
+
+    for start in range(0, tokens, quarter):
+        rows = slice(start, start + quarter)
+        upstream = grad_ref[rows]
+        normed = u2_ref[rows]
+        gather(2, upstream * normed)
+        gather(3, upstream)
+        sum_two = norm_pull(upstream * vec_ref[2:3], normed, r2_ref[rows])
+        low_two = sum_two.astype(BF16)
+        low2_ref[rows] = low_two
+        gather(5, low_two.astype(F32))
+        hid = (dot_nt(low_two, w2_ref[...]) * slope_ref[rows]).astype(BF16)
+        hid_ref[rows] = hid
+        gather(4, hid.astype(F32))
+        upstream = sum_two + dot_nt(hid, w1_ref[...])
+        normed = u1_ref[rows]
+        gather(0, upstream * normed)
+        gather(1, upstream)
+        sum_one = norm_pull(upstream * vec_ref[0:1], normed, r1_ref[rows])
+        sum1_ref[rows] = sum_one
+        low_one = sum_one.astype(BF16)
+        low1_ref[rows] = low_one
+        gmix_ref[rows] = dot_nt(low_one, wo_ref[...]).astype(BF16)
+    gvec_ref[...] = jnp.concatenate(sums + [jnp.zeros((2, D), F32)])
+
+    marks = head_marks(PAIR)
+    far_half = slice(quarter, tokens)
+    queries = q_ref[far_half].astype(F32)
+    mixed = gmix_ref[far_half].astype(F32)
+    product = queries * k_ref[far_half].astype(F32) * SCALING
+    own_prob = jnp.exp(weigh(marks, product) - lse_ref[:, far_half])
+    own_grad = weigh(marks, mixed * v_ref[far_half].astype(F32))
+    own_p_ref[...] = own_prob
+    own_s_ref[...] = own_grad
+
+    def pair_step(pair, carry):
+        lanes = pl.ds(pl.multiple_of(pair * PAIR, PAIR), PAIR)
+        key_pair = keys_ref[:, lanes]
+        value_pair = values_ref[:, lanes]
+        q_pair = q_ref[:, lanes]
+        mix_pair = gmix_ref[:, lanes]
+        grad_k = jnp.zeros((tokens, PAIR), F32)
+        grad_v = jnp.zeros((tokens, PAIR), F32)
+        for side in range(2):
+            head = 2 * pair + side
+            scaled = q_pair * lane_marks(side, SCALING).astype(BF16)
+            mix_side = mix_pair * lane_marks(side, 1.0).astype(BF16)
+            lse = lse_ref[pl.ds(head, 1), :]
+            prob = jnp.exp(dot_nt(key_pair, scaled) + bias_ref[...] - lse)
+            grad_p = dot_nt(value_pair, mix_side)
+            delta = jnp.sum(prob * grad_p, axis=0, keepdims=True)
+            own_p = own_p_ref[pl.ds(head, 1), :]
+            own_g = own_s_ref[pl.ds(head, 1), :]
+            delta = jnp.concatenate([delta[:, :quarter], delta[:, quarter:] + own_p * own_g], axis=1)
+            own_s_ref[pl.ds(head, 1), :] = own_p * (own_g - delta[:, quarter:])
+            grad_s = (prob * (grad_p - delta)).astype(BF16)
+            grad_k = grad_k + dot(grad_s, scaled)
+            grad_v = grad_v + dot(prob.astype(BF16), mix_side)
+            part = pl.ds(pl.multiple_of(pair * PAIR + side * HEAD_DIM, HEAD_DIM), HEAD_DIM)
+            wide_ref[part, :] = dot(turned_ref[part, :], grad_s)
+        gk_ref[:, lanes] = grad_k
+        gv_ref[:, lanes] = grad_v
+        return carry
+
+    lax.fori_loop(0, D // PAIR, pair_step, 0)
+    send_ref[:, :D] = gk_ref[quarter:].astype(BF16)
+    send_ref[:, D:] = gv_ref[quarter:].astype(BF16)
+    own_score = spread(marks, own_s_ref[...]) * SCALING
+    gv_ref[far_half] = spread(marks, own_p_ref[...]) * mixed
+    gk_ref[far_half] = own_score * queries
+    grad_q = wide_ref[...].T * SCALING
+    gq_ref[:quarter] = grad_q[:quarter].astype(BF16)
+    gq_ref[far_half] = (grad_q[far_half] + own_score * k_ref[far_half].astype(F32)).astype(BF16)
+
+
+def weights_kernel(x_ref, gq_ref, mix_ref, g1_ref, h_ref, gz_ref, act_ref, g2_ref, out_ref):
+    out_ref[0] = dot_tn(x_ref[...].astype(BF16), gq_ref[...]).astype(BF16)
+    out_ref[1] = dot_tn(mix_ref[...], g1_ref[...]).astype(BF16)
+    out_ref[2] = dot_tn(h_ref[...], gz_ref[...]).astype(BF16)
+    out_ref[3] = dot_tn(act_ref[...], g2_ref[...]).astype(BF16)
+
+
+def inputs_kernel(
+    x_ref, sum1_ref, gq_ref, gk_ref, gv_ref, got_ref, wq_ref, wk_ref, wv_ref,
+    grad_ref, out_ref, low_k_ref, low_v_ref,
+):
+    quarter = got_ref.shape[0]
+    low_k_ref[:quarter] = (gk_ref[:quarter] + got_ref[:, :D].astype(F32)).astype(BF16)
+    low_v_ref[:quarter] = (gv_ref[:quarter] + got_ref[:, D:].astype(F32)).astype(BF16)
+    low_k_ref[quarter:] = gk_ref[quarter:].astype(BF16)
+    low_v_ref[quarter:] = gv_ref[quarter:].astype(BF16)
+    grad_ref[...] = (
+        sum1_ref[...]
+        + dot_nt(gq_ref[...], wq_ref[...])
+        + dot_nt(low_k_ref[...], wk_ref[...])
+        + dot_nt(low_v_ref[...], wv_ref[...])
+    )
+    low = x_ref[...].astype(BF16)
+    out_ref[0] = dot_tn(low, low_k_ref[...]).astype(BF16)
+    out_ref[1] = dot_tn(low, low_v_ref[...]).astype(BF16)
+
+
+def layer_forward(state, mats, vecs, places):
+    tokens = state.shape[0]
+    quarter = tokens // 2
+    own_col, own_row, key_col, key_row = places
+    wide = ((tokens, D), F32)
+    slim = ((tokens, D), BF16)
+    queries, keys, values, near = call(
+        project_kernel, [slim, slim, slim, ((quarter, 2 * D), BF16)], (state, *mats[:3])
+    )
+    far = flip(near, "c")
+    col = ((tokens, 1), F32)
+    out, mix, lse, u1, r1, low1, slope, act, u2, r2 = call(
+        forward_kernel,
+        [wide, slim, ((HEADS, tokens), F32), wide, col, slim, wide, slim, wide, col],
+        (state, queries, keys, values, far, own_row, key_col, *mats[3:], vecs),
+        [
+            pltpu.VMEM((tokens, D), BF16),
+            pltpu.VMEM((tokens, D), BF16),
+            pltpu.VMEM((tokens, tokens), F32),
+            pltpu.VMEM((HEADS, quarter), F32),
+            pltpu.VMEM((tokens, D), F32),
+            pltpu.VMEM((D, tokens), F32),
+        ],
+        4 * 10**9,
+    )
+    return (out, (state, queries, keys, values, far, mix, lse, u1, r1, low1, slope, act, u2, r2))
+
+
+def layer_backward(gradient, mats, vecs, saved, places):
+    state, queries, keys, values, far, mix, lse, u1, r1, low1, slope, act, u2, r2 = saved
+    tokens = state.shape[0]
+    quarter = tokens // 2
+    own_col, own_row, key_col, key_row = places
+    wide = ((tokens, D), F32)
+    slim = ((tokens, D), BF16)
+    sum1, g2, gz, g1, gq, gk, gv, send, gvec = call(
+        backward_kernel,
+        [wide, slim, slim, slim, slim, wide, wide, ((quarter, 2 * D), BF16), ((8, D), F32)],
+        (gradient, u2, r2, slope, u1, r1, queries, keys, values, far, lse, own_row, key_col, *mats[3:], vecs),
+        [
+            pltpu.VMEM((tokens, D), BF16),
+            pltpu.VMEM((tokens, D), BF16),
+            pltpu.VMEM((tokens, tokens), F32),
+            pltpu.VMEM((tokens, D), BF16),
+            pltpu.VMEM((HEADS, quarter), F32),
+            pltpu.VMEM((HEADS, quarter), F32),
+            pltpu.VMEM((D, tokens), BF16),
+            pltpu.VMEM((D, tokens), F32),
+        ],
+        8 * 10**9,
+    )
+    got = flip(send, "c")
+    (part_one,) = call(
+        weights_kernel, [((4, D, D), BF16)], (state, gq, mix, g1, low1, gz, act, g2)
+    )
+    grad, part_two = call(
+        inputs_kernel,
+        [wide, ((2, D, D), BF16)],
+        (state, sum1, gq, gk, gv, got, *mats[:3]),
+        [pltpu.VMEM((tokens, D), BF16), pltpu.VMEM((tokens, D), BF16)],
+    )
+    mat_grads = [part_one[0], part_two[0], part_two[1], part_one[1], part_one[2], part_one[3]]
+    return (grad, mat_grads, gvec[:6])
 
 
 def local(
@@ -274,8 +482,7 @@
     place = jnp.arange(codes.shape[0])
     code = jnp.sum(jnp.where(picks[:, None] == place[None, :], codes[None, :], 0), axis=1)
     genes, levels = code >> 6, code & 63
-    allowed = own_cells[:, None] == key_cells[None, :]
-    self_on = jnp.arange(tokens) >= quarter
+    places = (own_cells[:, None], own_cells[None, :], key_cells[:, None], key_cells[None, :])
 
     plane_genes = xy_gather(genes, 0).reshape(-1)
     owner, inner = plane_genes // rows_dev, plane_genes % rows_dev
@@ -307,7 +514,7 @@
     saved = []
     for layer in range(LAYERS):
         state, kept = layer_forward(
-            state, mats[6 * layer : 6 * layer + 6], vectors[layer], allowed, self_on
+            state, mats[6 * layer : 6 * layer + 6], vectors[layer], places
         )
         saved.append(kept)
 
@@ -338,7 +545,7 @@
     for layer in reversed(range(LAYERS)):
         span = slice(6 * layer, 6 * layer + 6)
         gradient, mat_grads[span], vec_grads[layer] = layer_backward(
-            gradient, mats[span], vectors[layer], saved[layer], allowed, self_on
+            gradient, mats[span], vectors[layer], saved[layer], places
         )
 
     grad_value = jnp.einsum("tb,td->bd", level_hot, gradient, precision=HIGHEST)

time: 463 us -> 413 us (0.89)
  matrix products: 109 us -> 18.4 us
  Pallas kernels: 0 us -> 72.3 us
  other arithmetic: 83.2 us -> 42 us
  starting transfers between devices: 74.2 us -> 96.3 us
  local copies, waits for them, and re-layouts: 48.5 us -> 40.8 us
    pallas_call x0 -> x15, Pallas kernels: none -> 72.3 us  [call(): pl.pallas_call(body, out_shape=shapes, scratch_shapes=list(scratch), comp...]
    dot_general x18 -> x0, matrix products: 27.3 us -> none  [the longest x3 6.97 us: layer_backward(): jnp.einsum('thc,shc->hts', grad_mix, heads_of(value_rows), preferred_elem...]
    dot_general x20 -> x2, matrix products: 29.4 us -> 7.1 us  [dot(): return jnp.dot(a, b, preferred_element_type=F32)]
    dot_general x20 -> x2, matrix products: 26.1 us -> 5.41 us  [dot_tn(): lax.dot_general(a, b, (((0,), (0,)), ((), ())), preferred_element_type=F32)]
    dot_general x19 -> x1, matrix products: 21.5 us -> 2.88 us  [dot_nt(): lax.dot_general(a, b, (((1,), (1,)), ((), ())), preferred_element_type=F32)]
    unnamed x437 -> x269, local copies, waits for them, and re-layouts: 13.4 us -> 27.5 us
    convert_element_type x11 -> x1, other arithmetic: 12.5 us -> 0.13 us  [local(): grad_embedded = (math.sqrt(D) * gradient).astype(BF16)]
    ppermute x9, starting transfers between devices: 12.7 us -> 25 us  [z_exchange(): lax.ppermute(blocks[k], 'z', [(i, i ^ k) for i in range(planes)])]
  transfers between devices with their start and end apart: 72 -> 72, of which waited for: 36 -> 35; matrix products, arithmetic and copies ran while one was open for 28% -> 14% of each run, Pallas kernels for 0% -> 2%
where the time goes in v2:
time: 413 us; the launch traced here: 408 us
  waiting for transfers between devices  131 us (32%)
  starting transfers between devices  96.3 us (23%)
  Pallas kernels  72.3 us (18%)
  other arithmetic  42 us (10%)
  local copies, waits for them, and re-layouts  40.8 us (10%)
  matrix products  18.4 us (4%)
  between operations  7.17 us (2%)
    ppermute x53, waiting for transfers between devices, flip(): return lax.ppermute(block, axis, [(0, 1), (1, 0)])  96.7 us
    pallas_call x15, Pallas kernels, call(): pl.pallas_call(body, out_shape=shapes, scratch_shapes=list(scratch), comp...  72.3 us
    ppermute x53, starting transfers between devices, flip(): return lax.ppermute(block, axis, [(0, 1), (1, 0)])  56.6 us
    unnamed x269, local copies, waits for them, and re-layouts  27.5 us
    ppermute x9, starting transfers between devices, z_exchange(): lax.ppermute(blocks[k], 'z', [(i, i ^ k) for i in range(planes)])  25 us
    ppermute x9, waiting for transfers between devices, z_exchange(): lax.ppermute(blocks[k], 'z', [(i, i ^ k) for i in range(planes)])  19.4 us
    ppermute x6, starting transfers between devices, z_gather(): got.append(lax.ppermute(block, 'z', [(i, i ^ k) for i in range(planes)]))  10.3 us
    ppermute x4, waiting for transfers between devices, all_sum(): lax.ppermute(block, 'z', [(i, i ^ k) for i in range(planes)])  9.17 us
  transfers between devices with their start and end apart: 72, of which 35 were waited for; matrix products, arithmetic and copies ran while one was open for 14% of the time, Pallas kernels for 2%

profile of v2, /device:TPU:0, one launch (start us, length us, event | category | flops | bytes accessed | tf_op | source)
XLA Modules:
  0.0 407.9 jit_solution(7119812535463372553)
XLA Ops:
  26.1 4.0 collective-permute-done.15
  31.9 8.4 %collective-permute-start.18 = (bf16[2,144,512]{2,1,0:T(8,128)(2,1)S(1)}, bf16[2,144,512]{2,1,0:T(8,128)(2,1)S(1)}, u32[]{:S(2)}, u32[]{:S(2)}) collective-permute-start(bf16[2,144,512]{2,1,0:T(8,128)(2,1)S(1)} %get-tuple-element.231), channel_id=1, source_target_pairs={{0,1},{1,0},{2,3},{3,2},{4,5},{5,4},{6,7},{7,6},{8,9},{9,8},{10,11... | collective-permute-start | bytes 884744 | tf_op jit(solution)/shard_map/ppermute | solution.py:31
  40.4 5.7 %collective-permute-done.18 = bf16[2,144,512]{2,1,0:T(8,128)(2,1)S(1)} collective-permute-done((bf16[2,144,512]{2,1,0:T(8,128)(2,1)S(1)}, bf16[2,144,512]{2,1,0:T(8,128)(2,1)S(1)}, u32[]{:S(2)}, u32[]{:S(2)}) %collective-permute-start.18) | collective-permute-done | bytes 294944 | tf_op jit(solution)/shard_map/ppermute | solution.py:31
  57.0 11.3 %collective-permute-done.17 = bf16[2,2,144,512]{3,2,1,0:T(8,128)(2,1)S(1)} collective-permute-done((bf16[2,2,144,512]{3,2,1,0:T(8,128)(2,1)S(1)}, bf16[2,2,144,512]{3,2,1,0:T(8,128)(2,1)S(1)}, u32[]{:S(2)}, u32[]{:S(2)}) %collective-permute-start.17) | collective-permute-done | bytes 589856 | tf_op jit(solution)/shard_map/ppermute | solution.py:31
  71.7 5.0 %fusion.6 = bf16[2048,512]{1,0:T(8,128)(2,1)S(1)} fusion(bf16[1920,512]{1,0:T(8,128)(2,1)S(1)} %bitcast.332, s32[2048]{0:T(1024)S(1)} %fusion.37), kind=kOutput, calls=%fused_computation.21 | convolution fusion | flops 4031512576 | bytes 4071424 | tf_op jit(solution)/shard_map/dot_general | solution.py:122
  80.3 10.8 %collective-permute-done.9 = bf16[2,256,512]{2,1,0:T(8,128)(2,1)S(1)} collective-permute-done((bf16[2,256,512]{2,1,0:T(8,128)(2,1)S(1)}, bf16[2,256,512]{2,1,0:T(8,128)(2,1)S(1)}, u32[]{:S(2)}, u32[]{:S(2)}) %collective-permute-start.9) | collective-permute-done | bytes 524320 | tf_op jit(solution)/shard_map/ppermute | solution.py:31
  97.4 4.0 collective-permute-done.12
  116.9 4.5 %select_bitcast_fusion.1 = (bf16[1,2,2,2,288,512]{5,4,3,2,1,0:T(8,128)(2,1)S(1)}, bf16[1,2,2,2,288,512]{5,4,3,2,1,0:T(8,128)(2,1)S(1)}) fusion(bf16[2,2,2,288,512]{4,3,2,1,0:T(8,128)(2,1)} %collective-permute-done.27, pred[]{:T(512)S(6)} %eq.134, bf16[2,2,2,288,512]{4,3,2,1,0:T(8,128)(2,1)} %copy-done.113, pred[]{:T(512)S(6)} %eq.132), kind=kLoop, calls=%fused_computation.33 | loop fusion | flops 3538944 | bytes 9437186 | tf_op jit(solution)/shard_map/stack | solution.py:37
  123.2 8.4 %shard_map.273 = (f32[512,512]{1,0:T(8,128)S(1)}, bf16[512,512]{1,0:T(8,128)(2,1)S(1)}, f32[8,512]{1,0:T(8,128)S(1)}, f32[512,512]{1,0:T(8,128)S(1)}, f32[512,1]...) custom-call(f32[512,512]{1,0:T(8,128)S(1)} %convolution_add_fusion.x, ...), custom_call_target="tpu_custom_call" | custom-call | flops 4000000000 | bytes 10522624 | tf_op jit(solution)/shard_map/pallas_call | solution.py:108
  137.4 8.2 %shard_map.275 = (f32[512,512]{1,0:T(8,128)S(1)}, bf16[512,512]{1,0:T(8,128)(2,1)S(1)}, f32[8,512]{1,0:T(8,128)S(1)}, f32[512,512]{1,0:T(8,128)S(1)}, f32[512,1]...) custom-call(f32[512,512]{1,0:T(8,128)S(1)} %get-tuple-element.93.x_r, ...), custom_call_target="tpu_custom_call" | custom-call | flops 4000000000 | bytes 10522624 | tf_op jit(solution)/shard_map/pallas_call | solution.py:108
  150.6 8.7 %shard_map.277 = (f32[512,512]{1,0:T(8,128)S(1)}, bf16[512,512]{1,0:T(8,128)(2,1)S(1)}, f32[8,512]{1,0:T(8,128)S(1)}, f32[512,512]{1,0:T(8,128)S(1)}, f32[512,1]...) custom-call(f32[512,512]{1,0:T(8,128)S(1)} %get-tuple-element.98.x_r, ...), custom_call_target="tpu_custom_call" | custom-call | flops 4000000000 | bytes 10522624 | tf_op jit(solution)/shard_map/pallas_call | solution.py:108
  168.8 9.9 %collective-permute-start.33 = (bf16[16,240]{1,0:T(8,128)(2,1)S(1)}, bf16[16,240]{1,0:T(8,128)(2,1)S(1)}, u32[]{:S(2)}, u32[]{:S(2)}) collective-permute-start(bf16[16,240]{1,0:T(8,128)(2,1)S(1)} %get-tuple-element.249), channel_id=1, source_target_pairs={{0,16},{8,24},{16,0},{24,8},{1,17},{9,25},{17,1},{25,9},{2,18},{10... | collective-permute-start | bytes 23048 | tf_op jit(solution)/shard_map/ppermute | solution.py:62
  209.0 11.8 %shard_map.278 = (f32[512,512]{1,0:T(8,128)S(1)}, bf16[512,512]{1,0:T(8,128)(2,1)S(1)}, bf16[512,512]{1,0:T(8,128)(2,1)S(1)}, bf16[512,512]{1,0:T(8,128)(2,1)S(1...) custom-call(f32[512,512]{1,0:T(8,128)S(1)} %fusion.34.grad_ref, ...), custom_call_target="tpu_custom_call" | custom-call | flops 8000000000 | bytes 13684736 | tf_op jit(solution)/shard_map/pallas_call | solution.py:108
  227.4 11.7 %shard_map.280 = (f32[512,512]{1,0:T(8,128)S(1)}, bf16[512,512]{1,0:T(8,128)(2,1)S(1)}, bf16[512,512]{1,0:T(8,128)(2,1)S(1)}, bf16[512,512]{1,0:T(8,128)(2,1)S(1...) custom-call(f32[512,512]{1,0:T(8,128)S(1)} %get-tuple-element.115.gr, ...), custom_call_target="tpu_custom_call" | custom-call | flops 8000000000 | bytes 13684736 | tf_op jit(solution)/shard_map/pallas_call | solution.py:108
  248.0 11.9 %shard_map.282 = (f32[512,512]{1,0:T(8,128)S(1)}, bf16[512,512]{1,0:T(8,128)(2,1)S(1)}, bf16[512,512]{1,0:T(8,128)(2,1)S(1)}, bf16[512,512]{1,0:T(8,128)(2,1)S(1...) custom-call(f32[512,512]{1,0:T(8,128)S(1)} %get-tuple-element.127.gr, ...), custom_call_target="tpu_custom_call" | custom-call | flops 8000000000 | bytes 13684736 | tf_op jit(solution)/shard_map/pallas_call | solution.py:108
  268.8 5.2 %collective-permute-done.56 = bf16[256,512]{1,0:T(8,128)(2,1)S(1)} collective-permute-done((bf16[256,512]{1,0:T(8,128)(2,1)S(1)}, bf16[256,512]{1,0:T(8,128)(2,1)S(1)}, u32[]{:S(2)}, u32[]{:S(2)}) %collective-permute-start.56) | collective-permute-done | bytes 262176 | tf_op jit(solution)/shard_map/ppermute | solution.py:31
  278.5 9.1 %collective-permute-done.57 = bf16[2,256,512]{2,1,0:T(8,128)(2,1)S(1)} collective-permute-done((bf16[2,256,512]{2,1,0:T(8,128)(2,1)S(1)}, bf16[2,256,512]{2,1,0:T(8,128)(2,1)S(1)}, u32[]{:S(2)}, u32[]{:S(2)}) %collective-permute-start.57) | collective-permute-done | bytes 524320 | tf_op jit(solution)/shard_map/ppermute | solution.py:31
  288.8 5.0 %fusion = f32[1920,512]{1,0:T(8,128)S(1)} fusion(bf16[2048,512]{1,0:T(8,128)(2,1)S(1)} %bitcast.339, s32[2048]{0:T(1024)S(1)} %fusion.37), kind=kOutput, calls=%fused_computation.1 | convolution fusion | flops 4030464000 | bytes 6037504 | tf_op jit(solution)/shard_map/dot_general | solution.py:126
  300.4 12.0 %collective-permute-done.47 = bf16[2,2,144,512]{3,2,1,0:T(8,128)(2,1)S(1)} collective-permute-done((bf16[2,2,144,512]{3,2,1,0:T(8,128)(2,1)S(1)}, bf16[2,2,144,512]{3,2,1,0:T(8,128)(2,1)S(1)}, u32[]{:S(2)}, u32[]{:S(2)}) %collective-permute-start.47) | collective-permute-done | bytes 589856 | tf_op jit(solution)/shard_map/ppermute | solution.py:31
  326.2 8.0 %collective-permute-done.42 = bf16[2,2,144,512]{3,2,1,0:T(8,128)(2,1)S(1)} collective-permute-done((bf16[2,2,144,512]{3,2,1,0:T(8,128)(2,1)S(1)}, bf16[2,2,144,512]{3,2,1,0:T(8,128)(2,1)S(1)}, u32[]{:S(2)}, u32[]{:S(2)}) %collective-permute-start.42) | collective-permute-done | bytes 589856 | tf_op jit(solution)/shard_map/ppermute | solution.py:31
  337.2 4.4 %collective-permute-done.48 = bf16[2,144,512]{2,1,0:T(8,128)(2,1)S(1)} collective-permute-done((bf16[2,144,512]{2,1,0:T(8,128)(2,1)S(1)}, bf16[2,144,512]{2,1,0:T(8,128)(2,1)S(1)}, u32[]{:S(2)}, u32[]{:S(2)}) %collective-permute-start.48) | collective-permute-done | bytes 294944 | tf_op jit(solution)/shard_map/ppermute | solution.py:31
  356.2 4.6 %collective-permute-done.53 = bf16[288,512]{1,0:T(8,128)(2,1)S(1)} collective-permute-done((bf16[288,512]{1,0:T(8,128)(2,1)S(1)}, bf16[288,512]{1,0:T(8,128)(2,1)S(1)}, u32[]{:S(2)}, u32[]{:S(2)}) %collective-permute-start.53) | collective-permute-done | bytes 294944 | tf_op jit(solution)/shard_map/ppermute | solution.py:62
  360.8 13.3 %collective-permute-done.52 = bf16[288,512]{1,0:T(8,128)(2,1)S(1)} collective-permute-done((bf16[288,512]{1,0:T(8,128)(2,1)S(1)}, bf16[288,512]{1,0:T(8,128)(2,1)S(1)}, u32[]{:S(2)}, u32[]{:S(2)}) %collective-permute-start.52) | collective-permute-done | bytes 294944 | tf_op jit(solution)/shard_map/ppermute | solution.py:62
  379.4 4.1 %collective-permute-done.70 = f32[69,512]{1,0:T(8,128)S(1)} collective-permute-done((f32[69,512]{1,0:T(8,128)S(1)}, f32[69,512]{1,0:T(8,128)S(1)}, u32[]{:S(2)}, u32[]{:S(2)}) %collective-permute-start.70) | collective-permute-done | bytes 141344 | tf_op jit(solution)/shard_map/ppermute | solution.py:97
  (554 shorter events, 211.1 us)
Async XLA Ops:
  4.4 20.8 %collective-permute-start.14 = (bf16[288,512]{1,0:T(8,128)(2,1)S(1)}, bf16[288,512]{1,0:T(8,128)(2,1)S(1)}, u32[]{:S(2)}, u32[]{:S(2)}) collective-permute-start(bf16[288,512]{1,0:T(8,128)(2,1)S(1)} %convert_element_type.245), channel_id=1, source_target_pairs={{0,16},{8,24},{16,0},{24,8},{1,17},{9,25},{17,1},{25,9},{2,18},{10... | collective-permute-start | bytes 884744 | tf_op jit(solution)/shard_map/ppermute | solution.py:53
  8.1 18.0 %collective-permute-start.13 = (bf16[288,512]{1,0:T(8,128)(2,1)S(1)}, bf16[288,512]{1,0:T(8,128)(2,1)S(1)}, u32[]{:S(2)}, u32[]{:S(2)}) collective-permute-start(bf16[288,512]{1,0:T(8,128)(2,1)S(1)} %convert_element_type.245), channel_id=1, source_target_pairs={{0,8},{8,0},{16,24},{24,16},{1,9},{9,1},{17,25},{25,17},{2,10},{10... | collective-permute-start | bytes 884744 | tf_op jit(solution)/shard_map/ppermute | solution.py:53
  9.7 20.4 %collective-permute-start.15 = (bf16[288,512]{1,0:T(8,128)(2,1)S(1)}, bf16[288,512]{1,0:T(8,128)(2,1)S(1)}, u32[]{:S(2)}, u32[]{:S(2)}) collective-permute-start(bf16[288,512]{1,0:T(8,128)(2,1)S(1)} %convert_element_type.245), channel_id=1, source_target_pairs={{0,24},{8,16},{16,8},{24,0},{1,25},{9,17},{17,9},{25,1},{2,26},{10... | collective-permute-start | bytes 884744 | tf_op jit(solution)/shard_map/ppermute | solution.py:53
  21.1 29.7 %collective-permute-start.6 = (bf16[240,512]{1,0:T(8,128)(2,1)}, bf16[240,512]{1,0:T(8,128)(2,1)S(1)}, u32[]{:S(2)}, u32[]{:S(2)}) collective-permute-start(bf16[240,512]{1,0:T(8,128)(2,1)} %convert_element_type.226), channel_id=1, source_target_pairs={{0,16},{8,24},{16,0},{24,8},{1,17},{9,25},{17,1},{25,9},{2,18},{10... | collective-permute-start | bytes 737288 | tf_op jit(solution)/shard_map/ppermute | solution.py:53
  22.8 29.8 %collective-permute-start.5 = (bf16[240,512]{1,0:T(8,128)(2,1)}, bf16[240,512]{1,0:T(8,128)(2,1)}, u32[]{:S(2)}, u32[]{:S(2)}) collective-permute-start(bf16[240,512]{1,0:T(8,128)(2,1)} %convert_element_type.226), channel_id=1, source_target_pairs={{0,8},{8,0},{16,24},{24,16},{1,9},{9,1},{17,25},{25,17},{2,10},{10... | collective-permute-start | bytes 737288 | tf_op jit(solution)/shard_map/ppermute | solution.py:53
  25.3 28.8 %collective-permute-start.7 = (bf16[240,512]{1,0:T(8,128)(2,1)}, bf16[240,512]{1,0:T(8,128)(2,1)}, u32[]{:S(2)}, u32[]{:S(2)}) collective-permute-start(bf16[240,512]{1,0:T(8,128)(2,1)} %convert_element_type.226), channel_id=1, source_target_pairs={{0,24},{8,16},{16,8},{24,0},{1,25},{9,17},{17,9},{25,1},{2,26},{10... | collective-permute-start | bytes 737288 | tf_op jit(solution)/shard_map/ppermute | solution.py:53
  30.4 17.3 %collective-permute-start.16 = (bf16[2,144,512]{2,1,0:T(8,128)(2,1)S(1)}, bf16[2,144,512]{2,1,0:T(8,128)(2,1)S(1)}, u32[]{:S(2)}, u32[]{:S(2)}) collective-permute-start(bf16[2,144,512]{2,1,0:T(8,128)(2,1)S(1)} %get-tuple-element.230), channel_id=1, source_target_pairs={{0,4},{4,0},{1,5},{5,1},{2,6},{6,2},{3,7},{7,3},{8,12},{12,8},{9,1... | collective-permute-start | bytes 884744 | tf_op jit(solution)/shard_map/ppermute | solution.py:31
  50.8 17.6 %collective-permute-start.17 = (bf16[2,2,144,512]{3,2,1,0:T(8,128)(2,1)S(1)}, bf16[2,2,144,512]{3,2,1,0:T(8,128)(2,1)S(1)}, u32[]{:S(2)}, u32[]{:S(2)}) collective-permute-start(bf16[2,2,144,512]{3,2,1,0:T(8,128)(2,1)S(1)} %get-tuple-element.229), channel_id=1, source_target_pairs={{0,1},{1,0},{2,3},{3,2},{4,5},{5,4},{6,7},{7,6},{8,9},{9,8},{10,11... | collective-permute-start | bytes 1769480 | tf_op jit(solution)/shard_map/ppermute | solution.py:31
  52.6 16.3 %collective-permute-start.19 = (bf16[2,2,144,512]{3,2,1,0:T(8,128)(2,1)S(1)}, bf16[2,2,144,512]{3,2,1,0:T(8,128)(2,1)S(1)}, u32[]{:S(2)}, u32[]{:S(2)}) collective-permute-start(bf16[2,2,144,512]{3,2,1,0:T(8,128)(2,1)S(1)} %get-tuple-element.233), channel_id=1, source_target_pairs={{0,4},{4,0},{1,5},{5,1},{2,6},{6,2},{3,7},{7,3},{8,12},{12,8},{9,1... | collective-permute-start | bytes 1769480 | tf_op jit(solution)/shard_map/ppermute | solution.py:31
  55.6 24.1 %collective-permute-start.24 = (bf16[2,2,144,512]{3,2,1,0:T(8,128)(2,1)S(1)}, bf16[2,2,144,512]{3,2,1,0:T(8,128)(2,1)S(1)}, u32[]{:S(2)}, u32[]{:S(2)}) collective-permute-start(bf16[2,2,144,512]{3,2,1,0:T(8,128)(2,1)S(1)} %get-tuple-element.223), channel_id=1, source_target_pairs={{0,1},{1,0},{2,3},{3,2},{4,5},{5,4},{6,7},{7,6},{8,9},{9,8},{10,11... | collective-permute-start | bytes 1769480 | tf_op jit(solution)/shard_map/ppermute | solution.py:31
  56.4 23.3 %collective-permute-start.26 = (bf16[2,2,144,512]{3,2,1,0:T(8,128)(2,1)S(1)}, bf16[2,2,144,512]{3,2,1,0:T(8,128)(2,1)S(1)}, u32[]{:S(2)}, u32[]{:S(2)}) collective-permute-start(bf16[2,2,144,512]{3,2,1,0:T(8,128)(2,1)S(1)} %get-tuple-element.227), channel_id=1, source_target_pairs={{0,4},{4,0},{1,5},{5,1},{2,6},{6,2},{3,7},{7,3},{8,12},{12,8},{9,1... | collective-permute-start | bytes 1769480 | tf_op jit(solution)/shard_map/ppermute | solution.py:31
  71.5 35.9 %collective-permute-start.20 = (bf16[2,2,2,288,512]{4,3,2,1,0:T(8,128)(2,1)}, bf16[2,2,2,288,512]{4,3,2,1,0:T(8,128)(2,1)}, u32[]{:S(2)}, u32[]{:S(2)}) collective-permute-start(bf16[2,2,2,288,512]{4,3,2,1,0:T(8,128)(2,1)} %reverse_select_fusion.7), channel_id=1, source_target_pairs={{0,2},{2,0},{1,3},{3,1},{4,6},{6,4},{5,7},{7,5},{8,10},{10,8},{9,1... | collective-permute-start | bytes 7077896 | tf_op jit(solution)/shard_map/ppermute | solution.py:31
  96.0 20.9 %collective-permute-start.27 = (bf16[2,2,2,288,512]{4,3,2,1,0:T(8,128)(2,1)}, bf16[2,2,2,288,512]{4,3,2,1,0:T(8,128)(2,1)}, u32[]{:S(2)}, u32[]{:S(2)}) collective-permute-start(bf16[2,2,2,288,512]{4,3,2,1,0:T(8,128)(2,1)} %reverse_select_fusion.5), channel_id=1, source_target_pairs={{0,2},{2,0},{1,3},{3,1},{4,6},{6,4},{5,7},{7,5},{8,10},{10,8},{9,1... | collective-permute-start | bytes 7077896 | tf_op jit(solution)/shard_map/ppermute | solution.py:31
  260.2 33.8 %collective-permute-start.46 = (bf16[2,2,2,288,512]{4,3,0,1,2:T(8,128)(2,1)S(1)}, bf16[2,2,2,288,512]{4,3,0,1,2:T(8,128)(2,1)S(1)}, u32[]{:S(2)}, u32[]{:S(2)}) collective-permute-start(bf16[2,2,2,288,512]{4,3,0,1,2:T(8,128)(2,1)S(1)} %slice_bitcast_fusion), channel_id=1, source_target_pairs={{0,2},{2,0},{1,3},{3,1},{4,6},{6,4},{5,7},{7,5},{8,10},{10,8},{9,1... | collective-permute-start | bytes 7077896 | tf_op jit(solution)/shard_map/ppermute | solution.py:31
  265.1 33.6 %collective-permute-start.67 = (f32[69,512]{1,0:T(8,128)S(1)}, f32[69,512]{1,0:T(8,128)S(1)}, u32[]{:S(2)}, u32[]{:S(2)}) collective-permute-start(f32[69,512]{1,0:T(8,128)S(1)} %pad_maximum_fusion.13), channel_id=1, source_target_pairs={{0,2},{2,0},{1,3},{3,1},{4,6},{6,4},{5,7},{7,5},{8,10},{10,8},{9,1... | collective-permute-start | bytes 423944 | tf_op jit(solution)/shard_map/ppermute | solution.py:31
  278.4 35.7 %collective-permute-start.41 = (bf16[2,2,2,288,512]{4,3,0,1,2:T(8,128)(2,1)S(1)}, bf16[2,2,2,288,512]{4,3,0,1,2:T(8,128)(2,1)S(1)}, u32[]{:S(2)}, u32[]{:S(2)}) collective-permute-start(bf16[2,2,2,288,512]{4,3,0,1,2:T(8,128)(2,1)S(1)} %slice_bitcast_fusion.2), channel_id=1, source_target_pairs={{0,2},{2,0},{1,3},{3,1},{4,6},{6,4},{5,7},{7,5},{8,10},{10,8},{9,1... | collective-permute-start | bytes 7077896 | tf_op jit(solution)/shard_map/ppermute | solution.py:31
  298.7 52.4 %collective-permute-start.68 = (f32[69,512]{1,0:T(8,128)S(1)}, f32[69,512]{1,0:T(8,128)S(1)}, u32[]{:S(2)}, u32[]{:S(2)}) collective-permute-start(f32[69,512]{1,0:T(8,128)S(1)} %fusion.67), channel_id=1, source_target_pairs={{0,4},{4,0},{1,5},{5,1},{2,6},{6,2},{3,7},{7,3},{8,12},{12,8},{9,1... | collective-permute-start | bytes 423944 | tf_op jit(solution)/shard_map/ppermute | solution.py:31
  316.0 18.2 %collective-permute-start.42 = (bf16[2,2,144,512]{3,2,1,0:T(8,128)(2,1)S(1)}, bf16[2,2,144,512]{3,2,1,0:T(8,128)(2,1)S(1)}, u32[]{:S(2)}, u32[]{:S(2)}) collective-permute-start(bf16[2,2,144,512]{3,2,1,0:T(8,128)(2,1)S(1)} %slice_bitcast_fusion.10), channel_id=1, source_target_pairs={{0,4},{4,0},{1,5},{5,1},{2,6},{6,2},{3,7},{7,3},{8,12},{12,8},{9,1... | collective-permute-start | bytes 1769480 | tf_op jit(solution)/shard_map/ppermute | solution.py:31
  317.2 18.5 %collective-permute-start.44 = (bf16[2,2,144,512]{3,2,1,0:T(8,128)(2,1)S(1)}, bf16[2,2,144,512]{3,2,1,0:T(8,128)(2,1)S(1)}, u32[]{:S(2)}, u32[]{:S(2)}) collective-permute-start(bf16[2,2,144,512]{3,2,1,0:T(8,128)(2,1)S(1)} %slice_bitcast_fusion.8), channel_id=1, source_target_pairs={{0,1},{1,0},{2,3},{3,2},{4,5},{5,4},{6,7},{7,6},{8,9},{9,8},{10,11... | collective-permute-start | bytes 1769480 | tf_op jit(solution)/shard_map/ppermute | solution.py:31
  318.5 33.1 %collective-permute-start.61 = (bf16[240,512]{1,0:T(8,128)(2,1)S(1)}, bf16[240,512]{1,0:T(8,128)(2,1)S(1)}, u32[]{:S(2)}, u32[]{:S(2)}) collective-permute-start(bf16[240,512]{1,0:T(8,128)(2,1)S(1)} %get-tuple-element.217), channel_id=1, source_target_pairs={{0,24},{8,16},{16,8},{24,0},{1,25},{9,17},{17,9},{25,1},{2,26},{10... | collective-permute-start | bytes 737288 | tf_op jit(solution)/shard_map/ppermute | solution.py:62
  323.2 30.5 %collective-permute-start.60 = (bf16[240,512]{1,0:T(8,128)(2,1)S(1)}, bf16[240,512]{1,0:T(8,128)(2,1)S(1)}, u32[]{:S(2)}, u32[]{:S(2)}) collective-permute-start(bf16[240,512]{1,0:T(8,128)(2,1)S(1)} %get-tuple-element.218), channel_id=1, source_target_pairs={{0,16},{8,24},{16,0},{24,8},{1,17},{9,25},{17,1},{25,9},{2,18},{10... | collective-permute-start | bytes 737288 | tf_op jit(solution)/shard_map/ppermute | solution.py:62
  351.1 23.0 %collective-permute-start.52 = (bf16[288,512]{1,0:T(8,128)(2,1)S(1)}, bf16[288,512]{1,0:T(8,128)(2,1)S(1)}, u32[]{:S(2)}, u32[]{:S(2)}) collective-permute-start(bf16[288,512]{1,0:T(8,128)(2,1)S(1)} %get-tuple-element.210), channel_id=1, source_target_pairs={{0,16},{8,24},{16,0},{24,8},{1,17},{9,25},{17,1},{25,9},{2,18},{10... | collective-permute-start | bytes 884744 | tf_op jit(solution)/shard_map/ppermute | solution.py:62
  351.7 22.5 %collective-permute-start.51 = (bf16[288,512]{1,0:T(8,128)(2,1)S(1)}, bf16[288,512]{1,0:T(8,128)(2,1)S(1)}, u32[]{:S(2)}, u32[]{:S(2)}) collective-permute-start(bf16[288,512]{1,0:T(8,128)(2,1)S(1)} %get-tuple-element.211), channel_id=1, source_target_pairs={{0,8},{8,0},{16,24},{24,16},{1,9},{9,1},{17,25},{25,17},{2,10},{10... | collective-permute-start | bytes 884744 | tf_op jit(solution)/shard_map/ppermute | solution.py:62
  353.7 23.4 %collective-permute-start.69 = (f32[69,512]{1,0:T(8,128)S(1)}, f32[69,512]{1,0:T(8,128)S(1)}, u32[]{:S(2)}, u32[]{:S(2)}) collective-permute-start(f32[69,512]{1,0:T(8,128)S(1)} %add.258), channel_id=1, source_target_pairs={{0,1},{1,0},{2,3},{3,2},{4,5},{5,4},{6,7},{7,6},{8,9},{9,8},{10,11... | collective-permute-start | bytes 423944 | tf_op jit(solution)/shard_map/ppermute | solution.py:31
  (181 other events, 1042.8 us)

commit v3 on v2

v3 whole, which is shorter than its diff:
```python
from functools import partial
import itertools
import math

import jax
import jax.numpy as jnp
from jax import lax
from jax.experimental import pallas as pl
from jax.experimental.pallas import tpu as pltpu
from jax.sharding import Mesh, PartitionSpec as P

D = 512
HEADS = 8
HEAD_DIM = 64
BINS = 51
LAYERS = 3
CELLS_ROW = 4
PAIR = 128
SLOT = 256

EPSILON = 1e-05
NEGATIVE = -1e30
LEARN_RATE = 200.0
MOMENTUM = 0.9
AVERAGE_DECAY = 0.7
CLIP_NORM = 0.25
HIGHEST = lax.Precision.HIGHEST
SCALING = 1.0 / math.sqrt(HEAD_DIM)
F32 = jnp.float32
BF16 = jnp.bfloat16


def flip(block, axis):
    return lax.ppermute(block, axis, [(0, 1), (1, 0)])


def after(values, *needed):
    values, tree = jax.tree.flatten(values)
    needed = jax.tree.leaves(needed)
    if not needed:
        return tree.unflatten(values)
    anywhere = pl.BlockSpec(memory_space=pl.ANY)
    values = pl.pallas_call(
        lambda *refs: None,
        out_shape=[jax.ShapeDtypeStruct(v.shape, v.dtype) for v in values],
        in_specs=[anywhere] * (len(values) + len(needed)),
        out_specs=[anywhere] * len(values),
        input_output_aliases={i: i for i in range(len(values))},
    )(*values, *needed)
    return tree.unflatten(values)


def ordered(own, other, bit, axis=0):
    low = jnp.where(bit == 0, own, other)
    high = jnp.where(bit == 0, other, own)
    return jnp.stack([low, high], axis=axis)


def pick(pair, bit, axis=0):
    first = lax.index_in_dim(pair, 0, axis, False)
    second = lax.index_in_dim(pair, 1, axis, False)
    return jnp.where(bit == 0, first, second)


def short_z(planes):
    return planes == 4


def slot_of(plane, z, planes):
    return plane ^ z if short_z(planes) else plane


def z_swap(block, k, planes, targets=None):
    pairs = [(p ^ k, p) for p in range(planes) if targets is None or p in targets]
    return lax.ppermute(block, "z", pairs)


def xy_gather(block, cut_axis):
    first, second = jnp.split(block, 2, axis=cut_axis)
    early = (flip(first, "x"), flip(second, "y"))
    first = jnp.stack([first, early[0]])
    second = jnp.stack([second, early[1]])
    first = jnp.stack([first, flip(first, "y")], axis=1)
    second = jnp.stack([second, flip(second, "x")], axis=0)
    return (jnp.concatenate([first, second], axis=cut_axis + 2), early)


def rounded_sum(a, b):
    return (a.astype(F32) + b.astype(F32)).astype(a.dtype)


def xy_reduce(blocks, cut_axis):
    first, second = jnp.split(blocks, 2, axis=cut_axis + 2)
    early = (flip(first[1], "x"), flip(second[:, 1], "y"))
    first = rounded_sum(first[0], early[0])
    second = rounded_sum(second[:, 0], early[1])
    first = rounded_sum(first[0], flip(first[1], "y"))
    second = rounded_sum(second[0], flip(second[1], "x"))
    return (jnp.concatenate([first, second], axis=cut_axis), early)


def by_distance(blocks, bit, axis):
    return jnp.where(bit == 0, blocks, jnp.flip(blocks, axis))


class PlaneGather:
    def __init__(self, block, x, y, c):
        self.block, self.bits = block, (x, y, c)

    def one(self, *needed):
        first, second = after(tuple(jnp.split(self.block, 2, axis=1)), *needed)
        self.early = (flip(first, "x"), flip(second, "y"))
        self.halves = (
            ordered(first, self.early[0], self.bits[0], 1),
            ordered(second, self.early[1], self.bits[1], 1),
        )

    def two(self, *needed):
        first, second = after(self.halves, *needed)
        first = ordered(first, flip(first, "y"), self.bits[1], 2)
        second = ordered(second, flip(second, "x"), self.bits[0], 1)
        self.block = jnp.concatenate([first, second], axis=3)

    def three(self, base, store, *needed):
        block = after(self.block, *needed)
        count = 2 * block.size // (D * D)
        return call(
            partial(join_kernel, base), [], (block, flip(block, "c")), [pltpu.VMEM((D, D), BF16)] * count,
            scalars=(self.bits[2][None],), store=store, fresh=store is None,
        )[-1]


class PlaneReduce:
    def __init__(self, near, far, x, y):
        self.bits = (x, y)
        self.block = rounded_sum(near, flip(far, "c"))

    def one(self, *needed):
        x, y = self.bits
        first, second = jnp.split(self.block, 2, axis=3)
        far = after((pick(first, 1 - x, 1), pick(second, 1 - y, 2)), *needed)
        first = rounded_sum(pick(first, x, 1), flip(far[0], "x"))
        second = rounded_sum(pick(second, y, 2), flip(far[1], "y"))
        self.halves = (first, second)

    def two(self, *needed):
        x, y = self.bits
        first, second = self.halves
        far = after((pick(first, 1 - y, 1), pick(second, 1 - x, 1)), *needed)
        first = rounded_sum(pick(first, y, 1), flip(far[0], "y"))
        second = rounded_sum(pick(second, x, 1), flip(far[1], "x"))
        return jnp.concatenate([first, second], axis=1)


def owner_sum(blocks, group, z, planes):
    if not short_z(planes):
        return jnp.sum(lax.all_to_all(blocks, "z", 0, 0).astype(F32), axis=0)
    odd = z & 1
    held = pick(blocks, odd).astype(F32) + z_swap(pick(blocks, 1 - odd), 1, planes).astype(F32)
    got = z_swap(held.astype(BF16), 2, planes, (2 * group, 2 * group + 1))
    return jnp.where(z >> 1 == group, held, 0.0) + got.astype(F32)


def small_sum(block, x, y, z, planes):
    block = block + flip(block, "c")
    near = [block] + [
        lax.ppermute(block, ("x", "y"), [(i, i ^ k) for i in range(4)]) for k in range(1, 4)
    ]
    near = jnp.stack(near)
    at = lambda stack, i: lax.dynamic_index_in_dim(stack, i, 0, False)
    place = 2 * x + y
    block = sum(at(near, place ^ i) for i in range(4))
    if not short_z(planes):
        return lax.psum(block, "z")
    far = jnp.stack([block] + [z_swap(block, k, planes) for k in range(1, planes)])
    return sum(at(far, z ^ i) for i in range(planes))


def all_sum(block, planes):
    for axis in ("c", "x", "y"):
        block = block + flip(block, axis)
    if not short_z(planes):
        return lax.psum(block, "z")
    k = 1
    while k < planes:
        block = block + z_swap(block, k, planes)
        k *= 2
    return block


LIMIT = 40 * 2**20
COST = 10**9
STORE = 132


class Moves:
    def __init__(self, sources, buffers, fetch_sems, store, save_sems):
        self.copies = [
            pltpu.make_async_copy(source, buffer, fetch_sems.at[i])
            for i, (source, buffer) in enumerate(zip(sources, buffers))
        ]
        for copy in self.copies:
            copy.start()
        self.buffers, self.waiting = buffers, set(range(len(buffers)))
        self.store, self.sems, self.saves = store, save_sems, []

    def get(self, i):
        if i in self.waiting:
            self.copies[i].wait()
            self.waiting.remove(i)
        return self.buffers[i]

    def put(self, square, ref, rows=None):
        target = self.store.at[square]
        if rows is not None:
            target = target.at[rows]
        copy = pltpu.make_async_copy(ref, target, self.sems.at[len(self.saves)])
        copy.start()
        self.saves.append(copy)

    def finish(self):
        for i in sorted(self.waiting):
            self.copies[i].wait()
        for copy in self.saves:
            copy.wait()


def call(body, outs, args, scratch=(), needed=(), scalars=(), fetch=(), store=None, fresh=False):
    needed = jax.tree.leaves(needed)
    saving = fresh or store is not None
    shapes = [jax.ShapeDtypeStruct(*o) for o in outs]
    if saving:
        shapes.append(jax.ShapeDtypeStruct((STORE, D, D), BF16))
    olds = [] if store is None else [store]
    counts = [len(scalars) + len(args), len(fetch), len(needed) + len(olds), len(outs), int(saving)]
    counts += [len(fetch), len(scratch)]

    def kernel(*refs):
        groups, at = [], 0
        for count in counts:
            groups.append(refs[at : at + count])
            at += count
        ins, sources, _, results, target, buffers, spare = groups
        sources = [ref.at[square] for ref, (_, square) in zip(sources, fetch)]
        moves = Moves(sources, buffers, refs[at], target[0] if saving else None, refs[at + 1])
        extra = (moves,) if saving or fetch else ()
        body(*extra, *ins, *results, *spare)
        moves.finish()

    small, anywhere = pl.BlockSpec(memory_space=pltpu.SMEM), pl.BlockSpec(memory_space=pl.ANY)
    near = pl.BlockSpec(memory_space=pltpu.VMEM)
    first = len(scalars) + len(args) + len(fetch) + len(needed)
    return pl.pallas_call(
        kernel,
        out_shape=shapes,
        in_specs=[small] * len(scalars)
        + [near] * len(args)
        + [anywhere] * (len(fetch) + len(needed) + len(olds)),
        out_specs=[near] * len(outs) + [anywhere] * int(saving),
        input_output_aliases={first: len(outs)} if olds else {},
        scratch_shapes=[pltpu.VMEM((D, D), BF16)] * len(fetch)
        + list(scratch)
        + [pltpu.SemaphoreType.DMA((max(1, len(fetch)),)), pltpu.SemaphoreType.DMA((24,))],
        compiler_params=pltpu.CompilerParams(vmem_limit_bytes=LIMIT),
        cost_estimate=pl.CostEstimate(flops=COST, bytes_accessed=COST // 1000, transcendentals=0),
    )(*scalars, *args, *(a for a, _ in fetch), *needed, *olds)


def dot(a, b):
    return jnp.dot(a, b, preferred_element_type=F32)


def dot_tn(a, b):
    return lax.dot_general(a, b, (((0,), (0,)), ((), ())), preferred_element_type=F32)


def dot_nt(a, b):
    return lax.dot_general(a, b, (((1,), (1,)), ((), ())), preferred_element_type=F32)


def head_marks(width):
    rows = lax.broadcasted_iota(jnp.int32, (D, width), 0) // HEAD_DIM
    return (rows == lax.broadcasted_iota(jnp.int32, (D, width), 1)).astype(F32)


def lane_marks(side, value):
    lanes = lax.broadcasted_iota(jnp.int32, (1, PAIR), 1) // HEAD_DIM
    return jnp.where(lanes == side, value, 0.0)


def norm(summed):
    average = jnp.mean(summed, axis=-1, keepdims=True)
    centered = summed - average
    scaling = lax.rsqrt(jnp.mean(centered * centered, axis=-1, keepdims=True) + EPSILON)
    return (centered * scaling, scaling)


def norm_pull(weighted, normed, scaling):
    centered = weighted - jnp.mean(weighted, axis=-1, keepdims=True)
    return scaling * (centered - normed * jnp.mean(weighted * normed, axis=-1, keepdims=True))


def project(low, rows, moves, first, q_ref, k_ref, v_ref, near_ref):
    quarter = near_ref.shape[0]
    keys = dot(low, moves.get(first + 1)[...]).astype(BF16)
    values = dot(low, moves.get(first + 2)[...]).astype(BF16)
    k_ref[rows] = keys
    v_ref[rows] = values
    if rows.start == 0:
        near_ref[:, :D] = keys[:quarter]
        near_ref[:, D:] = values[:quarter]
    q_ref[rows] = dot(low, moves.get(first)[...]).astype(BF16)


def first_kernel(moves, x_ref, q_ref, k_ref, v_ref, near_ref, low_ref):
    low = x_ref[...].astype(BF16)
    low_ref[...] = low
    moves.put(LOW, low_ref)
    rows = slice(0, x_ref.shape[0])
    project(low, rows, moves, 0, q_ref, k_ref, v_ref, near_ref)
    for i, ref in enumerate((q_ref, k_ref, v_ref)):
        moves.put(LOW + 1 + i, ref)


def weigh(marks, array):
    return lax.dot_general(
        marks, array, (((0,), (1,)), ((), ())), preferred_element_type=F32, precision=HIGHEST
    )[:HEADS]


def spread(marks, array):
    return lax.dot_general(
        array.astype(BF16), marks[:, :HEADS].astype(BF16), (((0,), (1,)), ((), ())),
        preferred_element_type=F32,
    )


def forward_kernel(last, base, moves, *refs):
    x_ref, q_ref, k_ref, v_ref, far_ref, own_row_ref, key_col_ref, own_col_ref, vec_ref = refs[:9]
    outs, refs = (refs[9:11], refs[11:]) if last else (refs[9:15], refs[15:])
    stat_ref, outs = outs[0], outs[1:]
    mix_ref, u1_ref, low1_ref, slope_ref, act_ref, u2_ref, low_ref = refs[:7]
    keys_ref, values_ref, bias_ref, own_ref, wide_ref, turned_ref, scale_ref = refs[7:]
    moves.put(base + FAR, far_ref.at[:, :D], slice(0, far_ref.shape[0]))
    moves.put(base + FAR, far_ref.at[:, D:], slice(far_ref.shape[0], x_ref.shape[0]))
    tokens = x_ref.shape[0]
    quarter = far_ref.shape[0]
    far_half = slice(quarter, tokens)
    keys_ref[:quarter] = k_ref[:quarter]
    keys_ref[quarter:] = far_ref[:, :D]
    values_ref[:, :quarter] = v_ref[:quarter].T
    values_ref[:, quarter:] = far_ref[:, D:].T
    bias_ref[...] = jnp.where(key_col_ref[...] == own_row_ref[...], 0.0, NEGATIVE)
    marks = head_marks(PAIR)
    product = q_ref[far_half].astype(F32) * k_ref[far_half].astype(F32) * SCALING
    own_ref[...] = weigh(marks, product)

    def pair_step(pair, carry):
        lanes = pl.ds(pl.multiple_of(pair * PAIR, PAIR), PAIR)
        key_pair = keys_ref[:, lanes]
        q_pair = q_ref[:, lanes]
        for side in range(2):
            head = pl.ds(2 * pair + side, 1)
            scores = dot_nt(key_pair, q_pair * lane_marks(side, SCALING).astype(BF16))
            scores = scores + bias_ref[...]
            top = jnp.max(scores, axis=0, keepdims=True)
            own = own_ref[head, :]
            top = jnp.concatenate([top[:, :quarter], jnp.maximum(top[:, quarter:], own)], axis=1)
            exps = jnp.exp(scores - top)
            own = jnp.exp(own - top[:, quarter:])
            amount = jnp.sum(exps, axis=0, keepdims=True)
            amount = jnp.concatenate([amount[:, :quarter], amount[:, quarter:] + own], axis=1)
            inverse = 1.0 / amount
            own_ref[head, :] = own * inverse[:, quarter:]
            stat_ref[head, :] = top + jnp.log(amount)
            prob = (exps * inverse).astype(BF16)
            part = pl.ds(pl.multiple_of(pair * PAIR + side * HEAD_DIM, HEAD_DIM), HEAD_DIM)
            turned_ref[part, :] = dot(values_ref[part, :], prob)
        return carry

    lax.fori_loop(0, D // PAIR, pair_step, 0)
    wide_ref[...] = turned_ref[...].T
    own_share = spread(marks, own_ref[...]) * v_ref[far_half].astype(F32)
    mix_ref[:quarter] = wide_ref[:quarter].astype(BF16)
    mix_ref[far_half] = (wide_ref[far_half] + own_share).astype(BF16)
    moves.put(base + MIX, mix_ref)
    sums = [jnp.zeros((1, D), F32) for _ in range(CELLS_ROW)]
    for start in range(0, tokens, quarter):
        rows = slice(start, start + quarter)
        normed, scaling = norm(x_ref[rows] + dot(mix_ref[rows], moves.get(0)[...]))
        u1_ref[rows] = normed.astype(BF16)
        scale_ref[rows, 0:1] = scaling
        first = normed * vec_ref[0:1] + vec_ref[1:2]
        first_low = first.astype(BF16)
        low1_ref[rows] = first_low
        hidden = dot(first_low, moves.get(1)[...]) + vec_ref[4:5]
        share = 0.5 + 0.5 * lax.erf(hidden * math.sqrt(0.5))
        active = (hidden * share).astype(BF16)
        act_ref[rows] = active
        density = jnp.exp(-0.5 * hidden * hidden) * (1.0 / math.sqrt(2.0 * math.pi))
        slope_ref[rows] = (share + hidden * density).astype(BF16)
        normed, scaling = norm(first + dot(active, moves.get(2)[...]) + vec_ref[5:6])
        u2_ref[rows] = normed.astype(BF16)
        scale_ref[rows, 1:2] = scaling
        state = normed * vec_ref[2:3] + vec_ref[3:4]
        for i, ref in enumerate((u1_ref, low1_ref, slope_ref, act_ref, u2_ref)):
            moves.put(base + U1 + i, ref.at[rows], rows)
        if last:
            for cell in range(CELLS_ROW):
                part = jnp.where(own_col_ref[rows] == cell, state, 0.0)
                sums[cell] = sums[cell] + jnp.sum(part, axis=0, keepdims=True)
        else:
            outs[0][rows] = state
            low = state.astype(BF16)
            low_ref[rows] = low
            project(low, rows, moves, 3, *outs[1:])
    stat_ref[HEADS:] = scale_ref[...].T[:HEADS]
    if last:
        outs[0][...] = jnp.concatenate(sums)
    else:
        for i, ref in enumerate((low_ref, *outs[1:4])):
            moves.put(base + NEXT + i, ref)


def head_kernel(rows_dev, scale, own_rows, pooled_ref, table_ref, target_ref, loss_ref, low_ref, grad_ref):
    table = table_ref[...]
    errors = dot_nt(pooled_ref[...], table) - (target_ref[...] * (4.0 / (BINS - 1)) - 2.0)
    spot = lax.broadcasted_iota(jnp.int32, errors.shape, 1) % SLOT
    errors = jnp.where(spot < rows_dev, errors, 0.0)
    mine = errors[:, :own_rows]
    loss_ref[...] = jnp.broadcast_to(jnp.sum(mine * mine), loss_ref.shape)
    low = (errors * scale).astype(BF16)
    low_ref[...] = low
    grad_ref[...] = dot(low, table)


def backward_kernel(
    seeded, moves,
    grad_ref, own_col_ref, stat_ref, own_row_ref, key_col_ref, vec_ref,
    sum1_ref, low2_ref, hid_ref, low1_ref, gq_ref, gk_ref, gv_ref, send_ref, gvec_ref,
    keys_ref, values_ref, bias_ref, gmix_ref, own_p_ref, own_s_ref, turned_ref, wide_ref, scale_ref,
):
    bias_ref[...] = jnp.where(key_col_ref[...] == own_row_ref[...], 0.0, NEGATIVE)
    scale_ref[...] = stat_ref[HEADS:].T
    u2_ref, w2_ref, slope_ref, w1_ref = (moves.get(i) for i in range(4))
    q_ref = moves.buffers[6]
    lse_ref = stat_ref
    tokens = q_ref.shape[0]
    quarter = tokens // 2
    sums = [jnp.zeros((1, D), F32) for _ in range(6)]

    def gather(index, value):
        sums[index] = sums[index] + jnp.sum(value, axis=0, keepdims=True)

    for start in range(0, tokens, quarter):
        rows = slice(start, start + quarter)
        if seeded:
            upstream = jnp.zeros((quarter, D), F32)
            for cell in range(CELLS_ROW):
                upstream = jnp.where(own_col_ref[rows] == cell, grad_ref[cell : cell + 1], upstream)
        else:
            upstream = grad_ref[rows]
        normed = u2_ref[rows].astype(F32)
        gather(2, upstream * normed)
        gather(3, upstream)
        sum_two = norm_pull(upstream * vec_ref[2:3], normed, scale_ref[rows, 1:2])
        low_two = sum_two.astype(BF16)
        low2_ref[rows] = low_two
        gather(5, low_two.astype(F32))
        hid = (dot_nt(low_two, w2_ref[...]) * slope_ref[rows].astype(F32)).astype(BF16)
        hid_ref[rows] = hid
        gather(4, hid.astype(F32))
        upstream = sum_two + dot_nt(hid, w1_ref[...])
        normed = moves.get(4)[rows].astype(F32)
        gather(0, upstream * normed)
        gather(1, upstream)
        sum_one = norm_pull(upstream * vec_ref[0:1], normed, scale_ref[rows, 0:1])
        sum1_ref[rows] = sum_one
        low_one = sum_one.astype(BF16)
        low1_ref[rows] = low_one
        gmix_ref[rows] = dot_nt(low_one, moves.get(5)[...]).astype(BF16)
    gvec_ref[...] = jnp.concatenate(sums + [jnp.zeros((2, D), F32)])

    q_ref, k_ref, v_ref, far_ref = (moves.get(i) for i in range(6, 10))
    keys_ref[:quarter] = k_ref[:quarter]
    keys_ref[quarter:] = far_ref[:quarter]
    values_ref[:quarter] = v_ref[:quarter]
    values_ref[quarter:] = far_ref[quarter:]
    turned_ref[...] = keys_ref[...].T
    marks = head_marks(PAIR)
    far_half = slice(quarter, tokens)
    queries = q_ref[far_half].astype(F32)
    mixed = gmix_ref[far_half].astype(F32)
    product = queries * k_ref[far_half].astype(F32) * SCALING
    own_prob = jnp.exp(weigh(marks, product) - lse_ref[:HEADS, far_half])
    own_grad = weigh(marks, mixed * v_ref[far_half].astype(F32))
    own_p_ref[...] = own_prob
    own_s_ref[...] = own_grad

    def pair_step(pair, carry):
        lanes = pl.ds(pl.multiple_of(pair * PAIR, PAIR), PAIR)
        key_pair = keys_ref[:, lanes]
        value_pair = values_ref[:, lanes]
        q_pair = q_ref[:, lanes]
        mix_pair = gmix_ref[:, lanes]
        grad_k = jnp.zeros((tokens, PAIR), F32)
        grad_v = jnp.zeros((tokens, PAIR), F32)
        for side in range(2):
            head = 2 * pair + side
            scaled = q_pair * lane_marks(side, SCALING).astype(BF16)
            mix_side = mix_pair * lane_marks(side, 1.0).astype(BF16)
            lse = lse_ref[pl.ds(head, 1), :]
            prob = jnp.exp(dot_nt(key_pair, scaled) + bias_ref[...] - lse)
            grad_p = dot_nt(value_pair, mix_side)
            delta = jnp.sum(prob * grad_p, axis=0, keepdims=True)
            own_p = own_p_ref[pl.ds(head, 1), :]
            own_g = own_s_ref[pl.ds(head, 1), :]
            delta = jnp.concatenate([delta[:, :quarter], delta[:, quarter:] + own_p * own_g], axis=1)
            own_s_ref[pl.ds(head, 1), :] = own_p * (own_g - delta[:, quarter:])
            grad_s = (prob * (grad_p - delta)).astype(BF16)
            grad_k = grad_k + dot(grad_s, scaled)
            grad_v = grad_v + dot(prob.astype(BF16), mix_side)
            part = pl.ds(pl.multiple_of(pair * PAIR + side * HEAD_DIM, HEAD_DIM), HEAD_DIM)
            wide_ref[part, :] = dot(turned_ref[part, :], grad_s)
        gk_ref[:, lanes] = grad_k
        gv_ref[:, lanes] = grad_v
        return carry

    lax.fori_loop(0, D // PAIR, pair_step, 0)
    send_ref[:, :D] = gk_ref[quarter:].astype(BF16)
    send_ref[:, D:] = gv_ref[quarter:].astype(BF16)
    own_score = spread(marks, own_s_ref[...]) * SCALING
    gv_ref[far_half] = spread(marks, own_p_ref[...]) * mixed
    gk_ref[far_half] = own_score * queries
    grad_q = wide_ref[...].T * SCALING
    gq_ref[:quarter] = grad_q[:quarter].astype(BF16)
    gq_ref[far_half] = (grad_q[far_half] + own_score * k_ref[far_half].astype(F32)).astype(BF16)


def weights_kernel(moves, gq_ref, g1_ref, gz_ref, g2_ref, out_ref):
    for i, ref in enumerate((gq_ref, g1_ref, gz_ref, g2_ref)):
        out_ref[i] = dot_tn(moves.get(i)[...], ref[...]).astype(BF16)


def inputs_kernel(
    moves, sum1_ref, gq_ref, gk_ref, gv_ref, got_ref, grad_ref, out_ref, low_k_ref, low_v_ref
):
    quarter = got_ref.shape[0]
    low_k_ref[:quarter] = (gk_ref[:quarter] + got_ref[:, :D].astype(F32)).astype(BF16)
    low_v_ref[:quarter] = (gv_ref[:quarter] + got_ref[:, D:].astype(F32)).astype(BF16)
    low_k_ref[quarter:] = gk_ref[quarter:].astype(BF16)
    low_v_ref[quarter:] = gv_ref[quarter:].astype(BF16)
    grad_ref[...] = (
        sum1_ref[...]
        + dot_nt(gq_ref[...], moves.get(0)[...])
        + dot_nt(low_k_ref[...], moves.get(1)[...])
        + dot_nt(low_v_ref[...], moves.get(2)[...])
    )
    low = moves.get(3)[...]
    out_ref[0] = dot_tn(low, low_k_ref[...]).astype(BF16)
    out_ref[1] = dot_tn(low, low_v_ref[...]).astype(BF16)


def join_kernel(base, moves, c_ref, own_ref, got_ref, *outs):
    count, _, _, rows, _ = own_ref.shape
    mine = c_ref[0] == 0
    for i, (plane, x, c, y) in enumerate(itertools.product(range(count), (0, 1), (0, 1), (0, 1))):
        at, end = rows * i, rows * (i + 1)
        while at < end:
            place, stop = at // D, min(end, (at // D + 1) * D)
            piece = slice(at - rows * i, stop - rows * i)
            own, got = own_ref[plane, x, y, piece], got_ref[plane, x, y, piece]
            chosen = jnp.where(mine, own, got) if c == 0 else jnp.where(mine, got, own)
            outs[place][at - place * D : stop - place * D] = chosen
            at = stop
            if at == place * D + D:
                moves.put(base + place, outs[place])


def split_kernel(plan, c_ref, *refs):
    ins, (near_ref, far_ref) = refs[:-2], refs[-2:]
    count, _, _, rows, _ = near_ref.shape
    mine = c_ref[0] == 0
    at = 0
    for place, index, low, size in plan:
        done = 0
        while done < size:
            i = at // rows
            step = min(size - done, rows * (i + 1) - at)
            plane, x, c, y = i // 8, i // 4 % 2, i // 2 % 2, i % 2
            piece = slice(at - rows * i, at - rows * i + step)
            value = ins[place][index, low + done : low + done + step]
            stays = mine if c == 0 else jnp.logical_not(mine)

            @pl.when(stays)
            def _():
                near_ref[plane, x, y, piece] = value

            @pl.when(jnp.logical_not(stays))
            def _():
                far_ref[plane, x, y, piece] = value

            at, done = at + step, done + step


def shapes_of(tokens):
    return (((tokens, D), F32), ((tokens, D), BF16), ((tokens // 2, 2 * D), BF16))


def vmem(*shape_types):
    return [pltpu.VMEM(*s) for s in shape_types]


SQUARES = 16
LOW, NEXT, FAR, MIX, U1 = 0, 16, 4, 5, 6


def begin(state, mats):
    wide, slim, half = shapes_of(state.shape[0])
    fetch = [(mats, i) for i in range(3)]
    return call(first_kernel, [slim, slim, slim, half], (state,), vmem(slim), fetch=fetch, fresh=True)


def layer_forward(state, queries, keys, values, far, places, vecs, mats, store, layer):
    tokens = state.shape[0]
    wide, slim, half = shapes_of(tokens)
    last = layer == LAYERS - 1
    square = ((tokens, tokens), F32)
    own, turned = ((HEADS, tokens // 2), F32), ((D, tokens), F32)
    outs = [((2 * HEADS, tokens), F32)]
    outs += [((CELLS_ROW, D), F32)] if last else [wide, slim, slim, slim, half]
    own_col, own_row, key_col = places
    return call(
        partial(forward_kernel, last, SQUARES * layer),
        outs,
        (state, queries, keys, values, far, own_row, key_col, own_col, vecs),
        vmem(*[slim] * 7, slim, ((D, tokens), BF16), square, own, wide, turned, ((tokens, PAIR), F32)),
        fetch=[(mats, 6 * layer + i) for i in range(3, 6 if last else 9)],
        store=store,
    )


def layer_backward(gradient, stat, store, places, vecs, mats, layer, needed, more):
    tokens = stat.shape[1]
    wide, slim, half = shapes_of(tokens)
    own_col, own_row, key_col = places
    own, square = ((HEADS, tokens // 2), F32), ((tokens, tokens), F32)
    at, mat = SQUARES * layer, 6 * layer
    saved = lambda *squares: [(store, at + i) for i in squares]
    sum1, g2, gz, g1, gq, gk, gv, send, gvec = call(
        partial(backward_kernel, gradient.shape[0] == CELLS_ROW),
        [wide, slim, slim, slim, slim, wide, wide, half, ((8, D), F32)],
        (gradient, own_col, stat, own_row, key_col, vecs),
        vmem(
            slim, slim, square, slim, own, own, ((D, tokens), BF16), ((D, tokens), F32),
            ((tokens, HEADS), F32),
        ),
        needed,
        fetch=[
            *saved(U1 + 4), (mats, mat + 5), *saved(U1 + 2), (mats, mat + 4), *saved(U1),
            (mats, mat + 3), *saved(LOW + 1, LOW + 2, LOW + 3, FAR),
        ],
    )
    (part_one,) = call(
        weights_kernel,
        [((4, D, D), BF16)],
        (gq, g1, gz, g2),
        fetch=saved(LOW, MIX, U1 + 1, U1 + 3),
    )
    grad, part_two = call(
        inputs_kernel,
        [wide, ((2, D, D), BF16)],
        (sum1, gq, gk, gv, flip(send, "c")),
        vmem(slim, slim),
        more(part_one),
        fetch=[*((mats, mat + i) for i in range(3)), *saved(LOW)],
    )
    parts = [(part_one, 0), (part_two, 0), (part_two, 1), (part_one, 1), (part_one, 2), (part_one, 3)]
    return (grad, parts, gvec[:6])


def split_rows(parts, low, high, count, rows, c):
    arrays, plan = [], []
    for i in range(low // D, -(-high // D)):
        array, index = parts[i]
        known = [j for j, a in enumerate(arrays) if a is array]
        if not known:
            arrays.append(array)
            known = [len(arrays) - 1]
        start, stop = max(low, i * D), min(high, i * D + D)
        plan.append((known[0], index, start - i * D, stop - start))
    half = ((count, 2, 2, rows, D), BF16)
    return call(partial(split_kernel, plan), [half, half], arrays, scalars=(c[None],))


def local(
    gene_ids, expr_bins, gene_order, cell_ids, target_bins,
    matrices, vectors, value_table, gene_table,
    matrices_mom, vectors_mom, value_mom, gene_mom,
    matrices_avg, vectors_avg, value_avg, gene_avg,
):
    planes = lax.axis_size("z")
    short = short_z(planes)
    z, x, c, y = (lax.axis_index(a) for a in ("z", "x", "c", "y"))
    half = cell_ids.shape[2]
    quarter = half // 2
    rows_dev = gene_table.shape[0]
    vocab = rows_dev * planes * 8
    mat_rows = matrices.shape[0]
    plane_cells = 4 * CELLS_ROW

    mats_low = matrices.astype(BF16)
    if short:
        mats_all = [mats_low] + [z_swap(mats_low, k, planes) for k in range(1, planes)]

    codes = gene_ids[0] * 64 + expr_bins[0]
    mine = jnp.stack([codes, gene_order[0], cell_ids[0].reshape(-1)])
    mine = jnp.where(c == y, mine, flip(mine, "c"))
    codes, order, cells = mine[0], mine[1], mine[2]

    def own_part(array):
        return jnp.concatenate(
            [
                lax.dynamic_slice_in_dim(array, c * quarter, quarter),
                lax.dynamic_slice_in_dim(array, half + c * quarter, quarter),
            ]
        )

    picks = own_part(order)
    own_cells = own_part(cells)
    far_known = lax.dynamic_slice_in_dim(cells, (1 - c) * quarter, quarter)
    key_cells = jnp.concatenate([own_cells[:quarter], far_known])
    tokens = picks.shape[0]
    place = jnp.arange(codes.shape[0])
    code = jnp.sum(jnp.where(picks[:, None] == place[None, :], codes[None, :], 0), axis=1)
    genes, levels = code >> 6, code & 63
    places = (own_cells[:, None], own_cells[None, :], key_cells[:, None])
    numbers = jnp.arange(CELLS_ROW)
    counts = jnp.sum((cells[None, :] == numbers[:, None]).astype(F32), axis=1)

    plane_genes = xy_gather(genes, 0)[0].reshape(-1)

    table_low = gene_table.astype(BF16)
    targets = target_bins.astype(BF16).reshape(planes, plane_cells, rows_dev)
    targets = jnp.pad(targets, ((0, 0), (0, 0), (0, D - rows_dev)))
    if short:
        load = lambda k: jnp.concatenate(
            [table_low, lax.dynamic_index_in_dim(targets, z ^ k, 0, False)]
        )
        got = [load(0)] + [z_swap(load(k), k, planes) for k in range(1, planes)]
        slots = jnp.stack(got)
    else:
        rows = lax.all_gather(table_low, "z")
        slots = jnp.concatenate([rows, lax.all_to_all(targets, "z", 0, 0)], axis=1)
        got = [slots]
    table_col = jnp.stack([slots, flip(slots, "c")])
    target_col = table_col[:, :, rows_dev:, :SLOT].transpose(2, 0, 1, 3)
    table_col = table_col.reshape(-1, D)
    col_rows = table_col.shape[0]
    own_rows = col_rows // 2
    target_col = target_col.reshape(plane_cells, col_rows).astype(F32)

    owner, inner = plane_genes // rows_dev, plane_genes % rows_dev
    here = ((owner >> 2) & 1) * 2 + (owner & 1) == x * 2 + y
    slot = ((owner >> 1) & 1 ^ c) * planes + slot_of(owner >> 3, z, planes)
    index = jnp.where(here, slot * SLOT + inner, -1)
    hot = (index[:, None] == jnp.arange(col_rows)[None, :]).astype(BF16)
    found = dot(hot, table_col).astype(BF16).reshape(2, 2, tokens, D)
    embedded, early = xy_reduce(found, 0)
    level_hot = (levels[:, None] == jnp.arange(BINS)[None, :]).astype(F32)
    state = math.sqrt(D) * embedded.astype(F32) + jnp.dot(level_hot, value_table, precision=HIGHEST)

    if short:
        mats_all = jnp.stack(mats_all)
        gathers = []
        for group in range(2):
            part = [
                lax.dynamic_index_in_dim(mats_all, z ^ p, 0, False)
                for p in range(group * planes // 2, (group + 1) * planes // 2)
            ]
            gathers.append(PlaneGather(jnp.stack(part), x, y, c))
        gathers[0].one()
        gathers[0].two()
        gathers[1].one()
        mats = gathers[0].three(0, None)
    else:
        whole = lax.all_gather(mats_low, ("z", "x", "c", "y"), tiled=True).reshape(-1, D, D)
        mats = jnp.concatenate([whole, jnp.zeros((STORE - whole.shape[0], D, D), BF16)])

    queries, keys, values, near, store = begin(state, mats)
    stats = []
    for layer in range(LAYERS):
        far = flip(near, "c")
        if short and layer == 0:
            gathers[1].two()
        if short and layer == 1:
            mats = gathers[1].three(3 * LAYERS, mats)
        stat, *rest, store = layer_forward(
            state, queries, keys, values, far, places, vectors[layer], mats, store, layer
        )
        stats.append(stat)
        if layer < LAYERS - 1:
            state, queries, keys, values, near = rest

    pooled = (rest[0] + flip(rest[0], "c")) / counts[:, None]
    pooled = ordered(pooled, flip(pooled, "y"), y)
    pooled = ordered(pooled, flip(pooled, "x"), x)
    pooled_low = pooled.reshape(plane_cells, D).astype(BF16)
    loss_part, grad_pred, grad_pooled = call(
        partial(head_kernel, rows_dev, 2.0 / vocab, own_rows),
        [((8, 128), F32), ((plane_cells, col_rows), BF16), ((plane_cells, D), F32)],
        (pooled_low, table_col, target_col),
    )
    loss_part = loss_part[0, 0]
    grad_pooled = grad_pooled.reshape(2, 2, CELLS_ROW, D)
    grad_pooled = pick(grad_pooled, x) + flip(pick(grad_pooled, 1 - x), "x")
    grad_pooled = pick(grad_pooled, y) + flip(pick(grad_pooled, 1 - y), "y")
    gradient = grad_pooled / counts[:, None]

    parts = [None] * (6 * LAYERS)
    late = late_blocks = None
    vec_grads = [None] * LAYERS

    def gradients_of(low, high):
        rows = (8 * mat_rows * low, 8 * mat_rows * high)
        return PlaneReduce(*split_rows(parts, *rows, high - low, mat_rows, c), x, y)

    for layer in reversed(range(LAYERS)):
        span = slice(6 * layer, 6 * layer + 6)
        needed, more = (), lambda part: ()
        if short and layer == 1:

            def more(part):
                nonlocal late
                parts[9:12] = [(part, 1), (part, 2), (part, 3)]
                late = gradients_of(planes // 2, planes)
                return ()

        if short and layer == 0:
            late.one()
            needed = late.block
            more = lambda part: late.halves

        gradient, parts[span], vec_grads[layer] = layer_backward(
            gradient, stats[layer], store, places, vectors[layer], mats, layer, needed, more
        )

    grad_value = jnp.einsum("tb,td->bd", level_hot, gradient, precision=HIGHEST)
    grad_embedded = (math.sqrt(D) * gradient).astype(BF16)
    grad_plane, early = xy_gather(grad_embedded, 0)
    rest = gradients_of(0, planes // 2 if short else planes)
    rest.one()
    grad_col = dot_tn(hot, grad_plane.reshape(-1, D))
    grad_own = grad_col[:own_rows] + flip(grad_col[own_rows:].astype(BF16), "c").astype(F32)
    grad_own = grad_own + dot_tn(grad_pred[:, :own_rows], pooled_low)
    grad_own = grad_own.astype(BF16).reshape(planes, SLOT, D)[:, :rows_dev]
    if short:
        swaps = [z_swap(grad_own[k], k, planes) for k in range(1, planes)]
        grad_table = sum(term.astype(F32) for term in [grad_own[0], *swaps])
        blocks = jnp.concatenate([rest.two(grad_own), late.two(grad_own)])
        blocks = [lax.dynamic_index_in_dim(blocks, z ^ k, 0, False) for k in range(planes)]
        terms = [blocks[0]] + [z_swap(blocks[k], k, planes) for k in range(1, planes)]
        grad_matrices = sum(term.astype(F32) for term in terms)
    else:
        swaps = ()
        grad_table = jnp.sum(lax.all_to_all(grad_own, "z", 0, 0).astype(F32), axis=0)
        grad_matrices = owner_sum(rest.two(), 0, z, planes)

    small = jnp.concatenate([jnp.concatenate(vec_grads), grad_value])
    small = all_sum(small, planes)
    grad_vectors = small[: 6 * LAYERS].reshape(vectors.shape)
    grad_value = small[6 * LAYERS :]
    squares = jnp.sum(grad_matrices * grad_matrices) + jnp.sum(grad_table * grad_table)
    lanes = jnp.arange(128)[None, :]
    sums = jnp.where(lanes == 0, squares, jnp.where(lanes == 1, loss_part, 0.0))
    sums = small_sum(jnp.broadcast_to(sums, (8, 128)), x, y, z, planes)
    loss_sum = sums[0, 1]
    grad_norm = jnp.sqrt(sums[0, 0] + jnp.sum(small * small))
    factor = CLIP_NORM / grad_norm

    def update(weight, moment, average, grad_full):
        clipped = factor * grad_full
        moment_new = MOMENTUM * moment + clipped
        weight_new = weight - LEARN_RATE * (clipped + MOMENTUM * moment_new)
        return (
            moment_new,
            weight_new,
            AVERAGE_DECAY * average + (1.0 - AVERAGE_DECAY) * weight_new,
        )

    return (
        loss_sum,
        grad_norm,
        *update(matrices, matrices_mom, matrices_avg, grad_matrices),
        *update(vectors, vectors_mom, vectors_avg, grad_vectors),
        *update(value_table, value_mom, value_avg, grad_value),
        *update(gene_table, gene_mom, gene_avg, grad_table),
    )


def solution(mesh):
    devices = mesh.devices
    fine = Mesh(devices.reshape(devices.shape[0] // 4, 2, 2, devices.shape[1]), ("z", "x", "c", "y"))
    dp = ("z", "x", "c")
    every = ("z", "x", "c", "y")
    weights = (P(every, None), P(), P(), P(every, None))
    in_specs = (P(dp, None),) * 3 + (P(dp, None, None), P(None, every)) + weights * 3
    out_specs = (P(), P()) + (P(every, None),) * 3 + (P(),) * 6 + (P(every, None),) * 3
    return jax.shard_map(local, mesh=fine, in_specs=in_specs, out_specs=out_specs, check_vma=False)
```

time: 413 us -> 398 us (0.964)
  Pallas kernels: 72.3 us -> 112 us
  local copies, waits for them, and re-layouts: 40.8 us -> 8.95 us
  starting transfers between devices: 96.3 us -> 72.7 us
  waiting for transfers between devices: 131 us -> 141 us
  matrix products: 18.4 us -> 11.7 us
    pallas_call x15 -> x20, Pallas kernels: 72.3 us -> 112 us  [the longest x18 112 us: call(): pl.pallas_call(kernel, out_shape=shapes, in_specs=[small] * len(scalars)...]
    unnamed x269 -> x67, local copies, waits for them, and re-layouts: 27.5 us -> 3.05 us
    ppermute x19 -> x20, waiting for transfers between devices: 34.3 us -> 53.2 us  [the longest x17 50.1 us: z_swap(): return lax.ppermute(block, 'z', pairs)]
    ppermute x19 -> x20, starting transfers between devices: 39.7 us -> 26.5 us  [the longest x17 23 us: z_swap(): return lax.ppermute(block, 'z', pairs)]
    ppermute x53 -> x50, starting transfers between devices: 56.6 us -> 46.2 us  [flip(): return lax.ppermute(block, axis, [(0, 1), (1, 0)])]
    ppermute x53 -> x50, waiting for transfers between devices: 96.7 us -> 87.4 us  [flip(): return lax.ppermute(block, axis, [(0, 1), (1, 0)])]
    another operation x5 -> x16, other arithmetic: 7.17 us -> 0.9 us  [ordered(): return jnp.stack([low, high], axis=axis)]
    convert_element_type x10 -> x12, other arithmetic: 3.37 us -> 8.68 us  [the longest x11 7.89 us: rounded_sum(): return (a.astype(F32) + b.astype(F32)).astype(a.dtype)]
  transfers between devices with their start and end apart: 72 -> 70, of which waited for: 35 -> 34; matrix products, arithmetic and copies ran while one was open for 14% -> 13% of each run, Pallas kernels for 2% -> 13%
where the time goes in v3:
time: 398 us; the launch traced here: 394 us
  waiting for transfers between devices  141 us (35%)
  Pallas kernels  112 us (28%)
  starting transfers between devices  72.7 us (18%)
  other arithmetic  42.1 us (11%)
  matrix products  11.7 us (3%)
  local copies, waits for them, and re-layouts  8.95 us (2%)
  between operations  5.91 us (1%)
    pallas_call x18, Pallas kernels, call(): pl.pallas_call(kernel, out_shape=shapes, in_specs=[small] * len(scalars)...  112 us
    ppermute x50, waiting for transfers between devices, flip(): return lax.ppermute(block, axis, [(0, 1), (1, 0)])  87.4 us
    ppermute x17, waiting for transfers between devices, z_swap(): return lax.ppermute(block, 'z', pairs)  50.1 us
    ppermute x50, starting transfers between devices, flip(): return lax.ppermute(block, axis, [(0, 1), (1, 0)])  46.2 us
    ppermute x17, starting transfers between devices, z_swap(): return lax.ppermute(block, 'z', pairs)  23 us
  transfers between devices with their start and end apart: 70, of which 34 were waited for; matrix products, arithmetic and copies ran while one was open for 13% of the time, Pallas kernels for 13%

profile of v3, /device:TPU:0, one launch (start us, length us, event | category | flops | bytes accessed | tf_op | source)
XLA Modules:
  0.0 394.1 jit_solution(10352251530405457884)
XLA Ops:
  1.8 5.1 %collective-permute-start.15 = (bf16[288,512]{1,0:T(8,128)(2,1)S(1)}, bf16[288,512]{1,0:T(8,128)(2,1)S(1)}, u32[]{:S(2)}, u32[]{:S(2)}) collective-permute-start(bf16[288,512]{1,0:T(8,128)(2,1)S(1)} %convert_element_type.254), channel_id=1, source_target_pairs={{24,0},{16,8},{8,16},{0,24},{25,1},{17,9},{9,17},{1,25},{26,2},{18... | collective-permute-start | bytes 884744 | tf_op jit(solution)/shard_map/ppermute | solution.py:75
  28.1 16.2 %collective-permute-done.14 = bf16[288,512]{1,0:T(8,128)(2,1)S(1)} collective-permute-done((bf16[288,512]{1,0:T(8,128)(2,1)S(1)}, bf16[288,512]{1,0:T(8,128)(2,1)S(1)}, u32[]{:S(2)}, u32[]{:S(2)}) %collective-permute-start.14) | collective-permute-done | bytes 294944 | tf_op jit(solution)/shard_map/ppermute | solution.py:75
  46.2 8.3 %collective-permute-done.6 = bf16[256,512]{1,0:T(8,128)(2,1)S(1)} collective-permute-done((bf16[256,512]{1,0:T(8,128)(2,1)S(1)}, bf16[256,512]{1,0:T(8,128)(2,1)S(1)}, u32[]{:S(2)}, u32[]{:S(2)}) %collective-permute-start.6) | collective-permute-done | bytes 262176 | tf_op jit(solution)/shard_map/ppermute | solution.py:75
  60.2 4.5 %collective-permute-done.16 = bf16[2,144,512]{2,1,0:T(8,128)(2,1)S(1)} collective-permute-done((bf16[2,144,512]{2,1,0:T(8,128)(2,1)S(1)}, bf16[2,144,512]{2,1,0:T(8,128)(2,1)S(1)}, u32[]{:S(2)}, u32[]{:S(2)}) %collective-permute-start.16) | collective-permute-done | bytes 294944 | tf_op jit(solution)/shard_map/ppermute | solution.py:34
  72.7 10.9 %collective-permute-done.19 = bf16[2,2,144,512]{3,2,0,1:T(8,128)(2,1)S(1)} collective-permute-done((bf16[2,2,144,512]{3,2,0,1:T(8,128)(2,1)S(1)}, bf16[2,2,144,512]{3,2,0,1:T(8,128)(2,1)S(1)}, u32[]{:S(2)}, u32[]{:S(2)}) %collective-permute-start.19) | collective-permute-done | bytes 589856 | tf_op jit(solution)/shard_map/ppermute | solution.py:34
  85.6 4.8 %fusion.4 = bf16[2048,512]{1,0:T(8,128)(2,1)S(1)} fusion(bf16[2048,512]{1,0:T(8,128)(2,1)S(1)} %bitcast.288, s32[2048]{0:T(1024)S(1)} %fusion.43), kind=kOutput, calls=%fused_computation.7 | convolution fusion | flops 4300210176 | bytes 4202496 | tf_op jit(solution)/shard_map/dot_general | solution.py:270
  98.2 8.9 %collective-permute-done.9 = bf16[2,256,512]{2,1,0:T(8,128)(2,1)S(1)} collective-permute-done((bf16[2,256,512]{2,1,0:T(8,128)(2,1)S(1)}, bf16[2,256,512]{2,1,0:T(8,128)(2,1)S(1)}, u32[]{:S(2)}, u32[]{:S(2)}) %collective-permute-start.9) | collective-permute-done | bytes 524320 | tf_op jit(solution)/shard_map/ppermute | solution.py:34
  110.8 4.5 %collective-permute-done.12 = bf16[256,512]{1,0:T(8,128)(2,1)S(1)} collective-permute-done((bf16[256,512]{1,0:T(8,128)(2,1)S(1)}, bf16[256,512]{1,0:T(8,128)(2,1)S(1)}, u32[]{:S(2)}, u32[]{:S(2)}) %collective-permute-start.12) | collective-permute-done | bytes 262176 | tf_op jit(solution)/shard_map/ppermute | solution.py:34
  120.2 5.0 %shard_map.273 = (bf16[512,512]{1,0:T(8,128)(2,1)S(1)}, bf16[512,512]{1,0:T(8,128)(2,1)S(1)}, bf16[512,512]{1,0:T(8,128)(2,1)S(1)}, bf16[256,1024]{1,0:T(8,128)(2,1)}, bf16[132,512,512]{2,1,0:T(8,128)(2,1)}) custom-call(f32[512,512]{1,0:T(8,128)S(1)} %convolution_add_fusion.refs_0_, ...), custom_call_target="tpu_custom_call" | custom-call | flops 1000000000 | bytes 1000000 | tf_op jit(solution)/shard_map/pallas_call | solution.py:253
  127.5 13.5 %shard_map.274 = (f32[16,512]{1,0:T(8,128)S(1)}, f32[512,512]{1,0:T(8,128)S(1)}, bf16[512,512]{1,0:T(8,128)(2,1)S(1)}, bf16[512,512]{1,0:T(8,128)(2,1)S(1)}, bf1...) custom-call(f32[512,512]{1,0:T(8,128)S(1)} %convolution_add_fusion.r, ...), custom_call_target="tpu_custom_call", output_to_operand_aliasing={{6}: (15, {})} | custom-call | flops 1000000000 | bytes 1000000 | tf_op jit(solution)/shard_map/pallas_call | solution.py:253
  141.2 4.9 %shard_map.275.refs_9_.refs_10_.refs_11_.refs_12_.refs_13_.refs_14_.refs_7_.refs_5_.refs_6_ = bf16[132,512,512]{2,1,0:T(8,128)(2,1)} custom-call(s32[1]{0:T(128)} %bitcast.refs_0_, bf16[2,2,2,288,512]{4,3,2,1,0:T(8,128)(2,1)} %maximum_maximum_fusion.1.refs_1_, ...), custom_call_target="tpu_custom_call", output_to_operand_aliasing={{}: (3, {})} | custom-call | flops 1000000000 | bytes 1000000 | tf_op jit(solution)/shard_map/pallas_call | solution.py:253
  146.1 11.9 %shard_map.276 = (f32[16,512]{1,0:T(8,128)S(1)}, f32[512,512]{1,0:T(8,128)S(1)}, bf16[512,512]{1,0:T(8,128)(2,1)S(1)}, bf16[512,512]{1,0:T(8,128)(2,1)S(1)}, bf1...) custom-call(f32[512,512]{1,0:T(8,128)S(1)} %get-tuple-element.85.ref, ...), custom_call_target="tpu_custom_call", output_to_operand_aliasing={{6}: (15, {})} | custom-call | flops 1000000000 | bytes 1000000 | tf_op jit(solution)/shard_map/pallas_call | solution.py:253
  160.0 10.2 %shard_map.277 = (f32[16,512]{1,0:T(8,128)S(1)}, f32[4,512]{1,0:T(4,128)S(1)}, bf16[132,512,512]{2,1,0:T(8,128)(2,1)}) custom-call(f32[512,512]{1,0:T(8,128)S(1)} %get-tuple-element.91.refs_0_, bf16[512,512]{1,0:T(8,128)(2,1)S(1)} %get-tuple-element.92.refs_1_, bf16[512,512]{1,0:T(8,128)(2,1)S(1)} %get-tuple-element.93.refs_2_, ...), custom_call_target="tpu_custom_call", output_to_operand_aliasing={{2}: (12, {})} | custom-call | flops 1000000000 | bytes 1000000 | tf_op jit(solution)/shard_map/pallas_call | solution.py:253
  187.7 14.2 %shard_map.279 = (f32[512,512]{1,0:T(8,128)S(1)}, bf16[512,512]{1,0:T(8,128)(2,1)S(1)}, bf16[512,512]{1,0:T(8,128)(2,1)S(1)}, bf16[512,512]{1,0:T(8,128)(2,1)S(1...) custom-call(f32[4,512]{1,0:T(4,128)S(1)} %fusion.46.refs_0_, ...), custom_call_target="tpu_custom_call" | custom-call | flops 1000000000 | bytes 1000000 | tf_op jit(solution)/shard_map/pallas_call | solution.py:253
  208.4 13.5 %shard_map.281 = (f32[512,512]{1,0:T(8,128)S(1)}, bf16[512,512]{1,0:T(8,128)(2,1)S(1)}, bf16[512,512]{1,0:T(8,128)(2,1)S(1)}, bf16[512,512]{1,0:T(8,128)(2,1)S(1...) custom-call(f32[512,512]{1,0:T(8,128)S(1)} %get-tuple-element.106.re, ...), custom_call_target="tpu_custom_call" | custom-call | flops 1000000000 | bytes 1000000 | tf_op jit(solution)/shard_map/pallas_call | solution.py:253
  227.3 4.1 %collective-permute-done.36 = bf16[2,2,2,288,512]{4,3,0,2,1:T(8,128)(2,1)S(1)} collective-permute-done((bf16[2,2,2,288,512]{4,3,0,2,1:T(8,128)(2,1)S(1)}, bf16[2,2,2,288,512]{4,3,0,2,1:T(8,128)(2,1)S(1)}, u32[]{:S(2)}, u32[]{:S(2)}) %collective-permute-start.36) | collective-permute-done | bytes 2359328 | tf_op jit(solution)/shard_map/ppermute | solution.py:34
  239.5 13.6 %shard_map.286 = (f32[512,512]{1,0:T(8,128)S(1)}, bf16[512,512]{1,0:T(8,128)(2,1)S(1)}, bf16[512,512]{1,0:T(8,128)(2,1)S(1)}, bf16[512,512]{1,0:T(8,128)(2,1)S(1...) custom-call(f32[512,512]{1,0:T(8,128)S(1)} %get-tuple-element.113.re, ...), custom_call_target="tpu_custom_call" | custom-call | flops 1000000000 | bytes 1000000 | tf_op jit(solution)/shard_map/pallas_call | solution.py:253
  266.9 4.2 %collective-permute-done.45 = bf16[256,512]{1,0:T(8,128)(2,1)S(1)} collective-permute-done((bf16[256,512]{1,0:T(8,128)(2,1)S(1)}, bf16[256,512]{1,0:T(8,128)(2,1)S(1)}, u32[]{:S(2)}, u32[]{:S(2)}) %collective-permute-start.45) | collective-permute-done | bytes 262176 | tf_op jit(solution)/shard_map/ppermute | solution.py:34
  276.0 12.0 %collective-permute-done.66 = f32[69,512]{1,0:T(8,128)S(1)} collective-permute-done((f32[69,512]{1,0:T(8,128)S(1)}, f32[69,512]{1,0:T(8,128)S(1)}, u32[]{:S(2)}, u32[]{:S(2)}) %collective-permute-start.66) | collective-permute-done | bytes 141344 | tf_op jit(solution)/shard_map/ppermute | solution.py:34
  288.7 5.2 %fusion = f32[2048,512]{1,0:T(8,128)S(1)} fusion(bf16[2048,512]{1,0:T(8,128)(2,1)S(1)} %bitcast.312, s32[2048]{0:T(1024)S(1)} %copy-done.31), kind=kOutput, calls=%fused_computation.1 | convolution fusion | flops 4299161600 | bytes 6299648 | tf_op jit(solution)/shard_map/dot_general | solution.py:274
  304.6 7.7 %collective-permute-done.42 = bf16[2,2,144,512]{3,2,0,1:T(8,128)(2,1)} collective-permute-done((bf16[2,2,144,512]{3,2,0,1:T(8,128)(2,1)}, bf16[2,2,144,512]{3,2,0,1:T(8,128)(2,1)}, u32[]{:S(2)}, u32[]{:S(2)}) %collective-permute-start.42) | collective-permute-done | bytes 589856 | tf_op jit(solution)/shard_map/ppermute | solution.py:34
  324.5 4.3 %collective-permute-done.49 = bf16[2,144,512]{2,1,0:T(8,128)(2,1)S(1)} collective-permute-done((bf16[2,144,512]{2,1,0:T(8,128)(2,1)}, bf16[2,144,512]{2,1,0:T(8,128)(2,1)S(1)}, u32[]{:S(2)}, u32[]{:S(2)}) %collective-permute-start.49) | collective-permute-done | bytes 294944 | tf_op jit(solution)/shard_map/ppermute | solution.py:34
  338.8 8.8 %collective-permute-done.56 = bf16[240,512]{1,0:T(8,128)(2,1)} collective-permute-done((bf16[240,512]{1,0:T(8,128)(2,1)}, bf16[240,512]{1,0:T(8,128)(2,1)}, u32[]{:S(2)}, u32[]{:S(2)}) %collective-permute-start.56) | collective-permute-done | bytes 245792 | tf_op jit(solution)/shard_map/ppermute | solution.py:75
  349.5 15.2 %collective-permute-done.53 = bf16[288,512]{1,0:T(8,128)(2,1)} collective-permute-done((bf16[288,512]{1,0:T(8,128)(2,1)S(1)}, bf16[288,512]{1,0:T(8,128)(2,1)}, u32[]{:S(2)}, u32[]{:S(2)}) %collective-permute-start.53) | collective-permute-done | bytes 294944 | tf_op jit(solution)/shard_map/ppermute | solution.py:75
  (336 shorter events, 176.9 us)
Async XLA Ops:
  1.8 24.5 %collective-permute-start.15 = (bf16[288,512]{1,0:T(8,128)(2,1)S(1)}, bf16[288,512]{1,0:T(8,128)(2,1)S(1)}, u32[]{:S(2)}, u32[]{:S(2)}) collective-permute-start(bf16[288,512]{1,0:T(8,128)(2,1)S(1)} %convert_element_type.254), channel_id=1, source_target_pairs={{24,0},{16,8},{8,16},{0,24},{25,1},{17,9},{9,17},{1,25},{26,2},{18... | collective-permute-start | bytes 884744 | tf_op jit(solution)/shard_map/ppermute | solution.py:75
  6.9 37.3 %collective-permute-start.14 = (bf16[288,512]{1,0:T(8,128)(2,1)S(1)}, bf16[288,512]{1,0:T(8,128)(2,1)S(1)}, u32[]{:S(2)}, u32[]{:S(2)}) collective-permute-start(bf16[288,512]{1,0:T(8,128)(2,1)S(1)} %convert_element_type.254), channel_id=1, source_target_pairs={{16,0},{24,8},{0,16},{8,24},{17,1},{25,9},{1,17},{9,25},{18,2},{26... | collective-permute-start | bytes 884744 | tf_op jit(solution)/shard_map/ppermute | solution.py:75
  6.9 37.3 %collective-permute-start.13 = (bf16[288,512]{1,0:T(8,128)(2,1)S(1)}, bf16[288,512]{1,0:T(8,128)(2,1)S(1)}, u32[]{:S(2)}, u32[]{:S(2)}) collective-permute-start(bf16[288,512]{1,0:T(8,128)(2,1)S(1)} %convert_element_type.254), channel_id=1, source_target_pairs={{8,0},{0,8},{24,16},{16,24},{9,1},{1,9},{25,17},{17,25},{10,2},{2,... | collective-permute-start | bytes 884744 | tf_op jit(solution)/shard_map/ppermute | solution.py:75
  22.6 23.6 %collective-permute-start.7 = (bf16[256,512]{1,0:T(8,128)(2,1)S(1)}, bf16[256,512]{1,0:T(8,128)(2,1)S(1)}, u32[]{:S(2)}, u32[]{:S(2)}) collective-permute-start(bf16[256,512]{1,0:T(8,128)(2,1)S(1)} %get-tuple-element.211), channel_id=1, source_target_pairs={{24,0},{16,8},{8,16},{0,24},{25,1},{17,9},{9,17},{1,25},{26,2},{18... | collective-permute-start | bytes 786440 | tf_op jit(solution)/shard_map/ppermute | solution.py:75
  26.2 28.3 %collective-permute-start.6 = (bf16[256,512]{1,0:T(8,128)(2,1)S(1)}, bf16[256,512]{1,0:T(8,128)(2,1)S(1)}, u32[]{:S(2)}, u32[]{:S(2)}) collective-permute-start(bf16[256,512]{1,0:T(8,128)(2,1)S(1)} %get-tuple-element.210), channel_id=1, source_target_pairs={{16,0},{24,8},{0,16},{8,24},{17,1},{25,9},{1,17},{9,25},{18,2},{26... | collective-permute-start | bytes 786440 | tf_op jit(solution)/shard_map/ppermute | solution.py:75
  26.3 28.2 %collective-permute-start.5 = (bf16[256,512]{1,0:T(8,128)(2,1)S(1)}, bf16[256,512]{1,0:T(8,128)(2,1)S(1)}, u32[]{:S(2)}, u32[]{:S(2)}) collective-permute-start(bf16[256,512]{1,0:T(8,128)(2,1)S(1)} %get-tuple-element.209), channel_id=1, source_target_pairs={{8,0},{0,8},{24,16},{16,24},{9,1},{1,9},{25,17},{17,25},{10,2},{2,... | collective-permute-start | bytes 786440 | tf_op jit(solution)/shard_map/ppermute | solution.py:75
  54.7 29.9 %collective-permute-start.8 = (bf16[4,256,512]{2,1,0:T(8,128)(2,1)S(1)}, bf16[4,256,512]{2,1,0:T(8,128)(2,1)S(1)}, u32[]{:S(2)}, u32[]{:S(2)}) collective-permute-start(bf16[4,256,512]{2,1,0:T(8,128)(2,1)S(1)} %get-tuple-element.187), channel_id=1, source_target_pairs={{0,2},{2,0},{1,3},{3,1},{4,6},{6,4},{5,7},{7,5},{8,10},{10,8},{9,1... | collective-permute-start | bytes 3145736 | tf_op jit(solution)/shard_map/ppermute | solution.py:34
  58.6 25.0 %collective-permute-start.19 = (bf16[2,2,144,512]{3,2,0,1:T(8,128)(2,1)S(1)}, bf16[2,2,144,512]{3,2,0,1:T(8,128)(2,1)S(1)}, u32[]{:S(2)}, u32[]{:S(2)}) collective-permute-start(bf16[2,2,144,512]{3,2,0,1:T(8,128)(2,1)S(1)} %pad_maximum_fusion.5), channel_id=1, source_target_pairs={{0,4},{4,0},{1,5},{5,1},{2,6},{6,2},{3,7},{7,3},{8,12},{12,8},{9,1... | collective-permute-start | bytes 1769480 | tf_op jit(solution)/shard_map/ppermute | solution.py:34
  64.8 19.0 %collective-permute-start.17 = (bf16[2,2,144,512]{3,2,0,1:T(8,128)(2,1)S(1)}, bf16[2,2,144,512]{3,2,0,1:T(8,128)(2,1)S(1)}, u32[]{:S(2)}, u32[]{:S(2)}) collective-permute-start(bf16[2,2,144,512]{3,2,0,1:T(8,128)(2,1)S(1)} %pad_maximum_fusion.4), channel_id=1, source_target_pairs={{0,1},{1,0},{2,3},{3,2},{4,5},{5,4},{6,7},{7,6},{8,9},{9,8},{10,11... | collective-permute-start | bytes 1769480 | tf_op jit(solution)/shard_map/ppermute | solution.py:34
  66.5 29.8 %collective-permute-start.26 = (bf16[2,2,144,512]{3,2,1,0:T(8,128)(2,1)S(1)}, bf16[2,2,144,512]{3,2,1,0:T(8,128)(2,1)S(1)}, u32[]{:S(2)}, u32[]{:S(2)}) collective-permute-start(bf16[2,2,144,512]{3,2,1,0:T(8,128)(2,1)S(1)} %pad_maximum_fusion.7), channel_id=1, source_target_pairs={{0,4},{4,0},{1,5},{5,1},{2,6},{6,2},{3,7},{7,3},{8,12},{12,8},{9,1... | collective-permute-start | bytes 1769480 | tf_op jit(solution)/shard_map/ppermute | solution.py:34
  71.1 25.3 %collective-permute-start.24 = (bf16[2,2,144,512]{3,2,0,1:T(8,128)(2,1)S(1)}, bf16[2,2,144,512]{3,2,0,1:T(8,128)(2,1)S(1)}, u32[]{:S(2)}, u32[]{:S(2)}) collective-permute-start(bf16[2,2,144,512]{3,2,0,1:T(8,128)(2,1)S(1)} %pad_maximum_fusion.6), channel_id=1, source_target_pairs={{0,1},{1,0},{2,3},{3,2},{4,5},{5,4},{6,7},{7,6},{8,9},{9,8},{10,11... | collective-permute-start | bytes 1769480 | tf_op jit(solution)/shard_map/ppermute | solution.py:34
  84.5 32.9 %collective-permute-start.20 = (bf16[2,2,2,288,512]{4,3,2,0,1:T(8,128)(2,1)S(1)}, bf16[2,2,2,288,512]{4,3,2,0,1:T(8,128)(2,1)S(1)}, u32[]{:S(2)}, u32[]{:S(2)}) collective-permute-start(bf16[2,2,2,288,512]{4,3,2,0,1:T(8,128)(2,1)S(1)} %maximum_maximum_fusion), channel_id=1, source_target_pairs={{0,2},{2,0},{1,3},{3,1},{4,6},{6,4},{5,7},{7,5},{8,10},{10,8},{9,1... | collective-permute-start | bytes 7077896 | tf_op jit(solution)/shard_map/ppermute | solution.py:34
  98.2 43.0 %collective-permute-start.27 = (bf16[2,2,2,288,512]{4,3,2,1,0:T(8,128)(2,1)}, bf16[2,2,2,288,512]{4,3,2,1,0:T(8,128)(2,1)}, u32[]{:S(2)}, u32[]{:S(2)}) collective-permute-start(bf16[2,2,2,288,512]{4,3,2,1,0:T(8,128)(2,1)} %maximum_maximum_fusion.1.refs_1_), channel_id=1, source_target_pairs={{0,2},{2,0},{1,3},{3,1},{4,6},{6,4},{5,7},{7,5},{8,10},{10,8},{9,1... | collective-permute-start | bytes 7077896 | tf_op jit(solution)/shard_map/ppermute | solution.py:34
  234.1 22.5 %collective-permute-start.39 = (bf16[2,2,144,512]{3,2,0,1:T(8,128)(2,1)}, bf16[2,2,144,512]{3,2,0,1:T(8,128)(2,1)}, u32[]{:S(2)}, u32[]{:S(2)}) collective-permute-start(bf16[2,2,144,512]{3,2,0,1:T(8,128)(2,1)} %select_bitcast_fusion), channel_id=1, source_target_pairs={{0,1},{1,0},{2,3},{3,2},{4,5},{5,4},{6,7},{7,6},{8,9},{9,8},{10,11... | collective-permute-start | bytes 1769480 | tf_op jit(solution)/shard_map/ppermute | solution.py:34
  235.6 21.0 %collective-permute-start.38 = (bf16[2,2,144,512]{3,2,0,1:T(8,128)(2,1)}, bf16[2,2,144,512]{3,2,0,1:T(8,128)(2,1)}, u32[]{:S(2)}, u32[]{:S(2)}) collective-permute-start(bf16[2,2,144,512]{3,2,0,1:T(8,128)(2,1)} %select_bitcast_fusion.1), channel_id=1, source_target_pairs={{0,4},{4,0},{1,5},{5,1},{2,6},{6,2},{3,7},{7,3},{8,12},{12,8},{9,1... | collective-permute-start | bytes 1769480 | tf_op jit(solution)/shard_map/ppermute | solution.py:34
  266.2 27.9 %collective-permute-start.40 = (bf16[2,2,2,288,512]{4,3,0,1,2:T(8,128)(2,1)S(1)}, bf16[2,2,2,288,512]{4,3,0,1,2:T(8,128)(2,1)S(1)}, u32[]{:S(2)}, u32[]{:S(2)}) collective-permute-start(bf16[2,2,2,288,512]{4,3,0,1,2:T(8,128)(2,1)S(1)} %copy.148), channel_id=1, source_target_pairs={{0,2},{2,0},{1,3},{3,1},{4,6},{6,4},{5,7},{7,5},{8,10},{10,8},{9,1... | collective-permute-start | bytes 7077896 | tf_op jit(solution)/shard_map/ppermute | solution.py:34
  301.1 33.5 %collective-permute-start.68 = (f32[69,512]{1,0:T(8,128)}, f32[69,512]{1,0:T(8,128)}, u32[]{:S(2)}, u32[]{:S(2)}) collective-permute-start(f32[69,512]{1,0:T(8,128)} %add.327), channel_id=1, source_target_pairs={{8,0},{0,8},{24,16},{16,24},{9,1},{1,9},{25,17},{17,25},{10,2},{2,... | collective-permute-start | bytes 423944 | tf_op jit(solution)/shard_map/ppermute | solution.py:75
  303.2 19.7 %collective-permute-start.50 = (bf16[2,144,512]{2,1,0:T(8,128)(2,1)}, bf16[2,144,512]{2,1,0:T(8,128)(2,1)}, u32[]{:S(2)}, u32[]{:S(2)}) collective-permute-start(bf16[2,144,512]{2,1,0:T(8,128)(2,1)} %get-tuple-element.140), channel_id=1, source_target_pairs={{0,1},{1,0},{2,3},{3,2},{4,5},{5,4},{6,7},{7,6},{8,9},{9,8},{10,11... | collective-permute-start | bytes 884744 | tf_op jit(solution)/shard_map/ppermute | solution.py:34
  312.3 22.4 %collective-permute-start.57 = (bf16[240,512]{1,0:T(8,128)(2,1)}, bf16[240,512]{1,0:T(8,128)(2,1)}, u32[]{:S(2)}, u32[]{:S(2)}) collective-permute-start(bf16[240,512]{1,0:T(8,128)(2,1)} %get-tuple-element.184), channel_id=1, source_target_pairs={{24,0},{16,8},{8,16},{0,24},{25,1},{17,9},{9,17},{1,25},{26,2},{18... | collective-permute-start | bytes 737288 | tf_op jit(solution)/shard_map/ppermute | solution.py:75
  314.8 32.8 %collective-permute-start.56 = (bf16[240,512]{1,0:T(8,128)(2,1)}, bf16[240,512]{1,0:T(8,128)(2,1)}, u32[]{:S(2)}, u32[]{:S(2)}) collective-permute-start(bf16[240,512]{1,0:T(8,128)(2,1)} %get-tuple-element.185), channel_id=1, source_target_pairs={{16,0},{24,8},{0,16},{8,24},{17,1},{25,9},{1,17},{9,25},{18,2},{26... | collective-permute-start | bytes 737288 | tf_op jit(solution)/shard_map/ppermute | solution.py:75
  328.8 18.7 %collective-permute-start.55 = (bf16[240,512]{1,0:T(8,128)(2,1)}, bf16[240,512]{1,0:T(8,128)(2,1)}, u32[]{:S(2)}, u32[]{:S(2)}) collective-permute-start(bf16[240,512]{1,0:T(8,128)(2,1)} %get-tuple-element.183), channel_id=1, source_target_pairs={{8,0},{0,8},{24,16},{16,24},{9,1},{1,9},{25,17},{17,25},{10,2},{2,... | collective-permute-start | bytes 737288 | tf_op jit(solution)/shard_map/ppermute | solution.py:75
  334.6 30.1 %collective-permute-start.53 = (bf16[288,512]{1,0:T(8,128)(2,1)S(1)}, bf16[288,512]{1,0:T(8,128)(2,1)}, u32[]{:S(2)}, u32[]{:S(2)}) collective-permute-start(bf16[288,512]{1,0:T(8,128)(2,1)S(1)} %get-tuple-element.172), channel_id=1, source_target_pairs={{16,0},{24,8},{0,16},{8,24},{17,1},{25,9},{1,17},{9,25},{18,2},{26... | collective-permute-start | bytes 884744 | tf_op jit(solution)/shard_map/ppermute | solution.py:75
  334.6 30.1 %collective-permute-start.52 = (bf16[288,512]{1,0:T(8,128)(2,1)S(1)}, bf16[288,512]{1,0:T(8,128)(2,1)}, u32[]{:S(2)}, u32[]{:S(2)}) collective-permute-start(bf16[288,512]{1,0:T(8,128)(2,1)S(1)} %get-tuple-element.170), channel_id=1, source_target_pairs={{8,0},{0,8},{24,16},{16,24},{9,1},{1,9},{25,17},{17,25},{10,2},{2,... | collective-permute-start | bytes 884744 | tf_op jit(solution)/shard_map/ppermute | solution.py:75
  347.5 21.1 %collective-permute-start.69 = (f32[69,512]{1,0:T(8,128)}, f32[69,512]{1,0:T(8,128)}, u32[]{:S(2)}, u32[]{:S(2)}) collective-permute-start(f32[69,512]{1,0:T(8,128)} %add.328), channel_id=1, source_target_pairs={{16,0},{24,8},{0,16},{8,24},{17,1},{25,9},{1,17},{9,25},{18,2},{26... | collective-permute-start | bytes 423944 | tf_op jit(solution)/shard_map/ppermute | solution.py:75
  (78 other events, 792.9 us)

commit v4 on v3

--- a/solution.py
+++ b/solution.py
@@ -340,7 +340,7 @@
     outs, refs = (refs[9:11], refs[11:]) if last else (refs[9:15], refs[15:])
     stat_ref, outs = outs[0], outs[1:]
     mix_ref, u1_ref, low1_ref, slope_ref, act_ref, u2_ref, low_ref = refs[:7]
-    keys_ref, values_ref, bias_ref, own_ref, wide_ref, turned_ref, scale_ref = refs[7:]
+    keys_ref, values_ref, bias_ref, own_ref, wide_ref, turned_ref, scale_ref, prob_ref = refs[7:]
     moves.put(base + FAR, far_ref.at[:, :D], slice(0, far_ref.shape[0]))
     moves.put(base + FAR, far_ref.at[:, D:], slice(far_ref.shape[0], x_ref.shape[0]))
     tokens = x_ref.shape[0]
@@ -356,29 +356,36 @@
     own_ref[...] = weigh(marks, product)
 
     def pair_step(pair, carry):
-        lanes = pl.ds(pl.multiple_of(pair * PAIR, PAIR), PAIR)
+        lanes = slice(pair * PAIR, pair * PAIR + PAIR)
         key_pair = keys_ref[:, lanes]
         q_pair = q_ref[:, lanes]
         for side in range(2):
-            head = pl.ds(2 * pair + side, 1)
-            scores = dot_nt(key_pair, q_pair * lane_marks(side, SCALING).astype(BF16))
-            scores = scores + bias_ref[...]
-            top = jnp.max(scores, axis=0, keepdims=True)
-            own = own_ref[head, :]
-            top = jnp.concatenate([top[:, :quarter], jnp.maximum(top[:, quarter:], own)], axis=1)
-            exps = jnp.exp(scores - top)
-            own = jnp.exp(own - top[:, quarter:])
-            amount = jnp.sum(exps, axis=0, keepdims=True)
-            amount = jnp.concatenate([amount[:, :quarter], amount[:, quarter:] + own], axis=1)
-            inverse = 1.0 / amount
-            own_ref[head, :] = own * inverse[:, quarter:]
-            stat_ref[head, :] = top + jnp.log(amount)
-            prob = (exps * inverse).astype(BF16)
-            part = pl.ds(pl.multiple_of(pair * PAIR + side * HEAD_DIM, HEAD_DIM), HEAD_DIM)
-            turned_ref[part, :] = dot(values_ref[part, :], prob)
+            head = slice(2 * pair + side, 2 * pair + side + 1)
+            scaled = q_pair * lane_marks(side, SCALING).astype(BF16)
+            for start in range(0, tokens, 256):
+                spots = slice(start, start + 256)
+                scores = dot_nt(key_pair, scaled[spots]) + bias_ref[:, spots]
+                top = jnp.max(scores, axis=0, keepdims=True)
+                if start >= quarter:
+                    far_spots = slice(start - quarter, start - quarter + 256)
+                    own = own_ref[head, far_spots]
+                    top = jnp.maximum(top, own)
+                exps = jnp.exp(scores - top)
+                amount = jnp.sum(exps, axis=0, keepdims=True)
+                if start >= quarter:
+                    own = jnp.exp(own - top)
+                    amount = amount + own
+                inverse = 1.0 / amount
+                if start >= quarter:
+                    own_ref[head, far_spots] = own * inverse
+                stat_ref[head, spots] = top + jnp.log(amount)
+                prob_ref[:, spots] = (exps * inverse).astype(BF16)
+            part = slice(pair * PAIR + side * HEAD_DIM, pair * PAIR + side * HEAD_DIM + HEAD_DIM)
+            turned_ref[part, :] = dot(values_ref[part, :], prob_ref[...])
         return carry
 
-    lax.fori_loop(0, D // PAIR, pair_step, 0)
+    for pair in range(D // PAIR):
+        pair_step(pair, 0)
     wide_ref[...] = turned_ref[...].T
     own_share = spread(marks, own_ref[...]) * v_ref[far_half].astype(F32)
     mix_ref[:quarter] = wide_ref[:quarter].astype(BF16)
@@ -439,6 +446,7 @@
     grad_ref, own_col_ref, stat_ref, own_row_ref, key_col_ref, vec_ref,
     sum1_ref, low2_ref, hid_ref, low1_ref, gq_ref, gk_ref, gv_ref, send_ref, gvec_ref,
     keys_ref, values_ref, bias_ref, gmix_ref, own_p_ref, own_s_ref, turned_ref, wide_ref, scale_ref,
+    score_ref, prob_ref,
 ):
     bias_ref[...] = jnp.where(key_col_ref[...] == own_row_ref[...], 0.0, NEGATIVE)
     scale_ref[...] = stat_ref[HEADS:].T
@@ -498,7 +506,7 @@
     own_s_ref[...] = own_grad
 
     def pair_step(pair, carry):
-        lanes = pl.ds(pl.multiple_of(pair * PAIR, PAIR), PAIR)
+        lanes = slice(pair * PAIR, pair * PAIR + PAIR)
         key_pair = keys_ref[:, lanes]
         value_pair = values_ref[:, lanes]
         q_pair = q_ref[:, lanes]
@@ -509,24 +517,31 @@
             head = 2 * pair + side
             scaled = q_pair * lane_marks(side, SCALING).astype(BF16)
             mix_side = mix_pair * lane_marks(side, 1.0).astype(BF16)
-            lse = lse_ref[pl.ds(head, 1), :]
-            prob = jnp.exp(dot_nt(key_pair, scaled) + bias_ref[...] - lse)
-            grad_p = dot_nt(value_pair, mix_side)
-            delta = jnp.sum(prob * grad_p, axis=0, keepdims=True)
-            own_p = own_p_ref[pl.ds(head, 1), :]
-            own_g = own_s_ref[pl.ds(head, 1), :]
-            delta = jnp.concatenate([delta[:, :quarter], delta[:, quarter:] + own_p * own_g], axis=1)
-            own_s_ref[pl.ds(head, 1), :] = own_p * (own_g - delta[:, quarter:])
-            grad_s = (prob * (grad_p - delta)).astype(BF16)
+            for start in range(0, tokens, 256):
+                spots = slice(start, start + 256)
+                prob = dot_nt(key_pair, scaled[spots]) + bias_ref[:, spots]
+                prob = jnp.exp(prob - lse_ref[slice(head, head + 1), spots])
+                grad_p = dot_nt(value_pair, mix_side[spots])
+                delta = jnp.sum(prob * grad_p, axis=0, keepdims=True)
+                if start >= quarter:
+                    far_spots = slice(start - quarter, start - quarter + 256)
+                    own_p = own_p_ref[slice(head, head + 1), far_spots]
+                    own_g = own_s_ref[slice(head, head + 1), far_spots]
+                    delta = delta + own_p * own_g
+                    own_s_ref[slice(head, head + 1), far_spots] = own_p * (own_g - delta)
+                score_ref[:, spots] = (prob * (grad_p - delta)).astype(BF16)
+                prob_ref[:, spots] = prob.astype(BF16)
+            grad_s = score_ref[...]
             grad_k = grad_k + dot(grad_s, scaled)
-            grad_v = grad_v + dot(prob.astype(BF16), mix_side)
-            part = pl.ds(pl.multiple_of(pair * PAIR + side * HEAD_DIM, HEAD_DIM), HEAD_DIM)
+            grad_v = grad_v + dot(prob_ref[...], mix_side)
+            part = slice(pair * PAIR + side * HEAD_DIM, pair * PAIR + side * HEAD_DIM + HEAD_DIM)
             wide_ref[part, :] = dot(turned_ref[part, :], grad_s)
         gk_ref[:, lanes] = grad_k
         gv_ref[:, lanes] = grad_v
         return carry
 
-    lax.fori_loop(0, D // PAIR, pair_step, 0)
+    for pair in range(D // PAIR):
+        pair_step(pair, 0)
     send_ref[:, :D] = gk_ref[quarter:].astype(BF16)
     send_ref[:, D:] = gv_ref[quarter:].astype(BF16)
     own_score = spread(marks, own_s_ref[...]) * SCALING
@@ -634,7 +649,8 @@
         partial(forward_kernel, last, SQUARES * layer),
         outs,
         (state, queries, keys, values, far, own_row, key_col, own_col, vecs),
-        vmem(*[slim] * 7, slim, ((D, tokens), BF16), square, own, wide, turned, ((tokens, PAIR), F32)),
+        vmem(*[slim] * 7, slim, ((D, tokens), BF16), square, own, wide, turned, ((tokens, PAIR), F32),
+            ((tokens, tokens), BF16)),
         fetch=[(mats, 6 * layer + i) for i in range(3, 6 if last else 9)],
         store=store,
     )
@@ -653,7 +669,7 @@
         (gradient, own_col, stat, own_row, key_col, vecs),
         vmem(
             slim, slim, square, slim, own, own, ((D, tokens), BF16), ((D, tokens), F32),
-            ((tokens, HEADS), F32),
+            ((tokens, HEADS), F32), ((tokens, tokens), BF16), ((tokens, tokens), BF16),
         ),
         needed,
         fetch=[

time: 398 us -> 394 us (0.990)
  Pallas kernels: 112 us -> 105 us
    pallas_call x18, Pallas kernels: 112 us -> 105 us  [call(): pl.pallas_call(kernel, out_shape=shapes, in_specs=[small] * len(scalars)...]
  transfers between devices with their start and end apart: 70 -> 70, of which waited for: 34 -> 34; matrix products, arithmetic and copies ran while one was open for 13% -> 13% of each run, Pallas kernels for 13% -> 12%
where the time goes in v4:
time: 394 us; the launch traced here: 388 us
  waiting for transfers between devices  141 us (36%)
  Pallas kernels  105 us (27%)
  starting transfers between devices  72.5 us (18%)
  other arithmetic  41.8 us (11%)
  matrix products  11.9 us (3%)
  local copies, waits for them, and re-layouts  9.42 us (2%)
  between operations  6.11 us (2%)
    pallas_call x18, Pallas kernels, call(): pl.pallas_call(kernel, out_shape=shapes, in_specs=[small] * len(scalars)...  105 us
    ppermute x50, waiting for transfers between devices, flip(): return lax.ppermute(block, axis, [(0, 1), (1, 0)])  87.8 us
    ppermute x17, waiting for transfers between devices, z_swap(): return lax.ppermute(block, 'z', pairs)  50.1 us
    ppermute x50, starting transfers between devices, flip(): return lax.ppermute(block, axis, [(0, 1), (1, 0)])  46.1 us
    ppermute x17, starting transfers between devices, z_swap(): return lax.ppermute(block, 'z', pairs)  23 us
    convert_element_type x11, other arithmetic, rounded_sum(): return (a.astype(F32) + b.astype(F32)).astype(a.dtype)  7.89 us
  transfers between devices with their start and end apart: 70, of which 34 were waited for; matrix products, arithmetic and copies ran while one was open for 13% of the time, Pallas kernels for 12%

profile of v4, /device:TPU:0, one launch (start us, length us, event | category | flops | bytes accessed | tf_op | source)
XLA Modules:
  0.0 387.8 jit_solution(6877313424439368259)
XLA Ops:
  1.8 5.1 %collective-permute-start.15 = (bf16[288,512]{1,0:T(8,128)(2,1)S(1)}, bf16[288,512]{1,0:T(8,128)(2,1)S(1)}, u32[]{:S(2)}, u32[]{:S(2)}) collective-permute-start(bf16[288,512]{1,0:T(8,128)(2,1)S(1)} %convert_element_type.254), channel_id=1, source_target_pairs={{24,0},{16,8},{8,16},{0,24},{25,1},{17,9},{9,17},{1,25},{26,2},{18... | collective-permute-start | bytes 884744 | tf_op jit(solution)/shard_map/ppermute | solution.py:75
  28.1 16.2 %collective-permute-done.14 = bf16[288,512]{1,0:T(8,128)(2,1)S(1)} collective-permute-done((bf16[288,512]{1,0:T(8,128)(2,1)S(1)}, bf16[288,512]{1,0:T(8,128)(2,1)S(1)}, u32[]{:S(2)}, u32[]{:S(2)}) %collective-permute-start.14) | collective-permute-done | bytes 294944 | tf_op jit(solution)/shard_map/ppermute | solution.py:75
  46.2 8.3 %collective-permute-done.6 = bf16[256,512]{1,0:T(8,128)(2,1)S(1)} collective-permute-done((bf16[256,512]{1,0:T(8,128)(2,1)S(1)}, bf16[256,512]{1,0:T(8,128)(2,1)S(1)}, u32[]{:S(2)}, u32[]{:S(2)}) %collective-permute-start.6) | collective-permute-done | bytes 262176 | tf_op jit(solution)/shard_map/ppermute | solution.py:75
  60.2 4.5 %collective-permute-done.16 = bf16[2,144,512]{2,1,0:T(8,128)(2,1)S(1)} collective-permute-done((bf16[2,144,512]{2,1,0:T(8,128)(2,1)S(1)}, bf16[2,144,512]{2,1,0:T(8,128)(2,1)S(1)}, u32[]{:S(2)}, u32[]{:S(2)}) %collective-permute-start.16) | collective-permute-done | bytes 294944 | tf_op jit(solution)/shard_map/ppermute | solution.py:34
  72.7 10.9 %collective-permute-done.19 = bf16[2,2,144,512]{3,2,0,1:T(8,128)(2,1)S(1)} collective-permute-done((bf16[2,2,144,512]{3,2,0,1:T(8,128)(2,1)S(1)}, bf16[2,2,144,512]{3,2,0,1:T(8,128)(2,1)S(1)}, u32[]{:S(2)}, u32[]{:S(2)}) %collective-permute-start.19) | collective-permute-done | bytes 589856 | tf_op jit(solution)/shard_map/ppermute | solution.py:34
  85.3 5.0 %fusion.4 = bf16[2048,512]{1,0:T(8,128)(2,1)S(1)} fusion(bf16[2048,512]{1,0:T(8,128)(2,1)S(1)} %bitcast.288, s32[2048]{0:T(1024)S(1)} %fusion.43), kind=kOutput, calls=%fused_computation.7 | convolution fusion | flops 4300210176 | bytes 4202496 | tf_op jit(solution)/shard_map/dot_general | solution.py:270
  98.2 8.9 %collective-permute-done.9 = bf16[2,256,512]{2,1,0:T(8,128)(2,1)S(1)} collective-permute-done((bf16[2,256,512]{2,1,0:T(8,128)(2,1)S(1)}, bf16[2,256,512]{2,1,0:T(8,128)(2,1)S(1)}, u32[]{:S(2)}, u32[]{:S(2)}) %collective-permute-start.9) | collective-permute-done | bytes 524320 | tf_op jit(solution)/shard_map/ppermute | solution.py:34
  110.8 4.5 %collective-permute-done.12 = bf16[256,512]{1,0:T(8,128)(2,1)S(1)} collective-permute-done((bf16[256,512]{1,0:T(8,128)(2,1)S(1)}, bf16[256,512]{1,0:T(8,128)(2,1)S(1)}, u32[]{:S(2)}, u32[]{:S(2)}) %collective-permute-start.12) | collective-permute-done | bytes 262176 | tf_op jit(solution)/shard_map/ppermute | solution.py:34
  120.2 5.0 %shard_map.273 = (bf16[512,512]{1,0:T(8,128)(2,1)S(1)}, bf16[512,512]{1,0:T(8,128)(2,1)S(1)}, bf16[512,512]{1,0:T(8,128)(2,1)S(1)}, bf16[256,1024]{1,0:T(8,128)(2,1)}, bf16[132,512,512]{2,1,0:T(8,128)(2,1)}) custom-call(f32[512,512]{1,0:T(8,128)S(1)} %convolution_add_fusion.refs_0_, ...), custom_call_target="tpu_custom_call" | custom-call | flops 1000000000 | bytes 1000000 | tf_op jit(solution)/shard_map/pallas_call | solution.py:253
  127.5 12.3 %shard_map.274 = (f32[16,512]{1,0:T(8,128)S(1)}, f32[512,512]{1,0:T(8,128)S(1)}, bf16[512,512]{1,0:T(8,128)(2,1)S(1)}, bf16[512,512]{1,0:T(8,128)(2,1)S(1)}, bf1...) custom-call(f32[512,512]{1,0:T(8,128)S(1)} %convolution_add_fusion.r, ...), custom_call_target="tpu_custom_call", output_to_operand_aliasing={{6}: (15, {})} | custom-call | flops 1000000000 | bytes 1000000 | tf_op jit(solution)/shard_map/pallas_call | solution.py:253
  140.0 4.9 %shard_map.275.refs_9_.refs_10_.refs_11_.refs_12_.refs_13_.refs_14_.refs_7_.refs_5_.refs_6_ = bf16[132,512,512]{2,1,0:T(8,128)(2,1)} custom-call(s32[1]{0:T(128)} %bitcast.refs_0_, bf16[2,2,2,288,512]{4,3,2,1,0:T(8,128)(2,1)} %maximum_maximum_fusion.1.refs_1_, ...), custom_call_target="tpu_custom_call", output_to_operand_aliasing={{}: (3, {})} | custom-call | flops 1000000000 | bytes 1000000 | tf_op jit(solution)/shard_map/pallas_call | solution.py:253
  144.9 11.2 %shard_map.276 = (f32[16,512]{1,0:T(8,128)S(1)}, f32[512,512]{1,0:T(8,128)S(1)}, bf16[512,512]{1,0:T(8,128)(2,1)S(1)}, bf16[512,512]{1,0:T(8,128)(2,1)S(1)}, bf1...) custom-call(f32[512,512]{1,0:T(8,128)S(1)} %get-tuple-element.85.ref, ...), custom_call_target="tpu_custom_call", output_to_operand_aliasing={{6}: (15, {})} | custom-call | flops 1000000000 | bytes 1000000 | tf_op jit(solution)/shard_map/pallas_call | solution.py:253
  158.2 9.5 %shard_map.277 = (f32[16,512]{1,0:T(8,128)S(1)}, f32[4,512]{1,0:T(4,128)S(1)}, bf16[132,512,512]{2,1,0:T(8,128)(2,1)}) custom-call(f32[512,512]{1,0:T(8,128)S(1)} %get-tuple-element.91.refs_0_, bf16[512,512]{1,0:T(8,128)(2,1)S(1)} %get-tuple-element.92.refs_1_, bf16[512,512]{1,0:T(8,128)(2,1)S(1)} %get-tuple-element.93.refs_2_, ...), custom_call_target="tpu_custom_call", output_to_operand_aliasing={{2}: (12, {})} | custom-call | flops 1000000000 | bytes 1000000 | tf_op jit(solution)/shard_map/pallas_call | solution.py:253
  185.3 12.8 %shard_map.279 = (f32[512,512]{1,0:T(8,128)S(1)}, bf16[512,512]{1,0:T(8,128)(2,1)S(1)}, bf16[512,512]{1,0:T(8,128)(2,1)S(1)}, bf16[512,512]{1,0:T(8,128)(2,1)S(1...) custom-call(f32[4,512]{1,0:T(4,128)S(1)} %fusion.46.refs_0_, ...), custom_call_target="tpu_custom_call" | custom-call | flops 1000000000 | bytes 1000000 | tf_op jit(solution)/shard_map/pallas_call | solution.py:253
  204.7 12.2 %shard_map.281 = (f32[512,512]{1,0:T(8,128)S(1)}, bf16[512,512]{1,0:T(8,128)(2,1)S(1)}, bf16[512,512]{1,0:T(8,128)(2,1)S(1)}, bf16[512,512]{1,0:T(8,128)(2,1)S(1...) custom-call(f32[512,512]{1,0:T(8,128)S(1)} %get-tuple-element.106.re, ...), custom_call_target="tpu_custom_call" | custom-call | flops 1000000000 | bytes 1000000 | tf_op jit(solution)/shard_map/pallas_call | solution.py:253
  222.2 4.1 %collective-permute-done.36 = bf16[2,2,2,288,512]{4,3,0,2,1:T(8,128)(2,1)S(1)} collective-permute-done((bf16[2,2,2,288,512]{4,3,0,2,1:T(8,128)(2,1)S(1)}, bf16[2,2,2,288,512]{4,3,0,2,1:T(8,128)(2,1)S(1)}, u32[]{:S(2)}, u32[]{:S(2)}) %collective-permute-start.36) | collective-permute-done | bytes 2359328 | tf_op jit(solution)/shard_map/ppermute | solution.py:34
  234.4 12.2 %shard_map.286 = (f32[512,512]{1,0:T(8,128)S(1)}, bf16[512,512]{1,0:T(8,128)(2,1)S(1)}, bf16[512,512]{1,0:T(8,128)(2,1)S(1)}, bf16[512,512]{1,0:T(8,128)(2,1)S(1...) custom-call(f32[512,512]{1,0:T(8,128)S(1)} %get-tuple-element.113.re, ...), custom_call_target="tpu_custom_call" | custom-call | flops 1000000000 | bytes 1000000 | tf_op jit(solution)/shard_map/pallas_call | solution.py:253
  260.2 4.3 %collective-permute-done.45 = bf16[256,512]{1,0:T(8,128)(2,1)S(1)} collective-permute-done((bf16[256,512]{1,0:T(8,128)(2,1)S(1)}, bf16[256,512]{1,0:T(8,128)(2,1)S(1)}, u32[]{:S(2)}, u32[]{:S(2)}) %collective-permute-start.45) | collective-permute-done | bytes 262176 | tf_op jit(solution)/shard_map/ppermute | solution.py:34
  269.5 11.9 %collective-permute-done.66 = f32[69,512]{1,0:T(8,128)S(1)} collective-permute-done((f32[69,512]{1,0:T(8,128)S(1)}, f32[69,512]{1,0:T(8,128)S(1)}, u32[]{:S(2)}, u32[]{:S(2)}) %collective-permute-start.66) | collective-permute-done | bytes 141344 | tf_op jit(solution)/shard_map/ppermute | solution.py:34
  282.2 5.2 %fusion = f32[2048,512]{1,0:T(8,128)S(1)} fusion(bf16[2048,512]{1,0:T(8,128)(2,1)S(1)} %bitcast.312, s32[2048]{0:T(1024)S(1)} %copy-done.31), kind=kOutput, calls=%fused_computation.1 | convolution fusion | flops 4299161600 | bytes 6299648 | tf_op jit(solution)/shard_map/dot_general | solution.py:274
  298.0 7.7 %collective-permute-done.42 = bf16[2,2,144,512]{3,2,0,1:T(8,128)(2,1)} collective-permute-done((bf16[2,2,144,512]{3,2,0,1:T(8,128)(2,1)}, bf16[2,2,144,512]{3,2,0,1:T(8,128)(2,1)}, u32[]{:S(2)}, u32[]{:S(2)}) %collective-permute-start.42) | collective-permute-done | bytes 589856 | tf_op jit(solution)/shard_map/ppermute | solution.py:34
  318.0 4.3 %collective-permute-done.49 = bf16[2,144,512]{2,1,0:T(8,128)(2,1)S(1)} collective-permute-done((bf16[2,144,512]{2,1,0:T(8,128)(2,1)}, bf16[2,144,512]{2,1,0:T(8,128)(2,1)S(1)}, u32[]{:S(2)}, u32[]{:S(2)}) %collective-permute-start.49) | collective-permute-done | bytes 294944 | tf_op jit(solution)/shard_map/ppermute | solution.py:34
  332.3 8.7 %collective-permute-done.56 = bf16[240,512]{1,0:T(8,128)(2,1)} collective-permute-done((bf16[240,512]{1,0:T(8,128)(2,1)}, bf16[240,512]{1,0:T(8,128)(2,1)}, u32[]{:S(2)}, u32[]{:S(2)}) %collective-permute-start.56) | collective-permute-done | bytes 245792 | tf_op jit(solution)/shard_map/ppermute | solution.py:75
  342.9 15.3 %collective-permute-done.53 = bf16[288,512]{1,0:T(8,128)(2,1)} collective-permute-done((bf16[288,512]{1,0:T(8,128)(2,1)S(1)}, bf16[288,512]{1,0:T(8,128)(2,1)}, u32[]{:S(2)}, u32[]{:S(2)}) %collective-permute-start.53) | collective-permute-done | bytes 294944 | tf_op jit(solution)/shard_map/ppermute | solution.py:75
  (336 shorter events, 176.6 us)
Async XLA Ops:
  1.8 24.5 %collective-permute-start.15 = (bf16[288,512]{1,0:T(8,128)(2,1)S(1)}, bf16[288,512]{1,0:T(8,128)(2,1)S(1)}, u32[]{:S(2)}, u32[]{:S(2)}) collective-permute-start(bf16[288,512]{1,0:T(8,128)(2,1)S(1)} %convert_element_type.254), channel_id=1, source_target_pairs={{24,0},{16,8},{8,16},{0,24},{25,1},{17,9},{9,17},{1,25},{26,2},{18... | collective-permute-start | bytes 884744 | tf_op jit(solution)/shard_map/ppermute | solution.py:75
  6.9 37.3 %collective-permute-start.14 = (bf16[288,512]{1,0:T(8,128)(2,1)S(1)}, bf16[288,512]{1,0:T(8,128)(2,1)S(1)}, u32[]{:S(2)}, u32[]{:S(2)}) collective-permute-start(bf16[288,512]{1,0:T(8,128)(2,1)S(1)} %convert_element_type.254), channel_id=1, source_target_pairs={{16,0},{24,8},{0,16},{8,24},{17,1},{25,9},{1,17},{9,25},{18,2},{26... | collective-permute-start | bytes 884744 | tf_op jit(solution)/shard_map/ppermute | solution.py:75
  6.9 37.3 %collective-permute-start.13 = (bf16[288,512]{1,0:T(8,128)(2,1)S(1)}, bf16[288,512]{1,0:T(8,128)(2,1)S(1)}, u32[]{:S(2)}, u32[]{:S(2)}) collective-permute-start(bf16[288,512]{1,0:T(8,128)(2,1)S(1)} %convert_element_type.254), channel_id=1, source_target_pairs={{8,0},{0,8},{24,16},{16,24},{9,1},{1,9},{25,17},{17,25},{10,2},{2,... | collective-permute-start | bytes 884744 | tf_op jit(solution)/shard_map/ppermute | solution.py:75
  22.6 23.6 %collective-permute-start.7 = (bf16[256,512]{1,0:T(8,128)(2,1)S(1)}, bf16[256,512]{1,0:T(8,128)(2,1)S(1)}, u32[]{:S(2)}, u32[]{:S(2)}) collective-permute-start(bf16[256,512]{1,0:T(8,128)(2,1)S(1)} %get-tuple-element.211), channel_id=1, source_target_pairs={{24,0},{16,8},{8,16},{0,24},{25,1},{17,9},{9,17},{1,25},{26,2},{18... | collective-permute-start | bytes 786440 | tf_op jit(solution)/shard_map/ppermute | solution.py:75
  26.2 28.3 %collective-permute-start.6 = (bf16[256,512]{1,0:T(8,128)(2,1)S(1)}, bf16[256,512]{1,0:T(8,128)(2,1)S(1)}, u32[]{:S(2)}, u32[]{:S(2)}) collective-permute-start(bf16[256,512]{1,0:T(8,128)(2,1)S(1)} %get-tuple-element.210), channel_id=1, source_target_pairs={{16,0},{24,8},{0,16},{8,24},{17,1},{25,9},{1,17},{9,25},{18,2},{26... | collective-permute-start | bytes 786440 | tf_op jit(solution)/shard_map/ppermute | solution.py:75
  26.3 28.2 %collective-permute-start.5 = (bf16[256,512]{1,0:T(8,128)(2,1)S(1)}, bf16[256,512]{1,0:T(8,128)(2,1)S(1)}, u32[]{:S(2)}, u32[]{:S(2)}) collective-permute-start(bf16[256,512]{1,0:T(8,128)(2,1)S(1)} %get-tuple-element.209), channel_id=1, source_target_pairs={{8,0},{0,8},{24,16},{16,24},{9,1},{1,9},{25,17},{17,25},{10,2},{2,... | collective-permute-start | bytes 786440 | tf_op jit(solution)/shard_map/ppermute | solution.py:75
  54.7 29.6 %collective-permute-start.8 = (bf16[4,256,512]{2,1,0:T(8,128)(2,1)S(1)}, bf16[4,256,512]{2,1,0:T(8,128)(2,1)S(1)}, u32[]{:S(2)}, u32[]{:S(2)}) collective-permute-start(bf16[4,256,512]{2,1,0:T(8,128)(2,1)S(1)} %get-tuple-element.187), channel_id=1, source_target_pairs={{0,2},{2,0},{1,3},{3,1},{4,6},{6,4},{5,7},{7,5},{8,10},{10,8},{9,1... | collective-permute-start | bytes 3145736 | tf_op jit(solution)/shard_map/ppermute | solution.py:34
  58.6 25.0 %collective-permute-start.19 = (bf16[2,2,144,512]{3,2,0,1:T(8,128)(2,1)S(1)}, bf16[2,2,144,512]{3,2,0,1:T(8,128)(2,1)S(1)}, u32[]{:S(2)}, u32[]{:S(2)}) collective-permute-start(bf16[2,2,144,512]{3,2,0,1:T(8,128)(2,1)S(1)} %pad_maximum_fusion.5), channel_id=1, source_target_pairs={{0,4},{4,0},{1,5},{5,1},{2,6},{6,2},{3,7},{7,3},{8,12},{12,8},{9,1... | collective-permute-start | bytes 1769480 | tf_op jit(solution)/shard_map/ppermute | solution.py:34
  64.8 19.0 %collective-permute-start.17 = (bf16[2,2,144,512]{3,2,0,1:T(8,128)(2,1)S(1)}, bf16[2,2,144,512]{3,2,0,1:T(8,128)(2,1)S(1)}, u32[]{:S(2)}, u32[]{:S(2)}) collective-permute-start(bf16[2,2,144,512]{3,2,0,1:T(8,128)(2,1)S(1)} %pad_maximum_fusion.4), channel_id=1, source_target_pairs={{0,1},{1,0},{2,3},{3,2},{4,5},{5,4},{6,7},{7,6},{8,9},{9,8},{10,11... | collective-permute-start | bytes 1769480 | tf_op jit(solution)/shard_map/ppermute | solution.py:34
  66.5 29.8 %collective-permute-start.26 = (bf16[2,2,144,512]{3,2,1,0:T(8,128)(2,1)S(1)}, bf16[2,2,144,512]{3,2,1,0:T(8,128)(2,1)S(1)}, u32[]{:S(2)}, u32[]{:S(2)}) collective-permute-start(bf16[2,2,144,512]{3,2,1,0:T(8,128)(2,1)S(1)} %pad_maximum_fusion.7), channel_id=1, source_target_pairs={{0,4},{4,0},{1,5},{5,1},{2,6},{6,2},{3,7},{7,3},{8,12},{12,8},{9,1... | collective-permute-start | bytes 1769480 | tf_op jit(solution)/shard_map/ppermute | solution.py:34
  71.1 25.3 %collective-permute-start.24 = (bf16[2,2,144,512]{3,2,0,1:T(8,128)(2,1)S(1)}, bf16[2,2,144,512]{3,2,0,1:T(8,128)(2,1)S(1)}, u32[]{:S(2)}, u32[]{:S(2)}) collective-permute-start(bf16[2,2,144,512]{3,2,0,1:T(8,128)(2,1)S(1)} %pad_maximum_fusion.6), channel_id=1, source_target_pairs={{0,1},{1,0},{2,3},{3,2},{4,5},{5,4},{6,7},{7,6},{8,9},{9,8},{10,11... | collective-permute-start | bytes 1769480 | tf_op jit(solution)/shard_map/ppermute | solution.py:34
  84.2 33.2 %collective-permute-start.20 = (bf16[2,2,2,288,512]{4,3,2,0,1:T(8,128)(2,1)S(1)}, bf16[2,2,2,288,512]{4,3,2,0,1:T(8,128)(2,1)S(1)}, u32[]{:S(2)}, u32[]{:S(2)}) collective-permute-start(bf16[2,2,2,288,512]{4,3,2,0,1:T(8,128)(2,1)S(1)} %maximum_maximum_fusion), channel_id=1, source_target_pairs={{0,2},{2,0},{1,3},{3,1},{4,6},{6,4},{5,7},{7,5},{8,10},{10,8},{9,1... | collective-permute-start | bytes 7077896 | tf_op jit(solution)/shard_map/ppermute | solution.py:34
  98.2 41.8 %collective-permute-start.27 = (bf16[2,2,2,288,512]{4,3,2,1,0:T(8,128)(2,1)}, bf16[2,2,2,288,512]{4,3,2,1,0:T(8,128)(2,1)}, u32[]{:S(2)}, u32[]{:S(2)}) collective-permute-start(bf16[2,2,2,288,512]{4,3,2,1,0:T(8,128)(2,1)} %maximum_maximum_fusion.1.refs_1_), channel_id=1, source_target_pairs={{0,2},{2,0},{1,3},{3,1},{4,6},{6,4},{5,7},{7,5},{8,10},{10,8},{9,1... | collective-permute-start | bytes 7077896 | tf_op jit(solution)/shard_map/ppermute | solution.py:34
  228.9 21.1 %collective-permute-start.39 = (bf16[2,2,144,512]{3,2,0,1:T(8,128)(2,1)}, bf16[2,2,144,512]{3,2,0,1:T(8,128)(2,1)}, u32[]{:S(2)}, u32[]{:S(2)}) collective-permute-start(bf16[2,2,144,512]{3,2,0,1:T(8,128)(2,1)} %select_bitcast_fusion), channel_id=1, source_target_pairs={{0,1},{1,0},{2,3},{3,2},{4,5},{5,4},{6,7},{7,6},{8,9},{9,8},{10,11... | collective-permute-start | bytes 1769480 | tf_op jit(solution)/shard_map/ppermute | solution.py:34
  230.4 19.6 %collective-permute-start.38 = (bf16[2,2,144,512]{3,2,0,1:T(8,128)(2,1)}, bf16[2,2,144,512]{3,2,0,1:T(8,128)(2,1)}, u32[]{:S(2)}, u32[]{:S(2)}) collective-permute-start(bf16[2,2,144,512]{3,2,0,1:T(8,128)(2,1)} %select_bitcast_fusion.1), channel_id=1, source_target_pairs={{0,4},{4,0},{1,5},{5,1},{2,6},{6,2},{3,7},{7,3},{8,12},{12,8},{9,1... | collective-permute-start | bytes 1769480 | tf_op jit(solution)/shard_map/ppermute | solution.py:34
  259.6 28.0 %collective-permute-start.40 = (bf16[2,2,2,288,512]{4,3,0,1,2:T(8,128)(2,1)S(1)}, bf16[2,2,2,288,512]{4,3,0,1,2:T(8,128)(2,1)S(1)}, u32[]{:S(2)}, u32[]{:S(2)}) collective-permute-start(bf16[2,2,2,288,512]{4,3,0,1,2:T(8,128)(2,1)S(1)} %copy.148), channel_id=1, source_target_pairs={{0,2},{2,0},{1,3},{3,1},{4,6},{6,4},{5,7},{7,5},{8,10},{10,8},{9,1... | collective-permute-start | bytes 7077896 | tf_op jit(solution)/shard_map/ppermute | solution.py:34
  294.6 33.5 %collective-permute-start.68 = (f32[69,512]{1,0:T(8,128)}, f32[69,512]{1,0:T(8,128)}, u32[]{:S(2)}, u32[]{:S(2)}) collective-permute-start(f32[69,512]{1,0:T(8,128)} %add.327), channel_id=1, source_target_pairs={{8,0},{0,8},{24,16},{16,24},{9,1},{1,9},{25,17},{17,25},{10,2},{2,... | collective-permute-start | bytes 423944 | tf_op jit(solution)/shard_map/ppermute | solution.py:75
  296.7 19.7 %collective-permute-start.50 = (bf16[2,144,512]{2,1,0:T(8,128)(2,1)}, bf16[2,144,512]{2,1,0:T(8,128)(2,1)}, u32[]{:S(2)}, u32[]{:S(2)}) collective-permute-start(bf16[2,144,512]{2,1,0:T(8,128)(2,1)} %get-tuple-element.140), channel_id=1, source_target_pairs={{0,1},{1,0},{2,3},{3,2},{4,5},{5,4},{6,7},{7,6},{8,9},{9,8},{10,11... | collective-permute-start | bytes 884744 | tf_op jit(solution)/shard_map/ppermute | solution.py:34
  305.7 22.4 %collective-permute-start.57 = (bf16[240,512]{1,0:T(8,128)(2,1)}, bf16[240,512]{1,0:T(8,128)(2,1)}, u32[]{:S(2)}, u32[]{:S(2)}) collective-permute-start(bf16[240,512]{1,0:T(8,128)(2,1)} %get-tuple-element.184), channel_id=1, source_target_pairs={{24,0},{16,8},{8,16},{0,24},{25,1},{17,9},{9,17},{1,25},{26,2},{18... | collective-permute-start | bytes 737288 | tf_op jit(solution)/shard_map/ppermute | solution.py:75
  308.3 32.7 %collective-permute-start.56 = (bf16[240,512]{1,0:T(8,128)(2,1)}, bf16[240,512]{1,0:T(8,128)(2,1)}, u32[]{:S(2)}, u32[]{:S(2)}) collective-permute-start(bf16[240,512]{1,0:T(8,128)(2,1)} %get-tuple-element.185), channel_id=1, source_target_pairs={{16,0},{24,8},{0,16},{8,24},{17,1},{25,9},{1,17},{9,25},{18,2},{26... | collective-permute-start | bytes 737288 | tf_op jit(solution)/shard_map/ppermute | solution.py:75
  322.3 18.7 %collective-permute-start.55 = (bf16[240,512]{1,0:T(8,128)(2,1)}, bf16[240,512]{1,0:T(8,128)(2,1)}, u32[]{:S(2)}, u32[]{:S(2)}) collective-permute-start(bf16[240,512]{1,0:T(8,128)(2,1)} %get-tuple-element.183), channel_id=1, source_target_pairs={{8,0},{0,8},{24,16},{16,24},{9,1},{1,9},{25,17},{17,25},{10,2},{2,... | collective-permute-start | bytes 737288 | tf_op jit(solution)/shard_map/ppermute | solution.py:75
  328.1 30.0 %collective-permute-start.53 = (bf16[288,512]{1,0:T(8,128)(2,1)S(1)}, bf16[288,512]{1,0:T(8,128)(2,1)}, u32[]{:S(2)}, u32[]{:S(2)}) collective-permute-start(bf16[288,512]{1,0:T(8,128)(2,1)S(1)} %get-tuple-element.172), channel_id=1, source_target_pairs={{16,0},{24,8},{0,16},{8,24},{17,1},{25,9},{1,17},{9,25},{18,2},{26... | collective-permute-start | bytes 884744 | tf_op jit(solution)/shard_map/ppermute | solution.py:75
  328.2 30.0 %collective-permute-start.52 = (bf16[288,512]{1,0:T(8,128)(2,1)S(1)}, bf16[288,512]{1,0:T(8,128)(2,1)}, u32[]{:S(2)}, u32[]{:S(2)}) collective-permute-start(bf16[288,512]{1,0:T(8,128)(2,1)S(1)} %get-tuple-element.170), channel_id=1, source_target_pairs={{8,0},{0,8},{24,16},{16,24},{9,1},{1,9},{25,17},{17,25},{10,2},{2,... | collective-permute-start | bytes 884744 | tf_op jit(solution)/shard_map/ppermute | solution.py:75
  341.0 21.2 %collective-permute-start.69 = (f32[69,512]{1,0:T(8,128)}, f32[69,512]{1,0:T(8,128)}, u32[]{:S(2)}, u32[]{:S(2)}) collective-permute-start(f32[69,512]{1,0:T(8,128)} %add.328), channel_id=1, source_target_pairs={{16,0},{24,8},{0,16},{8,24},{17,1},{25,9},{1,17},{9,25},{18,2},{26... | collective-permute-start | bytes 423944 | tf_op jit(solution)/shard_map/ppermute | solution.py:75
  (78 other events, 792.2 us)

commit v5 on v4

--- a/solution.py
+++ b/solution.py
@@ -392,8 +392,8 @@
     mix_ref[far_half] = (wide_ref[far_half] + own_share).astype(BF16)
     moves.put(base + MIX, mix_ref)
     sums = [jnp.zeros((1, D), F32) for _ in range(CELLS_ROW)]
-    for start in range(0, tokens, quarter):
-        rows = slice(start, start + quarter)
+    for start in range(0, tokens, tokens):
+        rows = slice(start, start + tokens)
         normed, scaling = norm(x_ref[rows] + dot(mix_ref[rows], moves.get(0)[...]))
         u1_ref[rows] = normed.astype(BF16)
         scale_ref[rows, 0:1] = scaling

time: 394 us -> 393 us (level)
  no operation moved by 1% of the time
where the time goes in v5:
time: 393 us; the launch traced here: 387 us
  waiting for transfers between devices  141 us (36%)
  Pallas kernels  104 us (26%)
  starting transfers between devices  72.7 us (18%)
  other arithmetic  41.8 us (11%)
  matrix products  11.9 us (3%)
  local copies, waits for them, and re-layouts  9.42 us (2%)
  between operations  6.11 us (2%)
    pallas_call x18, Pallas kernels, call(): pl.pallas_call(kernel, out_shape=shapes, in_specs=[small] * len(scalars)...  104 us
    ppermute x50, waiting for transfers between devices, flip(): return lax.ppermute(block, axis, [(0, 1), (1, 0)])  87.7 us
    ppermute x17, waiting for transfers between devices, z_swap(): return lax.ppermute(block, 'z', pairs)  50.1 us
    ppermute x50, starting transfers between devices, flip(): return lax.ppermute(block, axis, [(0, 1), (1, 0)])  46.2 us
    ppermute x17, starting transfers between devices, z_swap(): return lax.ppermute(block, 'z', pairs)  23 us
    convert_element_type x11, other arithmetic, rounded_sum(): return (a.astype(F32) + b.astype(F32)).astype(a.dtype)  7.89 us
  transfers between devices with their start and end apart: 70, of which 34 were waited for; matrix products, arithmetic and copies ran while one was open for 13% of the time, Pallas kernels for 12%

profile of v5, /device:TPU:0, one launch (start us, length us, event | category | flops | bytes accessed | tf_op | source)
XLA Modules:
  0.0 386.8 jit_solution(4172949055092034424)
XLA Ops:
  1.8 5.1 %collective-permute-start.15 = (bf16[288,512]{1,0:T(8,128)(2,1)S(1)}, bf16[288,512]{1,0:T(8,128)(2,1)S(1)}, u32[]{:S(2)}, u32[]{:S(2)}) collective-permute-start(bf16[288,512]{1,0:T(8,128)(2,1)S(1)} %convert_element_type.254), channel_id=1, source_target_pairs={{24,0},{16,8},{8,16},{0,24},{25,1},{17,9},{9,17},{1,25},{26,2},{18... | collective-permute-start | bytes 884744 | tf_op jit(solution)/shard_map/ppermute | solution.py:75
  28.1 16.2 %collective-permute-done.14 = bf16[288,512]{1,0:T(8,128)(2,1)S(1)} collective-permute-done((bf16[288,512]{1,0:T(8,128)(2,1)S(1)}, bf16[288,512]{1,0:T(8,128)(2,1)S(1)}, u32[]{:S(2)}, u32[]{:S(2)}) %collective-permute-start.14) | collective-permute-done | bytes 294944 | tf_op jit(solution)/shard_map/ppermute | solution.py:75
  46.2 8.3 %collective-permute-done.6 = bf16[256,512]{1,0:T(8,128)(2,1)S(1)} collective-permute-done((bf16[256,512]{1,0:T(8,128)(2,1)S(1)}, bf16[256,512]{1,0:T(8,128)(2,1)S(1)}, u32[]{:S(2)}, u32[]{:S(2)}) %collective-permute-start.6) | collective-permute-done | bytes 262176 | tf_op jit(solution)/shard_map/ppermute | solution.py:75
  60.2 4.5 %collective-permute-done.16 = bf16[2,144,512]{2,1,0:T(8,128)(2,1)S(1)} collective-permute-done((bf16[2,144,512]{2,1,0:T(8,128)(2,1)S(1)}, bf16[2,144,512]{2,1,0:T(8,128)(2,1)S(1)}, u32[]{:S(2)}, u32[]{:S(2)}) %collective-permute-start.16) | collective-permute-done | bytes 294944 | tf_op jit(solution)/shard_map/ppermute | solution.py:34
  72.7 10.9 %collective-permute-done.19 = bf16[2,2,144,512]{3,2,0,1:T(8,128)(2,1)S(1)} collective-permute-done((bf16[2,2,144,512]{3,2,0,1:T(8,128)(2,1)S(1)}, bf16[2,2,144,512]{3,2,0,1:T(8,128)(2,1)S(1)}, u32[]{:S(2)}, u32[]{:S(2)}) %collective-permute-start.19) | collective-permute-done | bytes 589856 | tf_op jit(solution)/shard_map/ppermute | solution.py:34
  85.3 5.0 %fusion.4 = bf16[2048,512]{1,0:T(8,128)(2,1)S(1)} fusion(bf16[2048,512]{1,0:T(8,128)(2,1)S(1)} %bitcast.288, s32[2048]{0:T(1024)S(1)} %fusion.43), kind=kOutput, calls=%fused_computation.7 | convolution fusion | flops 4300210176 | bytes 4202496 | tf_op jit(solution)/shard_map/dot_general | solution.py:270
  98.2 8.9 %collective-permute-done.9 = bf16[2,256,512]{2,1,0:T(8,128)(2,1)S(1)} collective-permute-done((bf16[2,256,512]{2,1,0:T(8,128)(2,1)S(1)}, bf16[2,256,512]{2,1,0:T(8,128)(2,1)S(1)}, u32[]{:S(2)}, u32[]{:S(2)}) %collective-permute-start.9) | collective-permute-done | bytes 524320 | tf_op jit(solution)/shard_map/ppermute | solution.py:34
  110.8 4.5 %collective-permute-done.12 = bf16[256,512]{1,0:T(8,128)(2,1)S(1)} collective-permute-done((bf16[256,512]{1,0:T(8,128)(2,1)S(1)}, bf16[256,512]{1,0:T(8,128)(2,1)S(1)}, u32[]{:S(2)}, u32[]{:S(2)}) %collective-permute-start.12) | collective-permute-done | bytes 262176 | tf_op jit(solution)/shard_map/ppermute | solution.py:34
  120.2 5.0 %shard_map.273 = (bf16[512,512]{1,0:T(8,128)(2,1)S(1)}, bf16[512,512]{1,0:T(8,128)(2,1)S(1)}, bf16[512,512]{1,0:T(8,128)(2,1)S(1)}, bf16[256,1024]{1,0:T(8,128)(2,1)}, bf16[132,512,512]{2,1,0:T(8,128)(2,1)}) custom-call(f32[512,512]{1,0:T(8,128)S(1)} %convolution_add_fusion.refs_0_, ...), custom_call_target="tpu_custom_call" | custom-call | flops 1000000000 | bytes 1000000 | tf_op jit(solution)/shard_map/pallas_call | solution.py:253
  127.5 11.8 %shard_map.274 = (f32[16,512]{1,0:T(8,128)S(1)}, f32[512,512]{1,0:T(8,128)S(1)}, bf16[512,512]{1,0:T(8,128)(2,1)S(1)}, bf16[512,512]{1,0:T(8,128)(2,1)S(1)}, bf1...) custom-call(f32[512,512]{1,0:T(8,128)S(1)} %convolution_add_fusion.r, ...), custom_call_target="tpu_custom_call", output_to_operand_aliasing={{6}: (15, {})} | custom-call | flops 1000000000 | bytes 1000000 | tf_op jit(solution)/shard_map/pallas_call | solution.py:253
  139.5 4.9 %shard_map.275.refs_9_.refs_10_.refs_11_.refs_12_.refs_13_.refs_14_.refs_7_.refs_5_.refs_6_ = bf16[132,512,512]{2,1,0:T(8,128)(2,1)} custom-call(s32[1]{0:T(128)} %bitcast.refs_0_, bf16[2,2,2,288,512]{4,3,2,1,0:T(8,128)(2,1)} %maximum_maximum_fusion.1.refs_1_, ...), custom_call_target="tpu_custom_call", output_to_operand_aliasing={{}: (3, {})} | custom-call | flops 1000000000 | bytes 1000000 | tf_op jit(solution)/shard_map/pallas_call | solution.py:253
  144.4 10.8 %shard_map.276 = (f32[16,512]{1,0:T(8,128)S(1)}, f32[512,512]{1,0:T(8,128)S(1)}, bf16[512,512]{1,0:T(8,128)(2,1)S(1)}, bf16[512,512]{1,0:T(8,128)(2,1)S(1)}, bf1...) custom-call(f32[512,512]{1,0:T(8,128)S(1)} %get-tuple-element.85.ref, ...), custom_call_target="tpu_custom_call", output_to_operand_aliasing={{6}: (15, {})} | custom-call | flops 1000000000 | bytes 1000000 | tf_op jit(solution)/shard_map/pallas_call | solution.py:253
  157.2 9.5 %shard_map.277 = (f32[16,512]{1,0:T(8,128)S(1)}, f32[4,512]{1,0:T(4,128)S(1)}, bf16[132,512,512]{2,1,0:T(8,128)(2,1)}) custom-call(f32[512,512]{1,0:T(8,128)S(1)} %get-tuple-element.91.refs_0_, bf16[512,512]{1,0:T(8,128)(2,1)S(1)} %get-tuple-element.92.refs_1_, bf16[512,512]{1,0:T(8,128)(2,1)S(1)} %get-tuple-element.93.refs_2_, ...), custom_call_target="tpu_custom_call", output_to_operand_aliasing={{2}: (12, {})} | custom-call | flops 1000000000 | bytes 1000000 | tf_op jit(solution)/shard_map/pallas_call | solution.py:253
  184.3 12.8 %shard_map.279 = (f32[512,512]{1,0:T(8,128)S(1)}, bf16[512,512]{1,0:T(8,128)(2,1)S(1)}, bf16[512,512]{1,0:T(8,128)(2,1)S(1)}, bf16[512,512]{1,0:T(8,128)(2,1)S(1...) custom-call(f32[4,512]{1,0:T(4,128)S(1)} %fusion.46.refs_0_, ...), custom_call_target="tpu_custom_call" | custom-call | flops 1000000000 | bytes 1000000 | tf_op jit(solution)/shard_map/pallas_call | solution.py:253
  203.6 12.2 %shard_map.281 = (f32[512,512]{1,0:T(8,128)S(1)}, bf16[512,512]{1,0:T(8,128)(2,1)S(1)}, bf16[512,512]{1,0:T(8,128)(2,1)S(1)}, bf16[512,512]{1,0:T(8,128)(2,1)S(1...) custom-call(f32[512,512]{1,0:T(8,128)S(1)} %get-tuple-element.106.re, ...), custom_call_target="tpu_custom_call" | custom-call | flops 1000000000 | bytes 1000000 | tf_op jit(solution)/shard_map/pallas_call | solution.py:253
  221.2 4.1 %collective-permute-done.36 = bf16[2,2,2,288,512]{4,3,0,2,1:T(8,128)(2,1)S(1)} collective-permute-done((bf16[2,2,2,288,512]{4,3,0,2,1:T(8,128)(2,1)S(1)}, bf16[2,2,2,288,512]{4,3,0,2,1:T(8,128)(2,1)S(1)}, u32[]{:S(2)}, u32[]{:S(2)}) %collective-permute-start.36) | collective-permute-done | bytes 2359328 | tf_op jit(solution)/shard_map/ppermute | solution.py:34
  233.4 12.2 %shard_map.286 = (f32[512,512]{1,0:T(8,128)S(1)}, bf16[512,512]{1,0:T(8,128)(2,1)S(1)}, bf16[512,512]{1,0:T(8,128)(2,1)S(1)}, bf16[512,512]{1,0:T(8,128)(2,1)S(1...) custom-call(f32[512,512]{1,0:T(8,128)S(1)} %get-tuple-element.113.re, ...), custom_call_target="tpu_custom_call" | custom-call | flops 1000000000 | bytes 1000000 | tf_op jit(solution)/shard_map/pallas_call | solution.py:253
  259.2 4.4 %collective-permute-done.45 = bf16[256,512]{1,0:T(8,128)(2,1)S(1)} collective-permute-done((bf16[256,512]{1,0:T(8,128)(2,1)S(1)}, bf16[256,512]{1,0:T(8,128)(2,1)S(1)}, u32[]{:S(2)}, u32[]{:S(2)}) %collective-permute-start.45) | collective-permute-done | bytes 262176 | tf_op jit(solution)/shard_map/ppermute | solution.py:34
  268.5 11.9 %collective-permute-done.66 = f32[69,512]{1,0:T(8,128)S(1)} collective-permute-done((f32[69,512]{1,0:T(8,128)S(1)}, f32[69,512]{1,0:T(8,128)S(1)}, u32[]{:S(2)}, u32[]{:S(2)}) %collective-permute-start.66) | collective-permute-done | bytes 141344 | tf_op jit(solution)/shard_map/ppermute | solution.py:34
  281.3 5.2 %fusion = f32[2048,512]{1,0:T(8,128)S(1)} fusion(bf16[2048,512]{1,0:T(8,128)(2,1)S(1)} %bitcast.312, s32[2048]{0:T(1024)S(1)} %copy-done.31), kind=kOutput, calls=%fused_computation.1 | convolution fusion | flops 4299161600 | bytes 6299648 | tf_op jit(solution)/shard_map/dot_general | solution.py:274
  297.1 7.7 %collective-permute-done.42 = bf16[2,2,144,512]{3,2,0,1:T(8,128)(2,1)} collective-permute-done((bf16[2,2,144,512]{3,2,0,1:T(8,128)(2,1)}, bf16[2,2,144,512]{3,2,0,1:T(8,128)(2,1)}, u32[]{:S(2)}, u32[]{:S(2)}) %collective-permute-start.42) | collective-permute-done | bytes 589856 | tf_op jit(solution)/shard_map/ppermute | solution.py:34
  317.0 4.3 %collective-permute-done.49 = bf16[2,144,512]{2,1,0:T(8,128)(2,1)S(1)} collective-permute-done((bf16[2,144,512]{2,1,0:T(8,128)(2,1)}, bf16[2,144,512]{2,1,0:T(8,128)(2,1)S(1)}, u32[]{:S(2)}, u32[]{:S(2)}) %collective-permute-start.49) | collective-permute-done | bytes 294944 | tf_op jit(solution)/shard_map/ppermute | solution.py:34
  331.3 8.7 %collective-permute-done.56 = bf16[240,512]{1,0:T(8,128)(2,1)} collective-permute-done((bf16[240,512]{1,0:T(8,128)(2,1)}, bf16[240,512]{1,0:T(8,128)(2,1)}, u32[]{:S(2)}, u32[]{:S(2)}) %collective-permute-start.56) | collective-permute-done | bytes 245792 | tf_op jit(solution)/shard_map/ppermute | solution.py:75
  342.0 15.3 %collective-permute-done.53 = bf16[288,512]{1,0:T(8,128)(2,1)} collective-permute-done((bf16[288,512]{1,0:T(8,128)(2,1)S(1)}, bf16[288,512]{1,0:T(8,128)(2,1)}, u32[]{:S(2)}, u32[]{:S(2)}) %collective-permute-start.53) | collective-permute-done | bytes 294944 | tf_op jit(solution)/shard_map/ppermute | solution.py:75
  (336 shorter events, 176.6 us)
Async XLA Ops:
  1.8 24.5 %collective-permute-start.15 = (bf16[288,512]{1,0:T(8,128)(2,1)S(1)}, bf16[288,512]{1,0:T(8,128)(2,1)S(1)}, u32[]{:S(2)}, u32[]{:S(2)}) collective-permute-start(bf16[288,512]{1,0:T(8,128)(2,1)S(1)} %convert_element_type.254), channel_id=1, source_target_pairs={{24,0},{16,8},{8,16},{0,24},{25,1},{17,9},{9,17},{1,25},{26,2},{18... | collective-permute-start | bytes 884744 | tf_op jit(solution)/shard_map/ppermute | solution.py:75
  6.9 37.3 %collective-permute-start.14 = (bf16[288,512]{1,0:T(8,128)(2,1)S(1)}, bf16[288,512]{1,0:T(8,128)(2,1)S(1)}, u32[]{:S(2)}, u32[]{:S(2)}) collective-permute-start(bf16[288,512]{1,0:T(8,128)(2,1)S(1)} %convert_element_type.254), channel_id=1, source_target_pairs={{16,0},{24,8},{0,16},{8,24},{17,1},{25,9},{1,17},{9,25},{18,2},{26... | collective-permute-start | bytes 884744 | tf_op jit(solution)/shard_map/ppermute | solution.py:75
  6.9 37.3 %collective-permute-start.13 = (bf16[288,512]{1,0:T(8,128)(2,1)S(1)}, bf16[288,512]{1,0:T(8,128)(2,1)S(1)}, u32[]{:S(2)}, u32[]{:S(2)}) collective-permute-start(bf16[288,512]{1,0:T(8,128)(2,1)S(1)} %convert_element_type.254), channel_id=1, source_target_pairs={{8,0},{0,8},{24,16},{16,24},{9,1},{1,9},{25,17},{17,25},{10,2},{2,... | collective-permute-start | bytes 884744 | tf_op jit(solution)/shard_map/ppermute | solution.py:75
  22.6 23.6 %collective-permute-start.7 = (bf16[256,512]{1,0:T(8,128)(2,1)S(1)}, bf16[256,512]{1,0:T(8,128)(2,1)S(1)}, u32[]{:S(2)}, u32[]{:S(2)}) collective-permute-start(bf16[256,512]{1,0:T(8,128)(2,1)S(1)} %get-tuple-element.211), channel_id=1, source_target_pairs={{24,0},{16,8},{8,16},{0,24},{25,1},{17,9},{9,17},{1,25},{26,2},{18... | collective-permute-start | bytes 786440 | tf_op jit(solution)/shard_map/ppermute | solution.py:75
  26.2 28.3 %collective-permute-start.6 = (bf16[256,512]{1,0:T(8,128)(2,1)S(1)}, bf16[256,512]{1,0:T(8,128)(2,1)S(1)}, u32[]{:S(2)}, u32[]{:S(2)}) collective-permute-start(bf16[256,512]{1,0:T(8,128)(2,1)S(1)} %get-tuple-element.210), channel_id=1, source_target_pairs={{16,0},{24,8},{0,16},{8,24},{17,1},{25,9},{1,17},{9,25},{18,2},{26... | collective-permute-start | bytes 786440 | tf_op jit(solution)/shard_map/ppermute | solution.py:75
  26.3 28.2 %collective-permute-start.5 = (bf16[256,512]{1,0:T(8,128)(2,1)S(1)}, bf16[256,512]{1,0:T(8,128)(2,1)S(1)}, u32[]{:S(2)}, u32[]{:S(2)}) collective-permute-start(bf16[256,512]{1,0:T(8,128)(2,1)S(1)} %get-tuple-element.209), channel_id=1, source_target_pairs={{8,0},{0,8},{24,16},{16,24},{9,1},{1,9},{25,17},{17,25},{10,2},{2,... | collective-permute-start | bytes 786440 | tf_op jit(solution)/shard_map/ppermute | solution.py:75
  54.7 29.6 %collective-permute-start.8 = (bf16[4,256,512]{2,1,0:T(8,128)(2,1)S(1)}, bf16[4,256,512]{2,1,0:T(8,128)(2,1)S(1)}, u32[]{:S(2)}, u32[]{:S(2)}) collective-permute-start(bf16[4,256,512]{2,1,0:T(8,128)(2,1)S(1)} %get-tuple-element.187), channel_id=1, source_target_pairs={{0,2},{2,0},{1,3},{3,1},{4,6},{6,4},{5,7},{7,5},{8,10},{10,8},{9,1... | collective-permute-start | bytes 3145736 | tf_op jit(solution)/shard_map/ppermute | solution.py:34
  58.6 25.0 %collective-permute-start.19 = (bf16[2,2,144,512]{3,2,0,1:T(8,128)(2,1)S(1)}, bf16[2,2,144,512]{3,2,0,1:T(8,128)(2,1)S(1)}, u32[]{:S(2)}, u32[]{:S(2)}) collective-permute-start(bf16[2,2,144,512]{3,2,0,1:T(8,128)(2,1)S(1)} %pad_maximum_fusion.5), channel_id=1, source_target_pairs={{0,4},{4,0},{1,5},{5,1},{2,6},{6,2},{3,7},{7,3},{8,12},{12,8},{9,1... | collective-permute-start | bytes 1769480 | tf_op jit(solution)/shard_map/ppermute | solution.py:34
  64.8 19.0 %collective-permute-start.17 = (bf16[2,2,144,512]{3,2,0,1:T(8,128)(2,1)S(1)}, bf16[2,2,144,512]{3,2,0,1:T(8,128)(2,1)S(1)}, u32[]{:S(2)}, u32[]{:S(2)}) collective-permute-start(bf16[2,2,144,512]{3,2,0,1:T(8,128)(2,1)S(1)} %pad_maximum_fusion.4), channel_id=1, source_target_pairs={{0,1},{1,0},{2,3},{3,2},{4,5},{5,4},{6,7},{7,6},{8,9},{9,8},{10,11... | collective-permute-start | bytes 1769480 | tf_op jit(solution)/shard_map/ppermute | solution.py:34
  66.5 29.8 %collective-permute-start.26 = (bf16[2,2,144,512]{3,2,1,0:T(8,128)(2,1)S(1)}, bf16[2,2,144,512]{3,2,1,0:T(8,128)(2,1)S(1)}, u32[]{:S(2)}, u32[]{:S(2)}) collective-permute-start(bf16[2,2,144,512]{3,2,1,0:T(8,128)(2,1)S(1)} %pad_maximum_fusion.7), channel_id=1, source_target_pairs={{0,4},{4,0},{1,5},{5,1},{2,6},{6,2},{3,7},{7,3},{8,12},{12,8},{9,1... | collective-permute-start | bytes 1769480 | tf_op jit(solution)/shard_map/ppermute | solution.py:34
  71.1 25.3 %collective-permute-start.24 = (bf16[2,2,144,512]{3,2,0,1:T(8,128)(2,1)S(1)}, bf16[2,2,144,512]{3,2,0,1:T(8,128)(2,1)S(1)}, u32[]{:S(2)}, u32[]{:S(2)}) collective-permute-start(bf16[2,2,144,512]{3,2,0,1:T(8,128)(2,1)S(1)} %pad_maximum_fusion.6), channel_id=1, source_target_pairs={{0,1},{1,0},{2,3},{3,2},{4,5},{5,4},{6,7},{7,6},{8,9},{9,8},{10,11... | collective-permute-start | bytes 1769480 | tf_op jit(solution)/shard_map/ppermute | solution.py:34
  84.2 33.2 %collective-permute-start.20 = (bf16[2,2,2,288,512]{4,3,2,0,1:T(8,128)(2,1)S(1)}, bf16[2,2,2,288,512]{4,3,2,0,1:T(8,128)(2,1)S(1)}, u32[]{:S(2)}, u32[]{:S(2)}) collective-permute-start(bf16[2,2,2,288,512]{4,3,2,0,1:T(8,128)(2,1)S(1)} %maximum_maximum_fusion), channel_id=1, source_target_pairs={{0,2},{2,0},{1,3},{3,1},{4,6},{6,4},{5,7},{7,5},{8,10},{10,8},{9,1... | collective-permute-start | bytes 7077896 | tf_op jit(solution)/shard_map/ppermute | solution.py:34
  98.2 41.3 %collective-permute-start.27 = (bf16[2,2,2,288,512]{4,3,2,1,0:T(8,128)(2,1)}, bf16[2,2,2,288,512]{4,3,2,1,0:T(8,128)(2,1)}, u32[]{:S(2)}, u32[]{:S(2)}) collective-permute-start(bf16[2,2,2,288,512]{4,3,2,1,0:T(8,128)(2,1)} %maximum_maximum_fusion.1.refs_1_), channel_id=1, source_target_pairs={{0,2},{2,0},{1,3},{3,1},{4,6},{6,4},{5,7},{7,5},{8,10},{10,8},{9,1... | collective-permute-start | bytes 7077896 | tf_op jit(solution)/shard_map/ppermute | solution.py:34
  227.9 21.2 %collective-permute-start.39 = (bf16[2,2,144,512]{3,2,0,1:T(8,128)(2,1)}, bf16[2,2,144,512]{3,2,0,1:T(8,128)(2,1)}, u32[]{:S(2)}, u32[]{:S(2)}) collective-permute-start(bf16[2,2,144,512]{3,2,0,1:T(8,128)(2,1)} %select_bitcast_fusion), channel_id=1, source_target_pairs={{0,1},{1,0},{2,3},{3,2},{4,5},{5,4},{6,7},{7,6},{8,9},{9,8},{10,11... | collective-permute-start | bytes 1769480 | tf_op jit(solution)/shard_map/ppermute | solution.py:34
  229.4 19.6 %collective-permute-start.38 = (bf16[2,2,144,512]{3,2,0,1:T(8,128)(2,1)}, bf16[2,2,144,512]{3,2,0,1:T(8,128)(2,1)}, u32[]{:S(2)}, u32[]{:S(2)}) collective-permute-start(bf16[2,2,144,512]{3,2,0,1:T(8,128)(2,1)} %select_bitcast_fusion.1), channel_id=1, source_target_pairs={{0,4},{4,0},{1,5},{5,1},{2,6},{6,2},{3,7},{7,3},{8,12},{12,8},{9,1... | collective-permute-start | bytes 1769480 | tf_op jit(solution)/shard_map/ppermute | solution.py:34
  258.6 28.1 %collective-permute-start.40 = (bf16[2,2,2,288,512]{4,3,0,1,2:T(8,128)(2,1)S(1)}, bf16[2,2,2,288,512]{4,3,0,1,2:T(8,128)(2,1)S(1)}, u32[]{:S(2)}, u32[]{:S(2)}) collective-permute-start(bf16[2,2,2,288,512]{4,3,0,1,2:T(8,128)(2,1)S(1)} %copy.148), channel_id=1, source_target_pairs={{0,2},{2,0},{1,3},{3,1},{4,6},{6,4},{5,7},{7,5},{8,10},{10,8},{9,1... | collective-permute-start | bytes 7077896 | tf_op jit(solution)/shard_map/ppermute | solution.py:34
  293.7 33.5 %collective-permute-start.68 = (f32[69,512]{1,0:T(8,128)}, f32[69,512]{1,0:T(8,128)}, u32[]{:S(2)}, u32[]{:S(2)}) collective-permute-start(f32[69,512]{1,0:T(8,128)} %add.327), channel_id=1, source_target_pairs={{8,0},{0,8},{24,16},{16,24},{9,1},{1,9},{25,17},{17,25},{10,2},{2,... | collective-permute-start | bytes 423944 | tf_op jit(solution)/shard_map/ppermute | solution.py:75
  295.7 19.7 %collective-permute-start.50 = (bf16[2,144,512]{2,1,0:T(8,128)(2,1)}, bf16[2,144,512]{2,1,0:T(8,128)(2,1)}, u32[]{:S(2)}, u32[]{:S(2)}) collective-permute-start(bf16[2,144,512]{2,1,0:T(8,128)(2,1)} %get-tuple-element.140), channel_id=1, source_target_pairs={{0,1},{1,0},{2,3},{3,2},{4,5},{5,4},{6,7},{7,6},{8,9},{9,8},{10,11... | collective-permute-start | bytes 884744 | tf_op jit(solution)/shard_map/ppermute | solution.py:34
  304.8 22.4 %collective-permute-start.57 = (bf16[240,512]{1,0:T(8,128)(2,1)}, bf16[240,512]{1,0:T(8,128)(2,1)}, u32[]{:S(2)}, u32[]{:S(2)}) collective-permute-start(bf16[240,512]{1,0:T(8,128)(2,1)} %get-tuple-element.184), channel_id=1, source_target_pairs={{24,0},{16,8},{8,16},{0,24},{25,1},{17,9},{9,17},{1,25},{26,2},{18... | collective-permute-start | bytes 737288 | tf_op jit(solution)/shard_map/ppermute | solution.py:75
  307.3 32.8 %collective-permute-start.56 = (bf16[240,512]{1,0:T(8,128)(2,1)}, bf16[240,512]{1,0:T(8,128)(2,1)}, u32[]{:S(2)}, u32[]{:S(2)}) collective-permute-start(bf16[240,512]{1,0:T(8,128)(2,1)} %get-tuple-element.185), channel_id=1, source_target_pairs={{16,0},{24,8},{0,16},{8,24},{17,1},{25,9},{1,17},{9,25},{18,2},{26... | collective-permute-start | bytes 737288 | tf_op jit(solution)/shard_map/ppermute | solution.py:75
  321.3 18.7 %collective-permute-start.55 = (bf16[240,512]{1,0:T(8,128)(2,1)}, bf16[240,512]{1,0:T(8,128)(2,1)}, u32[]{:S(2)}, u32[]{:S(2)}) collective-permute-start(bf16[240,512]{1,0:T(8,128)(2,1)} %get-tuple-element.183), channel_id=1, source_target_pairs={{8,0},{0,8},{24,16},{16,24},{9,1},{1,9},{25,17},{17,25},{10,2},{2,... | collective-permute-start | bytes 737288 | tf_op jit(solution)/shard_map/ppermute | solution.py:75
  327.2 30.1 %collective-permute-start.53 = (bf16[288,512]{1,0:T(8,128)(2,1)S(1)}, bf16[288,512]{1,0:T(8,128)(2,1)}, u32[]{:S(2)}, u32[]{:S(2)}) collective-permute-start(bf16[288,512]{1,0:T(8,128)(2,1)S(1)} %get-tuple-element.172), channel_id=1, source_target_pairs={{16,0},{24,8},{0,16},{8,24},{17,1},{25,9},{1,17},{9,25},{18,2},{26... | collective-permute-start | bytes 884744 | tf_op jit(solution)/shard_map/ppermute | solution.py:75
  327.2 30.1 %collective-permute-start.52 = (bf16[288,512]{1,0:T(8,128)(2,1)S(1)}, bf16[288,512]{1,0:T(8,128)(2,1)}, u32[]{:S(2)}, u32[]{:S(2)}) collective-permute-start(bf16[288,512]{1,0:T(8,128)(2,1)S(1)} %get-tuple-element.170), channel_id=1, source_target_pairs={{8,0},{0,8},{24,16},{16,24},{9,1},{1,9},{25,17},{17,25},{10,2},{2,... | collective-permute-start | bytes 884744 | tf_op jit(solution)/shard_map/ppermute | solution.py:75
  340.0 21.2 %collective-permute-start.69 = (f32[69,512]{1,0:T(8,128)}, f32[69,512]{1,0:T(8,128)}, u32[]{:S(2)}, u32[]{:S(2)}) collective-permute-start(f32[69,512]{1,0:T(8,128)} %add.328), channel_id=1, source_target_pairs={{16,0},{24,8},{0,16},{8,24},{17,1},{25,9},{1,17},{9,25},{18,2},{26... | collective-permute-start | bytes 423944 | tf_op jit(solution)/shard_map/ppermute | solution.py:75
  (78 other events, 792.3 us)
